TPU v7x, 256 devices: a whole 4x4x8 slice. The times are simulated.
256 devices in a mesh: gx: 64 (over x_lo, y, z), col: 4 (over x_hi, core).
Axes of the slice: x: 4 (x_hi: 2, x_lo: 2; x = x_hi * 2 + x_lo), y: 4, z: 8, core: 2. Of those that a mesh axis runs over, the one named last changes fastest.
Arguments:
- state: bfloat16 [128, 64, 128, 128], P(None, 'gx', 'col'), may hold values from -6 to 6
- target: bfloat16 [128, 64, 128, 128], P(None, 'gx', 'col'), may hold values from -6 to 6
- spectral_weight: bfloat16 [2, 128, 16, 512, 128], P(None, None, None, ('gx', 'col')), may hold values from -0.375 to 0.375
- direction_weight: bfloat16 [2, 128, 16, 512, 128], P(None, None, None, ('gx', 'col')), may hold values from -0.375 to 0.375
- inner_weight: bfloat16 [128, 512], replicated, may hold values from -0.5 to 0.5
- outer_weight: bfloat16 [512, 128], replicated, may hold values from -0.25 to 0.25
Outputs:
- gradient: bfloat16 [2, 128, 16, 512, 128], P(None, None, None, ('gx', 'col'))
- curvature: bfloat16 [2, 128, 16, 512, 128], P(None, None, None, ('gx', 'col'))
All inputs are finite; a program needn't handle non-finite values.
Results may differ from a plain program's by a relative error of at most 0.0045.
Values sent between devices are 32-bit elements; how exact they have to be, the bound alone decides.
No kernel may reach another device: no remote copies, remote signals or barrier semaphores. Data moves between devices by JAX's collectives and lax.ppermute only.
A program may use at most 128 MiB of HBM per device.

v0:
```python
import math

import jax
import jax.numpy as jnp
import ml_dtypes
import numpy as np
from jax import lax
from jax.experimental import pallas as pl
from jax.experimental.pallas import tpu as pltpu
from jax.sharding import Mesh
from jax.sharding import PartitionSpec as P

C = 128
FF = 512
NX = 64
NY = 128
NZ = 128
MX = 16
MY = 32
MZ = 16
ROWS = 32
COLUMNS = 4
POINTS = NX * NY * NZ
KEPT = MX * MY * MZ
FORWARD_FACTOR = 1.0 / math.sqrt(POINTS)
INVERSE_FACTOR = 2.0 / math.sqrt(KEPT)
LOSS_SCALE = 0.5 * math.sqrt(KEPT / POINTS)
ROWS_A_STEP = 4
CHUNK = ROWS_A_STEP * NZ
CB = 16

GX = ("xl", "y", "z")
COL = ("xh", "co")
WIDE = GX + ("xh",)
F32 = jnp.float32
BF16 = jnp.bfloat16


def params():
    return pltpu.CompilerParams(dimension_semantics=("arbitrary",), vmem_limit_bytes=44 * 1024 * 1024)


def signed(number):
    ladder = np.arange(number)
    return np.where(ladder < number // 2, ladder, ladder - number)


def angles(positions, frequencies, length):
    return (np.outer(positions, frequencies) % length) * (2.0 * math.pi / length)


def halves(table):
    high = table.astype(ml_dtypes.bfloat16)
    low = (table - high.astype(np.float64)).astype(ml_dtypes.bfloat16)
    return high, low


def wide(table):
    high, low = halves(table)
    return np.concatenate([high, high, low], axis=-1)


def tall(table):
    high, low = halves(table)
    return np.concatenate([high, low], axis=-2)


def rotation(positions, frequencies, length, sign):
    a = angles(positions, frequencies, length)
    c, s = np.cos(a), sign * np.sin(a)
    return np.stack([np.stack([c, -s]), np.stack([s, c])])


def z_order(core):
    order = []
    for which in range(2):
        co = core if which == 0 else 1 - core
        for zh in range(2):
            for xh in range(2):
                for m in range(2):
                    order.append(8 * zh + 4 * xh + 2 * co + m)
    return np.array(order)


def z_tables():
    inverse, forward = [], []
    for core in range(2):
        a = angles(np.arange(NZ), z_order(core), NZ)
        inverse.append(wide(np.stack([np.cos(a), -np.sin(a)], -1).reshape(NZ, 2 * MZ)))
        forward.append(tall(np.stack([np.cos(a), -np.sin(a)], -1).reshape(NZ, 2 * MZ).T))
    return np.stack(inverse), np.stack(forward)


def y_tables():
    inverse, forward = [], []
    for column in range(COLUMNS):
        rows = column * ROWS + np.arange(ROWS)
        r = rotation(rows, signed(MY), NY, 1.0)
        inverse.append(wide(r.transpose(0, 2, 1, 3).reshape(2 * ROWS, 2 * MY)))
        r = rotation(rows, signed(MY), NY, -1.0)
        forward.append(wide(r.transpose(0, 3, 1, 2).reshape(2 * MY, 2 * ROWS)))
    return np.stack(inverse), np.stack(forward)


def x_forward_table(fields, factor):
    r = rotation(np.arange(NX), signed(MX), NX, -1.0) * factor
    t = np.zeros((fields, 2, MX, 2, NX, 2, 2, fields, 2))
    for s in range(fields):
        for m in range(2):
            for xh in range(2):
                t[s, :, :, m, :, xh, m, s, :] = r.transpose(0, 3, 2, 1)
    return tall(t.reshape(fields * 2 * MX * 2, NX * 2 * 2 * fields * 2))


def x_inverse_table(factor):
    r = rotation(np.arange(NX), signed(MX), NX, 1.0) * factor
    t = np.zeros((NX, 2, 2, 2, 2, 2, MX, 2))
    for s in range(2):
        for m in range(2):
            t[:, m, s, :, s, :, :, m] = r.transpose(2, 0, 1, 3)
    return wide(t.reshape(NX * 8, 128))


def dot(a, b):
    return jnp.dot(a, b, preferred_element_type=F32)


def two(values):
    high = values.astype(BF16)
    return high, (values - high.astype(F32)).astype(BF16)


def three(values):
    high, low = two(values)
    return jnp.concatenate([high, low, high], axis=0)


def tall_dot(table, values):
    rows = table.shape[0] // 2
    high, low = two(values)
    first = dot(table, high)
    return first[:rows] + first[rows:] + dot(table[:rows], low)


def field_kernel(
    mine, other, state, target, w1, w2, w1t, w2t, yi, zi, zf, yf, keep, give, half, after
):
    step = pl.program_id(0)

    @pl.when(step == 0)
    def _():
        for k in range(MZ):
            source = mine if k < 8 else other
            base = (k % 8) // 2 * 8 + k % 2 * 4
            parts = []
            for s in range(2):
                p = [source[pl.ds(base + 2 * s + i, MY, stride=32), :] for i in range(2)]
                parts.append(jnp.concatenate(p, axis=0))
            rows = dot(yi[...], three(jnp.concatenate(parts, axis=1)))
            for s in range(2):
                half[s, pl.ds(k * 64, 64), :] = rows[:, s * C : (s + 1) * C]

    fields = []
    for i in range(ROWS_A_STEP):
        y = step * ROWS_A_STEP + i
        taken = [half[s, pl.ds(y, 2 * MZ, stride=ROWS), :] for s in range(2)]
        fields.append(dot(zi[...], three(jnp.concatenate(taken, axis=1))))
    fields = jnp.concatenate(fields, axis=0).astype(BF16)
    primal, tangent = fields[:, :C], fields[:, C:]
    layer_input = state[...].astype(F32) + primal.astype(F32)
    hidden = dot(layer_input.astype(BF16), w1[...])
    mass = 0.5 * (1.0 + lax.erf(hidden * math.sqrt(0.5)))
    density = jnp.exp(-0.5 * hidden * hidden) * (1.0 / math.sqrt(2.0 * math.pi))
    slope = mass + hidden * density
    activation = (hidden * mass).astype(BF16)
    seed_primal = LOSS_SCALE * (layer_input + dot(activation, w2[...]) - target[...].astype(F32))
    hidden_tangent = dot(tangent, w1[...])
    activation_tangent = (slope * hidden_tangent).astype(BF16)
    seed_tangent = LOSS_SCALE * (tangent.astype(F32) + dot(activation_tangent, w2[...]))
    back_primal = dot(seed_primal.astype(BF16), w2t[...])
    back_tangent = dot(seed_tangent.astype(BF16), w2t[...])
    delta_primal = (slope * back_primal).astype(BF16)
    bend = density * (2.0 - hidden * hidden)
    delta_tangent = (bend * hidden_tangent * back_primal + slope * back_tangent).astype(BF16)
    cotangents = jnp.concatenate(
        [seed_primal + dot(delta_primal, w1t[...]), seed_tangent + dot(delta_tangent, w1t[...])], axis=1
    )
    for i in range(ROWS_A_STEP):
        rows = tall_dot(zf[...], cotangents[i * NZ : (i + 1) * NZ])
        start = pl.multiple_of((step * ROWS_A_STEP + i) * 2 * MZ, 2 * MZ)
        for s in range(2):
            after[s, pl.ds(start, 2 * MZ), :] = rows[:, s * C : (s + 1) * C]

    @pl.when(step == ROWS // ROWS_A_STEP - 1)
    def _():
        for k in range(MZ):
            sink = keep if k < 8 else give
            base = (k % 8) // 2 * 8 + k % 2 * 4
            parts = []
            for s in range(2):
                q = [after[s, pl.ds(2 * k + i, ROWS, stride=2 * MZ), :] for i in range(2)]
                parts.append(jnp.concatenate(q, axis=0))
            rows = dot(yf[...], three(jnp.concatenate(parts, axis=1)))
            for s in range(2):
                for r in range(2):
                    sink[pl.ds(base + 2 * s + r, MY, stride=32), :] = rows[
                        r * MY : (r + 1) * MY, s * C : (s + 1) * C
                    ]


def whole(shape):
    return pl.BlockSpec(shape, lambda i: (0,) * len(shape))


def field_stage(mine, other, state, target, w1, w2, yi, zi, zf, yf):
    operands = (mine, other, state, target, w1, w2, w1.T, w2.T, yi, zi, zf, yf)
    moving = pl.BlockSpec((CHUNK, C), lambda i: (i, 0))
    specs = [moving if i in (2, 3) else whole(a.shape) for i, a in enumerate(operands)]
    shape = jax.ShapeDtypeStruct((1024, C), F32)
    return pl.pallas_call(
        field_kernel,
        grid=(ROWS // ROWS_A_STEP,),
        in_specs=specs,
        out_specs=(whole((1024, C)), whole((1024, C))),
        out_shape=(shape, shape),
        scratch_shapes=[pltpu.VMEM((2, 1024, C), F32), pltpu.VMEM((2, 1024, C), F32)],
        compiler_params=params(),
    )(*operands)


def mix_kernel(received, weight, direction, xf, xi, spectra, planes, total):
    step = pl.program_id(0)

    @pl.when(step == 0)
    def _():
        spectra[...] = tall_dot(xf[...], received[...])
        total[...] = jnp.zeros_like(total)

    turned = pltpu.roll(spectra[...], C - step * CB, 1)
    sums = [total[i] for i in range(4)]
    for j in range(CB):
        column = jnp.broadcast_to(turned[:, j : j + 1], (64, C))
        real, imag = column[:32], column[32:]
        for s, w in ((0, weight), (1, direction)):
            wr, wi = w[0, j].astype(F32), w[1, j].astype(F32)
            sums[2 * s] = sums[2 * s] + (wr * real - wi * imag)
            sums[2 * s + 1] = sums[2 * s + 1] + (wr * imag + wi * real)
    for i in range(4):
        total[i] = sums[i]

    @pl.when(step == C // CB - 1)
    def _():
        out = dot(xi[...], three(jnp.concatenate(sums, axis=0))).reshape(NX, 8, C)
        planes[:, 0] = out
        planes[:, 1] = out


def mix_stage(received, weight, direction):
    xf = x_forward_table(1, FORWARD_FACTOR)
    xi = x_inverse_table(INVERSE_FACTOR)
    weight = weight.reshape(2, C, 32, C)
    direction = direction.reshape(2, C, 32, C)
    moving = pl.BlockSpec((2, CB, 32, C), lambda i: (0, i, 0, 0))
    return pl.pallas_call(
        mix_kernel,
        grid=(C // CB,),
        in_specs=[whole(received.shape), moving, moving, whole(xf.shape), whole(xi.shape)],
        out_specs=(whole((64, C)), whole((NX, 2, 8, C))),
        out_shape=(jax.ShapeDtypeStruct((64, C), F32), jax.ShapeDtypeStruct((NX, 2, 8, C), F32)),
        scratch_shapes=[pltpu.VMEM((4, 32, C), F32)],
        compiler_params=params(),
    )(received, weight, direction, jnp.asarray(xf), jnp.asarray(xi))


def outer_kernel(received, spectra, xf, gradient, curvature, adjoint):
    step = pl.program_id(0)

    @pl.when(step == 0)
    def _():
        adjoint[...] = tall_dot(xf[...], received[...])

    turned = pltpu.roll(spectra[...], C - step * CB, 1)
    pieces = [adjoint[32 * i : 32 * i + 32, :] for i in range(4)]
    for j in range(CB):
        column = jnp.broadcast_to(turned[:, j : j + 1], (64, C))
        real, imag = column[:32], column[32:]
        for s, sink in ((0, gradient), (1, curvature)):
            re, im = pieces[2 * s], pieces[2 * s + 1]
            sink[0, j] = (real * re + imag * im).astype(BF16)
            sink[1, j] = (real * im - imag * re).astype(BF16)


def outer_stage(received, spectra):
    xf = x_forward_table(2, INVERSE_FACTOR)
    moving = pl.BlockSpec((2, CB, 32, C), lambda i: (0, i, 0, 0))
    shape = jax.ShapeDtypeStruct((2, C, 32, C), BF16)
    return pl.pallas_call(
        outer_kernel,
        grid=(C // CB,),
        in_specs=[whole(received.shape), whole(spectra.shape), whole(xf.shape)],
        out_specs=(moving, moving),
        out_shape=(shape, shape),
        scratch_shapes=[pltpu.VMEM((128, C), F32)],
        compiler_params=params(),
    )(received, spectra, jnp.asarray(xf))


def to_owners(keep, give):
    summed = keep + lax.ppermute(give, "co", [(0, 1), (1, 0)])
    return lax.all_to_all(summed.reshape(2 * NX, -1, C), WIDE, 0, 0, tiled=True)


def state_modes(cells, core, column):
    a = angles(np.arange(NZ), np.arange(MZ), NZ)
    z_table = np.stack([np.cos(a), -np.sin(a)], axis=1).astype(np.float32)
    rows = np.arange(NY)
    r = rotation(rows, signed(MY), NY, -1.0).transpose(1, 2, 3, 0)
    y_table = r.reshape(2, COLUMNS, ROWS, MY, 2).astype(np.float32)
    y_table = lax.dynamic_index_in_dim(jnp.asarray(y_table), column, 1, keepdims=False)
    along_z = jnp.einsum("yzc,zpk->ypkc", cells, z_table, precision=lax.Precision.HIGHEST)
    modes = jnp.einsum("ypkc,pyjq->jkqc", along_z, y_table, precision=lax.Precision.HIGHEST)
    split = modes.reshape(MY, 2, 2, 2, 2, 2, C)
    keep = lax.dynamic_index_in_dim(split, core, 3, keepdims=False)
    give = lax.dynamic_index_in_dim(split, 1 - core, 3, keepdims=False)
    return keep, give


def local(state, target, spectral_weight, direction_weight, inner_weight, outer_weight):
    column = lax.axis_index(COL)
    core = lax.axis_index("co")

    def pick(table, index):
        return lax.dynamic_index_in_dim(jnp.asarray(table), index, 0, keepdims=False)

    yi, yf = (pick(t, column) for t in y_tables())
    zi, zf = (pick(t, core) for t in z_tables())
    state_rows = state[:, 0].transpose(1, 2, 0)
    target_rows = target[:, 0].transpose(1, 2, 0).reshape(ROWS * NZ, C)
    received = to_owners(*state_modes(state_rows.astype(F32), core, column))
    spectra, planes = mix_stage(received.reshape(512, C), spectral_weight, direction_weight)
    arrived = lax.all_to_all(planes.reshape(2 * NX, 8, C), WIDE, 0, 0, tiled=True).reshape(1024, C)
    other = lax.ppermute(arrived, "co", [(0, 1), (1, 0)])
    keep, give = field_stage(
        arrived, other, state_rows.reshape(ROWS * NZ, C), target_rows, inner_weight, outer_weight, yi, zi, zf, yf
    )
    adjoint = to_owners(keep, give)
    gradient, curvature = outer_stage(adjoint.reshape(1024, C), spectra)
    shape = (2, C, MX, 2, C)
    return gradient.reshape(shape), curvature.reshape(shape)


def solution(mesh):
    fine = Mesh(mesh.devices.reshape(2, 4, 8, 2, 2), GX + COL)
    grid = P(None, GX, COL, None)
    blocks = P(None, None, None, GX + COL, None)
    return jax.shard_map(
        local,
        mesh=fine,
        in_specs=(grid, grid, blocks, blocks, P(), P()),
        out_specs=(blocks, blocks),
        check_vma=False,
    )
```

profile of v0, /device:TPU:2, one launch (start us, length us, event | category | flops | bytes accessed | tf_op | source)
XLA Modules:
  0.0 122.1 jit_solution(8854461697103067950)
XLA Ops:
  0.6 2.0 %copy.36 = bf16[32,128,128]{2,1,0:T(8,128)(2,1)S(1)} copy(bf16[32,128,128]{1,0,2:T(8,128)(2,1)} %bitcast.72) | data formatting | bytes 2097152 | tf_op jit(solution)/shard_map/transpose | solution.py:337
  2.6 0.5 convolution_bitcast_fusion
  3.2 1.7 %fusion.1 = f32[32,2,16,128,1]{3,0,4,2,1:T(8,128)S(1)} fusion(f32[32,2,16,128]{3,2,0,1:T(8,128)S(1)} %convolution_bitcast_fusion, f32[2,4,32,32,2]{2,3,0,4,1:T(8,128)} %constant.60.clone, s32[]{:T(128)S(6)} %select_n.18), kind=kOutput, calls=%fused_computation.2 | convolution fusion | flops 100663296 | bytes 1114116 | tf_op jit(solution)/shard_map/ypkc,pyjq->jkqc/dot_general | solution.py:321
  4.9 0.1 constant_dynamic-slice_fusion.1
  5.0 0.1 collective-permute-start
  5.1 1.5 %collective-permute-done = f32[32,2,2,2,2,128]{5,0,4,3,2,1:T(8,128)S(1)} collective-permute-done((f32[32,2,2,2,2,128]{5,0,4,3,2,1:T(8,128)S(1)}, f32[32,2,2,2,2,128]{5,0,4,3,2,1:T(8,128)S(1)}, u32[]{:S(2)}, u32[]{:S(2)}) %collective-permute-start) | collective-permute-done | bytes 262176 | tf_op jit(solution)/shard_map/ppermute | solution.py:309
  6.7 0.2 copy.40
  6.9 0.2 copy.41
  7.1 29.0 %all_to_all.15 = f32[128,4,128]{2,1,0:T(4,128)S(1)} all-to-all(f32[128,4,128]{2,1,0:T(4,128)S(1)} %copy.41), channel_id=1, replica_groups=mesh['xl'=2,'y'=4,'z'=8,'xh'=2,'co'=2] {'xl','y','z','xh'}, dimensions={0} | all-to-all | bytes 524288 | tf_op jit(solution)/shard_map/all_to_all | solution.py:310
  36.1 3.6 %shard_map.158 = (f32[64,128]{1,0:T(8,128)S(1)}, f32[64,2,8,128]{3,2,1,0:T(8,128)S(1)}) custom-call(f32[512,128]{1,0:T(8,128)S(1)} %bitcast.67, bf16[2,128,32,128]{3,2,1,0:T(8,128)(2,1)S(1)} %bitcast.62, bf16[2,128,32,128]{3,2,1,0:T(8,128)(2,1)S(1)} %bitcast.63, bf16[128,512]{1,0:T(8,128)(2,1)S(1)} %copy-done.7, bf16[512,384]{1,0:T(8,128)(2,1)S(1)} %copy-done.6), custom_call_target="tpu_custom_call" | custom-call | tf_op jit(solution)/shard_map/pallas_call | solution.py:264
  39.8 24.3 %all_to_all.16 = f32[128,8,128]{2,1,0:T(8,128)S(1)} all-to-all(f32[128,8,128]{2,1,0:T(8,128)S(1)} %bitcast.68), channel_id=1, replica_groups=mesh['xl'=2,'y'=4,'z'=8,'xh'=2,'co'=2] {'xl','y','z','xh'}, dimensions={0} | all-to-all | bytes 1048576 | tf_op jit(solution)/shard_map/all_to_all | solution.py:341
  64.1 0.1 copy.44
  64.2 0.8 copy.45
  65.0 1.9 %copy.43 = bf16[32,128,128]{2,1,0:T(8,128)(2,1)S(1)} copy(bf16[32,128,128]{1,0,2:T(8,128)(2,1)} %bitcast.73) | data formatting | bytes 2097152 | tf_op jit(solution)/shard_map/transpose | solution.py:338
  67.0 0.7 dynamic-slice_bitcast_fusion.3.zf
  67.7 0.8 dynamic-slice_bitcast_fusion.1.zi
  68.5 0.8 dynamic-slice_bitcast_fusion
  69.2 0.9 copy-done.5
  70.1 17.6 %shard_map.159 = (f32[1024,128]{1,0:T(8,128)S(1)}, f32[1024,128]{1,0:T(8,128)S(1)}) custom-call(f32[1024,128]{1,0:T(8,128)S(1)} %bitcast.66, f32[1024,128]{1,0:T(8,128)S(1)} %collective-permute-done.1.other, bf16[4096,128]{1,0:T(8,128)(2,1)S(1)} %bitcast.60, bf16[4096,128]{1,0:T(8,128)(2,1)S(1)} %bitcast.61, bf16[128,512]{1,0:T(8,128)(2,1)S(1)} %copy-done.3, ...), custom_call_target="tpu_custom_call" | custom-call | tf_op jit(solution)/shard_map/pallas_call | solution.py:220
  87.8 0.6 collective-permute-start.2
  88.4 1.5 %collective-permute-done.2 = f32[1024,128]{1,0:T(8,128)S(1)} collective-permute-done((f32[1024,128]{1,0:T(8,128)S(1)}, f32[1024,128]{1,0:T(8,128)S(1)}, u32[]{:S(2)}, u32[]{:S(2)}) %collective-permute-start.2) | collective-permute-done | bytes 524320 | tf_op jit(solution)/shard_map/ppermute | solution.py:309
  89.9 0.1 add_bitcast_fusion
  90.0 27.1 %all_to_all.17 = f32[128,8,128]{2,1,0:T(8,128)S(1)} all-to-all(f32[128,8,128]{2,1,0:T(8,128)S(1)} %add_bitcast_fusion), channel_id=1, replica_groups=mesh['xl'=2,'y'=4,'z'=8,'xh'=2,'co'=2] {'xl','y','z','xh'}, dimensions={0} | all-to-all | bytes 1048576 | tf_op jit(solution)/shard_map/all_to_all | solution.py:310
  117.1 5.1 %shard_map.160 = (bf16[2,128,32,128]{3,2,1,0:T(8,128)(2,1)}, bf16[2,128,32,128]{3,2,1,0:T(8,128)(2,1)}) custom-call(f32[1024,128]{1,0:T(8,128)S(1)} %bitcast.64, f32[64,128]{1,0:T(8,128)S(1)} %copy-done.9, bf16[256,1024]{1,0:T(8,128)(2,1)S(1)} %copy-done.2), custom_call_target="tpu_custom_call" | custom-call | tf_op jit(solution)/shard_map/pallas_call | solution.py:297
  (25 shorter events, 0.1 us)
Async XLA Ops:
  0.6 2.0 %copy-start.10 = (f32[128,2,16,1]{0,2,3,1:T(8,128)S(1)}, f32[128,2,16,1]{0,2,3,1:T(8,128)}, u32[]{:S(2)}) copy-start(f32[128,2,16,1]{0,2,3,1:T(8,128)} %constant.69) | copy-start | bytes 49156
  3.2 32.9 %copy-start.1 = (bf16[2,128,16,2,128]{4,3,2,1,0:T(2,128)(2,1)S(1)}, bf16[2,128,16,2,128]{4,3,2,1,0:T(2,128)(2,1)}, u32[]{:S(2)}) copy-start(bf16[2,128,16,2,128]{4,3,2,1,0:T(2,128)(2,1)} %param.18) | copy-start | bytes 6291460
  4.9 31.2 %copy-start = (bf16[2,128,16,2,128]{4,3,2,1,0:T(2,128)(2,1)S(1)}, bf16[2,128,16,2,128]{4,3,2,1,0:T(2,128)(2,1)}, u32[]{:S(2)}) copy-start(bf16[2,128,16,2,128]{4,3,2,1,0:T(2,128)(2,1)} %param.17) | copy-start | bytes 6291460
  4.9 31.2 %copy-start.6 = (bf16[512,384]{1,0:T(8,128)(2,1)S(1)}, bf16[512,384]{1,0:T(8,128)(2,1)}, u32[]{:S(2)}) copy-start(bf16[512,384]{1,0:T(8,128)(2,1)} %constant.63.clone.xi) | copy-start | bytes 1179652
  4.9 31.2 %copy-start.7 = (bf16[128,512]{1,0:T(8,128)(2,1)S(1)}, bf16[128,512]{1,0:T(8,128)(2,1)}, u32[]{:S(2)}) copy-start(bf16[128,512]{1,0:T(8,128)(2,1)} %constant.62.clone.xf) | copy-start | bytes 393220
  5.0 1.6 %collective-permute-start = (f32[32,2,2,2,2,128]{5,0,4,3,2,1:T(8,128)S(1)}, f32[32,2,2,2,2,128]{5,0,4,3,2,1:T(8,128)S(1)}, u32[]{:S(2)}, u32[]{:S(2)}) collective-permute-start(f32[32,2,2,2,2,128]{5,0,4,3,2,1:T(8,128)S(1)} %bitcast.75), channel_id=1, source_target_pairs={{0,1},{1,0},{2,3},{3,2},{4,5},{5,4},{6,7},{7,6},{8,9},{9,8},{10,11... | collective-permute-start | bytes 786440 | tf_op jit(solution)/shard_map/ppermute | solution.py:309
  36.1 28.0 %copy-start.3 = (bf16[128,512]{1,0:T(8,128)(2,1)S(1)}, bf16[128,512]{1,0:T(8,128)(2,1)}, u32[]{:S(2)}) copy-start(bf16[128,512]{1,0:T(8,128)(2,1)} %w1.1) | copy-start | bytes 393220
  36.1 28.1 %copy-start.4 = (bf16[512,128]{1,0:T(8,128)(2,1)S(1)}, bf16[512,128]{1,0:T(8,128)(2,1)}, u32[]{:S(2)}) copy-start(bf16[512,128]{1,0:T(8,128)(2,1)} %w2.1) | copy-start | bytes 393220
  39.7 25.3 %copy-start.8 = (f32[64,128]{1,0:T(8,128)}, f32[64,128]{1,0:T(8,128)S(1)}, u32[]{:S(2)}) copy-start(f32[64,128]{1,0:T(8,128)S(1)} %get-tuple-element.11.spectra) | copy-start | bytes 98308
  64.1 5.1 %collective-permute-start.1 = (f32[1024,128]{1,0:T(8,128)S(1)}, f32[1024,128]{1,0:T(8,128)S(1)}, u32[]{:S(2)}, u32[]{:S(2)}) collective-permute-start(f32[1024,128]{1,0:T(8,128)S(1)} %bitcast.65), channel_id=1, source_target_pairs={{0,1},{1,0},{2,3},{3,2},{4,5},{5,4},{6,7},{7,6},{8,9},{9,8},{10,11... | collective-permute-start | bytes 1572872 | tf_op jit(solution)/shard_map/ppermute | solution.py:342
  69.2 0.9 copy-start.5
  87.8 29.3 %copy-start.2 = (bf16[256,1024]{1,0:T(8,128)(2,1)S(1)}, bf16[256,1024]{1,0:T(8,128)(2,1)}, u32[]{:S(2)}) copy-start(bf16[256,1024]{1,0:T(8,128)(2,1)} %constant.64.clone.xf) | copy-start | bytes 1572868
  87.8 29.3 %copy-start.9 = (f32[64,128]{1,0:T(8,128)S(1)}, f32[64,128]{1,0:T(8,128)}, u32[]{:S(2)}) copy-start(f32[64,128]{1,0:T(8,128)} %copy-done.8) | copy-start | bytes 98308
  87.8 2.1 %collective-permute-start.2 = (f32[1024,128]{1,0:T(8,128)S(1)}, f32[1024,128]{1,0:T(8,128)S(1)}, u32[]{:S(2)}, u32[]{:S(2)}) collective-permute-start(f32[1024,128]{1,0:T(8,128)S(1)} %get-tuple-element.10), channel_id=1, source_target_pairs={{0,1},{1,0},{2,3},{3,2},{4,5},{5,4},{6,7},{7,6},{8,9},{9,8},{10,11... | collective-permute-start | bytes 1572872 | tf_op jit(solution)/shard_map/ppermute | solution.py:309
where the time goes:
time: 123 us; the launch traced here: 122 us
  blocking collectives  80.4 us (65%)
  Pallas kernels  26.3 us (21%)
  local copies, waits for them, and re-layouts  8.45 us (7%)
  waiting for transfers between devices  3.06 us (2%)
  matrix products  2.26 us (2%)
    all_to_all x2, blocking collectives, to_owners(): return lax.all_to_all(summed.reshape(2 * NX, -1, C), WIDE, 0, 0, tiled=True)  56.1 us
    all_to_all x1, blocking collectives, local(): lax.all_to_all(planes.reshape(2 * NX, 8, C), WIDE, 0, 0, tiled=True)  24.3 us
    pallas_call x1, Pallas kernels, field_stage(): pl.pallas_call(field_kernel, grid=(ROWS // ROWS_A_STEP,), in_specs=specs,...  17.6 us
    pallas_call x1, Pallas kernels, outer_stage(): pl.pallas_call(outer_kernel, grid=(C // CB,), in_specs=[whole(received.sh...  5.06 us
    pallas_call x1, Pallas kernels, mix_stage(): pl.pallas_call(mix_kernel, grid=(C // CB,), in_specs=[whole(received.shap...  3.61 us
    ppermute x2, waiting for transfers between devices, to_owners(): summed = keep + lax.ppermute(give, 'co', [(0, 1), (1, 0)])  3.06 us
  transfers between devices with their start and end apart: 3, of which 2 were waited for; matrix products, arithmetic and copies ran while one was open for 4% of the time, Pallas kernels for 0%

commit v1 on v0

--- a/solution.py
+++ b/solution.py
@@ -25,13 +25,13 @@
 FORWARD_FACTOR = 1.0 / math.sqrt(POINTS)
 INVERSE_FACTOR = 2.0 / math.sqrt(KEPT)
 LOSS_SCALE = 0.5 * math.sqrt(KEPT / POINTS)
-ROWS_A_STEP = 4
+ROWS_A_STEP = 16
 CHUNK = ROWS_A_STEP * NZ
-CB = 16
+CB = 64
 
 GX = ("xl", "y", "z")
 COL = ("xh", "co")
-WIDE = GX + ("xh",)
+WIDE = ("y", "z", "xl", "xh")
 F32 = jnp.float32
 BF16 = jnp.bfloat16
 
@@ -102,8 +102,12 @@
     return np.stack(inverse), np.stack(forward)
 
 
+def x_places():
+    return np.arange(NX).reshape(2, 4, 8).transpose(1, 2, 0).reshape(NX)
+
+
 def x_forward_table(fields, factor):
-    r = rotation(np.arange(NX), signed(MX), NX, -1.0) * factor
+    r = rotation(x_places(), signed(MX), NX, -1.0) * factor
     t = np.zeros((fields, 2, MX, 2, NX, 2, 2, fields, 2))
     for s in range(fields):
         for m in range(2):
@@ -113,7 +117,7 @@
 
 
 def x_inverse_table(factor):
-    r = rotation(np.arange(NX), signed(MX), NX, 1.0) * factor
+    r = rotation(x_places(), signed(MX), NX, 1.0) * factor
     t = np.zeros((NX, 2, 2, 2, 2, 2, MX, 2))
     for s in range(2):
         for m in range(2):
@@ -142,28 +146,82 @@
     return first[:rows] + first[rows:] + dot(table[:rows], low)
 
 
+def mode_rows(k, extra):
+    zh, xh, m = k % 8 // 4, k % 4 // 2, k % 2
+    return [pl.ds(zh * 32 + xl * 16 + xh * 8 + m * 4 + extra, 16, stride=64) for xl in range(2)]
+
+
+def state_rows_of(k, extra):
+    zh, xh, m = k % 8 // 4, k % 4 // 2, k % 2
+    return [pl.ds(zh * 16 + xl * 8 + xh * 4 + m * 2 + extra, 16, stride=32) for xl in range(2)]
+
+
+def rows_forward(values, fields, table, after, y):
+    rows = tall_dot(table, values)
+    start = pl.multiple_of(y * 2 * MZ, 2 * MZ)
+    for s in range(fields):
+        after[s, pl.ds(start, 2 * MZ), :] = rows[:, s * C : (s + 1) * C]
+
+
+def columns_forward(fields, table, after, keep, give):
+    pieces = [(k, s) for k in range(MZ) for s in range(fields)]
+    for pair in zip(pieces[::2], pieces[1::2]):
+        parts = []
+        for k, s in pair:
+            q = [after[s, pl.ds(2 * k + i, ROWS, stride=2 * MZ), :] for i in range(2)]
+            parts.append(jnp.concatenate(q, axis=0))
+        rows = dot(table, three(jnp.concatenate(parts, axis=1)))
+        for i, (k, s) in enumerate(pair):
+            sink = keep if k < 8 else give
+            for r in range(2):
+                places = mode_rows(k, 2 * s + r) if fields == 2 else state_rows_of(k, r)
+                for xl, place in enumerate(places):
+                    at = r * MY + xl * 16
+                    sink[place, :] = rows[at : at + 16, i * C : (i + 1) * C]
+
+
+def state_kernel(place, state, zf, yf, keep, give, after):
+    for y in range(0, ROWS, 2):
+        pair = jnp.concatenate([state[(y + i) * NZ : (y + i + 1) * NZ] for i in range(2)], axis=1)
+        rows = dot(zf[0], pair)
+        rows = rows[: 2 * MZ] + rows[2 * MZ :]
+        for i in range(2):
+            after[0, pl.ds((y + i) * 2 * MZ, 2 * MZ), :] = rows[:, i * C : (i + 1) * C]
+    columns_forward(1, yf[0], after, keep, give)
+
+
 def field_kernel(
-    mine, other, state, target, w1, w2, w1t, w2t, yi, zi, zf, yf, keep, give, half, after
+    place, mine, other, state, target, w1_, w2_, yi_, zi_, zf_, yf_, keep, give,
+    half, after, w1, w2, w1t, w2t, yi, zi, zf, yf, arrivals
 ):
     step = pl.program_id(0)
 
     @pl.when(step == 0)
     def _():
+        column, core = place[0], place[1]
+        pairs = [(yi_.at[column], yi), (zi_.at[core], zi), (w1_, w1), (w2_, w2), (zf_.at[core], zf), (yf_.at[column], yf)]
+        copies = [pltpu.make_async_copy(a, b, arrivals.at[i]) for i, (a, b) in enumerate(pairs)]
+        for copy in copies:
+            copy.start()
+        copies[0].wait()
         for k in range(MZ):
             source = mine if k < 8 else other
-            base = (k % 8) // 2 * 8 + k % 2 * 4
             parts = []
             for s in range(2):
-                p = [source[pl.ds(base + 2 * s + i, MY, stride=32), :] for i in range(2)]
+                p = [source[place, :] for i in range(2) for place in mode_rows(k, 2 * s + i)]
                 parts.append(jnp.concatenate(p, axis=0))
             rows = dot(yi[...], three(jnp.concatenate(parts, axis=1)))
             for s in range(2):
                 half[s, pl.ds(k * 64, 64), :] = rows[:, s * C : (s + 1) * C]
-
+        for copy in copies[1:]:
+            copy.wait()
+        w1t[...] = w1[...].T
+        w2t[...] = w2[...].T
+
+    first = step * ROWS_A_STEP
     fields = []
     for i in range(ROWS_A_STEP):
-        y = step * ROWS_A_STEP + i
-        taken = [half[s, pl.ds(y, 2 * MZ, stride=ROWS), :] for s in range(2)]
+        taken = [half[s, pl.ds(first + i, 2 * MZ, stride=ROWS), :] for s in range(2)]
         fields.append(dot(zi[...], three(jnp.concatenate(taken, axis=1))))
     fields = jnp.concatenate(fields, axis=0).astype(BF16)
     primal, tangent = fields[:, :C], fields[:, C:]
@@ -182,57 +240,73 @@
     delta_primal = (slope * back_primal).astype(BF16)
     bend = density * (2.0 - hidden * hidden)
     delta_tangent = (bend * hidden_tangent * back_primal + slope * back_tangent).astype(BF16)
-    cotangents = jnp.concatenate(
-        [seed_primal + dot(delta_primal, w1t[...]), seed_tangent + dot(delta_tangent, w1t[...])], axis=1
-    )
+    cotangents = [seed_primal + dot(delta_primal, w1t[...]), seed_tangent + dot(delta_tangent, w1t[...])]
+    cotangents = jnp.concatenate(cotangents, axis=1)
     for i in range(ROWS_A_STEP):
-        rows = tall_dot(zf[...], cotangents[i * NZ : (i + 1) * NZ])
-        start = pl.multiple_of((step * ROWS_A_STEP + i) * 2 * MZ, 2 * MZ)
-        for s in range(2):
-            after[s, pl.ds(start, 2 * MZ), :] = rows[:, s * C : (s + 1) * C]
+        rows_forward(cotangents[i * NZ : (i + 1) * NZ], 2, zf[...], after, first + i)
 
     @pl.when(step == ROWS // ROWS_A_STEP - 1)
     def _():
-        for k in range(MZ):
-            sink = keep if k < 8 else give
-            base = (k % 8) // 2 * 8 + k % 2 * 4
-            parts = []
-            for s in range(2):
-                q = [after[s, pl.ds(2 * k + i, ROWS, stride=2 * MZ), :] for i in range(2)]
-                parts.append(jnp.concatenate(q, axis=0))
-            rows = dot(yf[...], three(jnp.concatenate(parts, axis=1)))
-            for s in range(2):
-                for r in range(2):
-                    sink[pl.ds(base + 2 * s + r, MY, stride=32), :] = rows[
-                        r * MY : (r + 1) * MY, s * C : (s + 1) * C
-                    ]
+        columns_forward(2, yf[...], after, keep, give)
 
 
 def whole(shape):
     return pl.BlockSpec(shape, lambda i: (0,) * len(shape))
 
 
-def field_stage(mine, other, state, target, w1, w2, yi, zi, zf, yf):
-    operands = (mine, other, state, target, w1, w2, w1.T, w2.T, yi, zi, zf, yf)
-    moving = pl.BlockSpec((CHUNK, C), lambda i: (i, 0))
-    specs = [moving if i in (2, 3) else whole(a.shape) for i, a in enumerate(operands)]
-    shape = jax.ShapeDtypeStruct((1024, C), F32)
+def still(shape):
+    return pl.BlockSpec(shape, lambda i, place: (0,) * len(shape))
+
+
+def picked(table, index):
+    return pl.BlockSpec((1,) + table.shape[1:], lambda i, place: (place[index], 0, 0))
+
+
+def call_rows(kernel, place, operands, specs, out_rows, scratch, steps):
+    shape = jax.ShapeDtypeStruct((out_rows, C), F32)
     return pl.pallas_call(
-        field_kernel,
-        grid=(ROWS // ROWS_A_STEP,),
-        in_specs=specs,
-        out_specs=(whole((1024, C)), whole((1024, C))),
+        kernel,
+        grid_spec=pltpu.PrefetchScalarGridSpec(
+            num_scalar_prefetch=1,
+            grid=(steps,),
+            in_specs=specs,
+            out_specs=(still((out_rows, C)), still((out_rows, C))),
+            scratch_shapes=scratch,
+        ),
         out_shape=(shape, shape),
-        scratch_shapes=[pltpu.VMEM((2, 1024, C), F32), pltpu.VMEM((2, 1024, C), F32)],
         compiler_params=params(),
-    )(*operands)
-
-
-def mix_kernel(received, weight, direction, xf, xi, spectra, planes, total):
+    )(place, *operands)
+
+
+MOVING = pl.BlockSpec((CHUNK, C), lambda i, place: (i, 0))
+
+
+def state_stage(place, state, zf, yf):
+    specs = [still(state.shape), picked(zf, 1), picked(yf, 0)]
+    return call_rows(state_kernel, place, (state, zf, yf), specs, 512, [pltpu.VMEM((1, 1024, C), F32)], 1)
+
+
+def field_stage(place, mine, other, state, target, weights, tables):
+    operands = (mine, other, state, target, *weights, *tables)
+    specs = [still(mine.shape), still(other.shape), MOVING, MOVING]
+    specs += [pl.BlockSpec(memory_space=pltpu.HBM)] * 6
+    scratch = [pltpu.VMEM((2, 1024, C), F32), pltpu.VMEM((2, 1024, C), F32)]
+    scratch += [pltpu.VMEM((C, FF), BF16), pltpu.VMEM((FF, C), BF16), pltpu.VMEM((FF, C), BF16), pltpu.VMEM((C, FF), BF16)]
+    scratch += [pltpu.VMEM(t.shape[1:], BF16) for t in tables]
+    scratch += [pltpu.SemaphoreType.DMA((6,))]
+    return call_rows(field_kernel, place, operands, specs, 1024, scratch, ROWS // ROWS_A_STEP)
+
+
+def mix_kernel(received, weight, direction, xf_, xi_, spectra, planes, total, xf, xi, arrivals):
     step = pl.program_id(0)
+    first = pltpu.make_async_copy(xf_, xf, arrivals.at[0])
+    second = pltpu.make_async_copy(xi_, xi, arrivals.at[1])
 
     @pl.when(step == 0)
     def _():
+        first.start()
+        second.start()
+        first.wait()
         spectra[...] = tall_dot(xf[...], received[...])
         total[...] = jnp.zeros_like(total)
 
@@ -250,6 +324,7 @@
 
     @pl.when(step == C // CB - 1)
     def _():
+        second.wait()
         out = dot(xi[...], three(jnp.concatenate(sums, axis=0))).reshape(NX, 8, C)
         planes[:, 0] = out
         planes[:, 1] = out
@@ -264,10 +339,15 @@
     return pl.pallas_call(
         mix_kernel,
         grid=(C // CB,),
-        in_specs=[whole(received.shape), moving, moving, whole(xf.shape), whole(xi.shape)],
+        in_specs=[whole(received.shape), moving, moving] + [pl.BlockSpec(memory_space=pltpu.HBM)] * 2,
         out_specs=(whole((64, C)), whole((NX, 2, 8, C))),
         out_shape=(jax.ShapeDtypeStruct((64, C), F32), jax.ShapeDtypeStruct((NX, 2, 8, C), F32)),
-        scratch_shapes=[pltpu.VMEM((4, 32, C), F32)],
+        scratch_shapes=[
+            pltpu.VMEM((4, 32, C), F32),
+            pltpu.VMEM(xf.shape, BF16),
+            pltpu.VMEM(xi.shape, BF16),
+            pltpu.SemaphoreType.DMA((2,)),
+        ],
         compiler_params=params(),
     )(received, weight, direction, jnp.asarray(xf), jnp.asarray(xi))
 
@@ -305,46 +385,31 @@
     )(received, spectra, jnp.asarray(xf))
 
 
-def to_owners(keep, give):
-    summed = keep + lax.ppermute(give, "co", [(0, 1), (1, 0)])
-    return lax.all_to_all(summed.reshape(2 * NX, -1, C), WIDE, 0, 0, tiled=True)
-
-
-def state_modes(cells, core, column):
-    a = angles(np.arange(NZ), np.arange(MZ), NZ)
-    z_table = np.stack([np.cos(a), -np.sin(a)], axis=1).astype(np.float32)
-    rows = np.arange(NY)
-    r = rotation(rows, signed(MY), NY, -1.0).transpose(1, 2, 3, 0)
-    y_table = r.reshape(2, COLUMNS, ROWS, MY, 2).astype(np.float32)
-    y_table = lax.dynamic_index_in_dim(jnp.asarray(y_table), column, 1, keepdims=False)
-    along_z = jnp.einsum("yzc,zpk->ypkc", cells, z_table, precision=lax.Precision.HIGHEST)
-    modes = jnp.einsum("ypkc,pyjq->jkqc", along_z, y_table, precision=lax.Precision.HIGHEST)
-    split = modes.reshape(MY, 2, 2, 2, 2, 2, C)
-    keep = lax.dynamic_index_in_dim(split, core, 3, keepdims=False)
-    give = lax.dynamic_index_in_dim(split, 1 - core, 3, keepdims=False)
-    return keep, give
+def exchange(rows):
+    return lax.all_to_all(rows.reshape(2 * NX, -1, C), WIDE, 0, 0, tiled=True).reshape(rows.shape)
+
+
+def summed(keep, give):
+    return keep + lax.ppermute(give, "co", [(0, 1), (1, 0)])
 
 
 def local(state, target, spectral_weight, direction_weight, inner_weight, outer_weight):
-    column = lax.axis_index(COL)
-    core = lax.axis_index("co")
-
-    def pick(table, index):
-        return lax.dynamic_index_in_dim(jnp.asarray(table), index, 0, keepdims=False)
-
-    yi, yf = (pick(t, column) for t in y_tables())
-    zi, zf = (pick(t, core) for t in z_tables())
-    state_rows = state[:, 0].transpose(1, 2, 0)
-    target_rows = target[:, 0].transpose(1, 2, 0).reshape(ROWS * NZ, C)
-    received = to_owners(*state_modes(state_rows.astype(F32), core, column))
-    spectra, planes = mix_stage(received.reshape(512, C), spectral_weight, direction_weight)
-    arrived = lax.all_to_all(planes.reshape(2 * NX, 8, C), WIDE, 0, 0, tiled=True).reshape(1024, C)
+    place = jnp.stack([lax.axis_index(COL), lax.axis_index("co")]).astype(jnp.int32)
+    yi, yf = (jnp.asarray(t) for t in y_tables())
+    zi, zf = (jnp.asarray(t) for t in z_tables())
+
+    def rows_of(cells):
+        return cells[:, 0].transpose(1, 2, 0).reshape(ROWS * NZ, C)
+
+    state_rows = rows_of(state)
+    received = exchange(summed(*state_stage(place, state_rows, zf, yf)))
+    spectra, planes = mix_stage(received, spectral_weight, direction_weight)
+    arrived = exchange(planes.reshape(1024, C))
     other = lax.ppermute(arrived, "co", [(0, 1), (1, 0)])
-    keep, give = field_stage(
-        arrived, other, state_rows.reshape(ROWS * NZ, C), target_rows, inner_weight, outer_weight, yi, zi, zf, yf
-    )
-    adjoint = to_owners(keep, give)
-    gradient, curvature = outer_stage(adjoint.reshape(1024, C), spectra)
+    weights = (inner_weight, outer_weight)
+    keep, give = field_stage(place, arrived, other, state_rows, rows_of(target), weights, (yi, zi, zf, yf))
+    adjoint = exchange(summed(keep, give))
+    gradient, curvature = outer_stage(adjoint, spectra)
     shape = (2, C, MX, 2, C)
     return gradient.reshape(shape), curvature.reshape(shape)
 

time: 123 us -> 118 us (0.959)
  matrix products: 2.26 us -> 0 us
  Pallas kernels: 26.3 us -> 24.4 us
  local copies, waits for them, and re-layouts: 8.45 us -> 6.89 us
    squeeze x3 -> x0, local copies, waits for them, and re-layouts: 2.27 us -> none  [pick(): lax.dynamic_index_in_dim(jnp.asarray(table), index, 0, keepdims=False)]
    dot_general x2 -> x0, matrix products: 2.26 us -> none  [the longest x1 1.72 us: state_modes(): jnp.einsum('ypkc,pyjq->jkqc', along_z, y_table, precision=lax.Precision.H...]
    pallas_call x1, Pallas kernels: 5.06 us -> 3.27 us  [outer_stage(): pl.pallas_call(outer_kernel, grid=(C // CB,), in_specs=[whole(received.sh...]
    unnamed x25 -> x22, local copies, waits for them, and re-layouts: 1.87 us -> 2.85 us
    pallas_call x1 -> x2, Pallas kernels: 17.6 us -> 18.1 us  [call_rows(): pl.pallas_call(kernel, grid_spec=pltpu.PrefetchScalarGridSpec(num_scalar_...]
  transfers between devices with their start and end apart: 3 -> 3, of which waited for: 2 -> 2; matrix products, arithmetic and copies ran while one was open for 4% -> 2% of each run, Pallas kernels for 0% -> 0%
where the time goes in v1:
time: 118 us; the launch traced here: 117 us
  blocking collectives  81.3 us (69%)
  Pallas kernels  24.4 us (21%)
  local copies, waits for them, and re-layouts  6.89 us (6%)
  waiting for transfers between devices  3.06 us (3%)
    all_to_all x3, blocking collectives, exchange(): lax.all_to_all(rows.reshape(2 * NX, -1, C), WIDE, 0, 0, tiled=True)  81.3 us
    pallas_call x2, Pallas kernels, call_rows(): pl.pallas_call(kernel, grid_spec=pltpu.PrefetchScalarGridSpec(num_scalar_...  18.1 us
    transpose x2, local copies, waits for them, and re-layouts, rows_of(): return cells[:, 0].transpose(1, 2, 0).reshape(ROWS * NZ, C)  4.05 us
    pallas_call x1, Pallas kernels, outer_stage(): pl.pallas_call(outer_kernel, grid=(C // CB,), in_specs=[whole(received.sh...  3.27 us
    pallas_call x1, Pallas kernels, mix_stage(): pl.pallas_call(mix_kernel, grid=(C // CB,), in_specs=[whole(received.shap...  3.11 us
    ppermute x2, waiting for transfers between devices, summed(): return keep + lax.ppermute(give, 'co', [(0, 1), (1, 0)])  3.06 us
    unnamed x22, local copies, waits for them, and re-layouts  2.85 us
  transfers between devices with their start and end apart: 3, of which 2 were waited for; matrix products, arithmetic and copies ran while one was open for 2% of the time, Pallas kernels for 0%

profile of v1, /device:TPU:2, one launch (start us, length us, event | category | flops | bytes accessed | tf_op | source)
XLA Modules:
  0.0 117.4 jit_solution(7343712017413300066)
XLA Ops:
  0.6 0.0 copy-start.5
  0.6 0.0 copy-start.2
  0.7 0.0 copy-start.9
  0.7 2.1 %copy.15 = bf16[32,128,128]{2,1,0:T(8,128)(2,1)S(1)} copy(bf16[32,128,128]{1,0,2:T(8,128)(2,1)} %bitcast.32) | data formatting | bytes 2097152 | tf_op jit(solution)/shard_map/transpose | solution.py:402
  2.8 0.1 pad_add_fusion.place
  2.9 1.4 %shard_map.140 = (f32[512,128]{1,0:T(8,128)S(1)}, f32[512,128]{1,0:T(8,128)S(1)}) custom-call(s32[2]{0:T(128)S(1)} %pad_add_fusion.place, bf16[4096,128]{1,0:T(8,128)(2,1)S(1)} %bitcast.21, bf16[2,64,128]{2,1,0:T(8,128)(2,1)S(1)} %copy-done.5, bf16[4,64,192]{2,1,0:T(8,128)(2,1)S(1)} %copy-done.2), custom_call_target="tpu_custom_call" | custom-call | tf_op jit(solution)/shard_map/pallas_call | solution.py:267
  4.3 0.1 collective-permute-start
  4.4 1.5 %collective-permute-done = f32[512,128]{1,0:T(8,128)S(1)} collective-permute-done((f32[512,128]{1,0:T(8,128)S(1)}, f32[512,128]{1,0:T(8,128)S(1)}, u32[]{:S(2)}, u32[]{:S(2)}) %collective-permute-start) | collective-permute-done | bytes 262176 | tf_op jit(solution)/shard_map/ppermute | solution.py:393
  6.0 29.6 %all_to_all.15 = f32[128,4,128]{2,1,0:T(4,128)S(1)} all-to-all(f32[128,4,128]{2,1,0:T(4,128)S(1)} %bitcast.31), channel_id=1, replica_groups=mesh['xl'=2,'y'=4,'z'=8,'xh'=2,'co'=2] {'y','z','xl','xh'}, dimensions={0} | all-to-all | bytes 524288 | tf_op jit(solution)/shard_map/all_to_all | solution.py:389
  35.6 0.0 copy-start.4
  35.6 1.0 copy-done.4
  36.6 3.1 %shard_map.141 = (f32[64,128]{1,0:T(8,128)S(1)}, f32[64,2,8,128]{3,2,1,0:T(8,128)S(1)}) custom-call(f32[512,128]{1,0:T(8,128)S(1)} %bitcast.29, bf16[2,128,32,128]{3,2,1,0:T(8,128)(2,1)S(1)} %bitcast.24, bf16[2,128,32,128]{3,2,1,0:T(8,128)(2,1)S(1)} %bitcast.25, bf16[128,512]{1,0:T(8,128)(2,1)S(1)} %copy-done.9, bf16[512,384]{1,0:T(8,128)(2,1)S(1)} %copy-done.4), custom_call_target="tpu_custom_call" | custom-call | tf_op jit(solution)/shard_map/pallas_call | solution.py:339
  39.7 0.0 copy-start.10
  39.7 25.4 %all_to_all.16 = f32[128,8,128]{2,1,0:T(8,128)S(1)} all-to-all(f32[128,8,128]{2,1,0:T(8,128)S(1)} %bitcast.30), channel_id=1, replica_groups=mesh['xl'=2,'y'=4,'z'=8,'xh'=2,'co'=2] {'y','z','xl','xh'}, dimensions={0} | all-to-all | bytes 1048576 | tf_op jit(solution)/shard_map/all_to_all | solution.py:389
  65.1 1.9 %copy.16 = bf16[32,128,128]{2,1,0:T(8,128)(2,1)S(1)} copy(bf16[32,128,128]{1,0,2:T(8,128)(2,1)} %bitcast.33) | data formatting | bytes 2097152 | tf_op jit(solution)/shard_map/transpose | solution.py:402
  67.1 0.9 copy-done.7
  68.0 0.9 copy-done.8
  68.9 16.7 %shard_map.142 = (f32[1024,128]{1,0:T(8,128)S(1)}, f32[1024,128]{1,0:T(8,128)S(1)}) custom-call(s32[2]{0:T(128)S(1)} %pad_add_fusion.place, f32[1024,128]{1,0:T(8,128)S(1)} %bitcast.28, f32[1024,128]{1,0:T(8,128)S(1)} %collective-permute-done.1.other, bf16[4096,128]{1,0:T(8,128)(2,1)S(1)} %bitcast.22, bf16[4096,128]{1,0:T(8,128)(2,1)S(1)} %bitcast.23, ...), custom_call_target="tpu_custom_call" | custom-call | tf_op jit(solution)/shard_map/pallas_call | solution.py:267
  85.5 0.0 copy-start.3
  85.6 0.6 collective-permute-start.2
  86.2 1.5 %collective-permute-done.2 = f32[1024,128]{1,0:T(8,128)S(1)} collective-permute-done((f32[1024,128]{1,0:T(8,128)S(1)}, f32[1024,128]{1,0:T(8,128)S(1)}, u32[]{:S(2)}, u32[]{:S(2)}) %collective-permute-start.2) | collective-permute-done | bytes 524320 | tf_op jit(solution)/shard_map/ppermute | solution.py:393
  87.7 0.1 add_bitcast_fusion
  87.8 26.3 %all_to_all.17 = f32[128,8,128]{2,1,0:T(8,128)S(1)} all-to-all(f32[128,8,128]{2,1,0:T(8,128)S(1)} %add_bitcast_fusion), channel_id=1, replica_groups=mesh['xl'=2,'y'=4,'z'=8,'xh'=2,'co'=2] {'y','z','xl','xh'}, dimensions={0} | all-to-all | bytes 1048576 | tf_op jit(solution)/shard_map/all_to_all | solution.py:389
  114.1 3.3 %shard_map.143 = (bf16[2,128,32,128]{3,2,1,0:T(8,128)(2,1)}, bf16[2,128,32,128]{3,2,1,0:T(8,128)(2,1)}) custom-call(f32[1024,128]{1,0:T(8,128)S(1)} %bitcast.26, f32[64,128]{1,0:T(8,128)S(1)} %get-tuple-element.15.spectra, bf16[256,1024]{1,0:T(8,128)(2,1)S(1)} %copy-done.3), custom_call_target="tpu_custom_call" | custom-call | tf_op jit(solution)/shard_map/pallas_call | solution.py:377
  (16 shorter events, 0.1 us)
Async XLA Ops:
  0.6 2.3 %copy-start.5 = (bf16[2,64,128]{2,1,0:T(8,128)(2,1)S(1)}, bf16[2,64,128]{2,1,0:T(8,128)(2,1)}, u32[]{:S(2)}) copy-start(bf16[2,64,128]{2,1,0:T(8,128)(2,1)} %constant.25.clone.zf.zf_) | copy-start | bytes 98308
  0.6 2.2 %copy-start.2 = (bf16[4,64,192]{2,1,0:T(8,128)(2,1)S(1)}, bf16[4,64,192]{2,1,0:T(8,128)(2,1)}, u32[]{:S(2)}) copy-start(bf16[4,64,192]{2,1,0:T(8,128)(2,1)} %constant.23.clone.yf.yf_) | copy-start | bytes 294916
  0.7 34.9 %copy-start = (bf16[2,128,16,2,128]{4,3,2,1,0:T(2,128)(2,1)S(1)}, bf16[2,128,16,2,128]{4,3,2,1,0:T(2,128)(2,1)}, u32[]{:S(2)}) copy-start(bf16[2,128,16,2,128]{4,3,2,1,0:T(2,128)(2,1)} %param.15) | copy-start | bytes 6291460
  0.7 34.9 %copy-start.9 = (bf16[128,512]{1,0:T(8,128)(2,1)S(1)}, bf16[128,512]{1,0:T(8,128)(2,1)}, u32[]{:S(2)}) copy-start(bf16[128,512]{1,0:T(8,128)(2,1)} %constant.26.clone.xf_) | copy-start | bytes 393220
  2.8 32.8 %copy-start.1 = (bf16[2,128,16,2,128]{4,3,2,1,0:T(2,128)(2,1)S(1)}, bf16[2,128,16,2,128]{4,3,2,1,0:T(2,128)(2,1)}, u32[]{:S(2)}) copy-start(bf16[2,128,16,2,128]{4,3,2,1,0:T(2,128)(2,1)} %param.16) | copy-start | bytes 6291460
  4.3 1.6 %collective-permute-start = (f32[512,128]{1,0:T(8,128)S(1)}, f32[512,128]{1,0:T(8,128)S(1)}, u32[]{:S(2)}, u32[]{:S(2)}) collective-permute-start(f32[512,128]{1,0:T(8,128)S(1)} %get-tuple-element.11), channel_id=1, source_target_pairs={{0,1},{1,0},{2,3},{3,2},{4,5},{5,4},{6,7},{7,6},{8,9},{9,8},{10,11... | collective-permute-start | bytes 786440 | tf_op jit(solution)/shard_map/ppermute | solution.py:393
  35.6 1.0 copy-start.4
  39.7 27.4 %copy-start.6 = (bf16[128,512]{1,0:T(8,128)(2,1)S(1)}, bf16[128,512]{1,0:T(8,128)(2,1)}, u32[]{:S(2)}) copy-start(bf16[128,512]{1,0:T(8,128)(2,1)} %w1_.1) | copy-start | bytes 393220
  39.7 27.4 %copy-start.10 = (bf16[2,128,96]{2,1,0:T(8,128)(2,1)S(1)}, bf16[2,128,96]{2,1,0:T(8,128)(2,1)}, u32[]{:S(2)}) copy-start(bf16[2,128,96]{2,1,0:T(8,128)(2,1)} %constant.24.clone.zi_) | copy-start | bytes 147460
  65.1 2.0 %collective-permute-start.1 = (f32[1024,128]{1,0:T(8,128)S(1)}, f32[1024,128]{1,0:T(8,128)S(1)}, u32[]{:S(2)}, u32[]{:S(2)}) collective-permute-start(f32[1024,128]{1,0:T(8,128)S(1)} %bitcast.27), channel_id=1, source_target_pairs={{0,1},{1,0},{2,3},{3,2},{4,5},{5,4},{6,7},{7,6},{8,9},{9,8},{10,11... | collective-permute-start | bytes 1572872 | tf_op jit(solution)/shard_map/ppermute | solution.py:408
  67.1 0.9 copy-start.7
  68.0 0.9 copy-start.8
  85.5 28.5 %copy-start.3 = (bf16[256,1024]{1,0:T(8,128)(2,1)S(1)}, bf16[256,1024]{1,0:T(8,128)(2,1)}, u32[]{:S(2)}) copy-start(bf16[256,1024]{1,0:T(8,128)(2,1)} %constant.28.clone.xf) | copy-start | bytes 1572868
  85.6 2.1 %collective-permute-start.2 = (f32[1024,128]{1,0:T(8,128)S(1)}, f32[1024,128]{1,0:T(8,128)S(1)}, u32[]{:S(2)}, u32[]{:S(2)}) collective-permute-start(f32[1024,128]{1,0:T(8,128)S(1)} %get-tuple-element.14), channel_id=1, source_target_pairs={{0,1},{1,0},{2,3},{3,2},{4,5},{5,4},{6,7},{7,6},{8,9},{9,8},{10,11... | collective-permute-start | bytes 1572872 | tf_op jit(solution)/shard_map/ppermute | solution.py:393

commit v2 on v1

--- a/solution.py
+++ b/solution.py
@@ -36,8 +36,8 @@
 BF16 = jnp.bfloat16
 
 
-def params():
-    return pltpu.CompilerParams(dimension_semantics=("arbitrary",), vmem_limit_bytes=44 * 1024 * 1024)
+def params(mebibytes=44):
+    return pltpu.CompilerParams(dimension_semantics=("arbitrary",), vmem_limit_bytes=mebibytes * 1024 * 1024)
 
 
 def signed(number):
@@ -71,23 +71,32 @@
     return np.stack([np.stack([c, -s]), np.stack([s, c])])
 
 
-def z_order(core):
+def back_order(column):
     order = []
-    for which in range(2):
-        co = core if which == 0 else 1 - core
+    for part in range(4):
+        xh, co = column // 2 ^ part % 2, column % 2 ^ part // 2
+        order += [8 * zh + 4 * xh + 2 * co + m for zh in range(2) for m in range(2)]
+    return np.array(order)
+
+
+def out_order(core):
+    order = []
+    for part in range(2):
         for zh in range(2):
             for xh in range(2):
-                for m in range(2):
-                    order.append(8 * zh + 4 * xh + 2 * co + m)
+                order += [8 * zh + 4 * xh + 2 * (core ^ part) + m for m in range(2)]
     return np.array(order)
 
 
 def z_tables():
     inverse, forward = [], []
+    for column in range(COLUMNS):
+        a = angles(np.arange(NZ), back_order(column), NZ)
+        inverse.append(wide(np.stack([np.cos(a), -np.sin(a)], -1).reshape(NZ, 2 * MZ)))
     for core in range(2):
-        a = angles(np.arange(NZ), z_order(core), NZ)
-        inverse.append(wide(np.stack([np.cos(a), -np.sin(a)], -1).reshape(NZ, 2 * MZ)))
-        forward.append(tall(np.stack([np.cos(a), -np.sin(a)], -1).reshape(NZ, 2 * MZ).T))
+        a = angles(np.arange(NZ), out_order(core), NZ)
+        high, low = halves(np.stack([np.cos(a), -np.sin(a)], -1).reshape(NZ, 2 * MZ).T)
+        forward.append(np.block([[high, high], [low, np.zeros_like(low)]]))
     return np.stack(inverse), np.stack(forward)
 
 
@@ -151,13 +160,19 @@
     return [pl.ds(zh * 32 + xl * 16 + xh * 8 + m * 4 + extra, 16, stride=64) for xl in range(2)]
 
 
+def back_rows(k, extra):
+    zh, m = k % 4 // 2, k % 2
+    return [pl.ds(zh * 16 + xl * 8 + m * 4 + extra, 16, stride=32) for xl in range(2)]
+
+
 def state_rows_of(k, extra):
     zh, xh, m = k % 8 // 4, k % 4 // 2, k % 2
     return [pl.ds(zh * 16 + xl * 8 + xh * 4 + m * 2 + extra, 16, stride=32) for xl in range(2)]
 
 
 def rows_forward(values, fields, table, after, y):
-    rows = tall_dot(table, values)
+    rows = dot(table, jnp.concatenate(two(values), axis=0))
+    rows = rows[: 2 * MZ] + rows[2 * MZ :]
     start = pl.multiple_of(y * 2 * MZ, 2 * MZ)
     for s in range(fields):
         after[s, pl.ds(start, 2 * MZ), :] = rows[:, s * C : (s + 1) * C]
@@ -183,40 +198,40 @@
 def state_kernel(place, state, zf, yf, keep, give, after):
     for y in range(0, ROWS, 2):
         pair = jnp.concatenate([state[(y + i) * NZ : (y + i + 1) * NZ] for i in range(2)], axis=1)
-        rows = dot(zf[0], pair)
+        rows = dot(zf[0, :, :NZ], pair)
         rows = rows[: 2 * MZ] + rows[2 * MZ :]
         for i in range(2):
             after[0, pl.ds((y + i) * 2 * MZ, 2 * MZ), :] = rows[:, i * C : (i + 1) * C]
     columns_forward(1, yf[0], after, keep, give)
 
 
+def ready_kernel(place, w1_, w2_, yi_, zi_, zf_, yf_, w1, w2, w1t, w2t, yi, zi, zf, yf):
+    w1[...] = w1_[...]
+    w2[...] = w2_[...]
+    w1t[...] = w1_[...].T
+    w2t[...] = w2_[...].T
+    yi[...] = yi_[0]
+    zi[...] = zi_[0]
+    zf[...] = zf_[0]
+    yf[...] = yf_[0]
+
+
 def field_kernel(
-    place, mine, other, state, target, w1_, w2_, yi_, zi_, zf_, yf_, keep, give,
-    half, after, w1, w2, w1t, w2t, yi, zi, zf, yf, arrivals
+    q00, q10, q01, q11, state, target, w1, w2, w1t, w2t, yi, zi, zf, yf, keep, give, half, after
 ):
     step = pl.program_id(0)
 
     @pl.when(step == 0)
     def _():
-        column, core = place[0], place[1]
-        pairs = [(yi_.at[column], yi), (zi_.at[core], zi), (w1_, w1), (w2_, w2), (zf_.at[core], zf), (yf_.at[column], yf)]
-        copies = [pltpu.make_async_copy(a, b, arrivals.at[i]) for i, (a, b) in enumerate(pairs)]
-        for copy in copies:
-            copy.start()
-        copies[0].wait()
         for k in range(MZ):
-            source = mine if k < 8 else other
+            source = (q00, q10, q01, q11)[k // 4]
             parts = []
             for s in range(2):
-                p = [source[place, :] for i in range(2) for place in mode_rows(k, 2 * s + i)]
+                p = [source[place, :] for i in range(2) for place in back_rows(k, 2 * s + i)]
                 parts.append(jnp.concatenate(p, axis=0))
             rows = dot(yi[...], three(jnp.concatenate(parts, axis=1)))
             for s in range(2):
                 half[s, pl.ds(k * 64, 64), :] = rows[:, s * C : (s + 1) * C]
-        for copy in copies[1:]:
-            copy.wait()
-        w1t[...] = w1[...].T
-        w2t[...] = w2[...].T
 
     first = step * ROWS_A_STEP
     fields = []
@@ -262,51 +277,58 @@
     return pl.BlockSpec((1,) + table.shape[1:], lambda i, place: (place[index], 0, 0))
 
 
-def call_rows(kernel, place, operands, specs, out_rows, scratch, steps):
-    shape = jax.ShapeDtypeStruct((out_rows, C), F32)
+def state_stage(place, state, zf, yf):
+    shape = jax.ShapeDtypeStruct((512, C), F32)
     return pl.pallas_call(
-        kernel,
+        state_kernel,
         grid_spec=pltpu.PrefetchScalarGridSpec(
             num_scalar_prefetch=1,
-            grid=(steps,),
-            in_specs=specs,
-            out_specs=(still((out_rows, C)), still((out_rows, C))),
-            scratch_shapes=scratch,
+            grid=(1,),
+            in_specs=[still(state.shape), picked(zf, 1), picked(yf, 0)],
+            out_specs=(still((512, C)), still((512, C))),
+            scratch_shapes=[pltpu.VMEM((1, 1024, C), F32)],
         ),
         out_shape=(shape, shape),
         compiler_params=params(),
-    )(place, *operands)
-
-
-MOVING = pl.BlockSpec((CHUNK, C), lambda i, place: (i, 0))
-
-
-def state_stage(place, state, zf, yf):
-    specs = [still(state.shape), picked(zf, 1), picked(yf, 0)]
-    return call_rows(state_kernel, place, (state, zf, yf), specs, 512, [pltpu.VMEM((1, 1024, C), F32)], 1)
-
-
-def field_stage(place, mine, other, state, target, weights, tables):
-    operands = (mine, other, state, target, *weights, *tables)
-    specs = [still(mine.shape), still(other.shape), MOVING, MOVING]
-    specs += [pl.BlockSpec(memory_space=pltpu.HBM)] * 6
-    scratch = [pltpu.VMEM((2, 1024, C), F32), pltpu.VMEM((2, 1024, C), F32)]
-    scratch += [pltpu.VMEM((C, FF), BF16), pltpu.VMEM((FF, C), BF16), pltpu.VMEM((FF, C), BF16), pltpu.VMEM((C, FF), BF16)]
-    scratch += [pltpu.VMEM(t.shape[1:], BF16) for t in tables]
-    scratch += [pltpu.SemaphoreType.DMA((6,))]
-    return call_rows(field_kernel, place, operands, specs, 1024, scratch, ROWS // ROWS_A_STEP)
-
-
-def mix_kernel(received, weight, direction, xf_, xi_, spectra, planes, total, xf, xi, arrivals):
+    )(place, state, zf, yf)
+
+
+def ready_stage(place, w1, w2, tables):
+    shapes = [(C, FF), (FF, C), (FF, C), (C, FF)] + [t.shape[1:] for t in tables]
+    return pl.pallas_call(
+        ready_kernel,
+        grid_spec=pltpu.PrefetchScalarGridSpec(
+            num_scalar_prefetch=1,
+            grid=(1,),
+            in_specs=[still(w1.shape), still(w2.shape)] + [picked(t, i) for t, i in zip(tables, (0, 0, 1, 0))],
+            out_specs=tuple(still(shape) for shape in shapes),
+        ),
+        out_shape=tuple(jax.ShapeDtypeStruct(shape, BF16) for shape in shapes),
+        compiler_params=params(16),
+    )(place, w1, w2, *tables)
+
+
+def field_stage(quarters, state, target, ready):
+    moving = pl.BlockSpec((CHUNK, C), lambda i: (i, 0))
+    shape = jax.ShapeDtypeStruct((1024, C), F32)
+    return pl.pallas_call(
+        field_kernel,
+        grid=(ROWS // ROWS_A_STEP,),
+        in_specs=[whole((512, C))] * 4 + [moving] * 2 + [whole(r.shape) for r in ready],
+        out_specs=(whole((1024, C)), whole((1024, C))),
+        out_shape=(shape, shape),
+        scratch_shapes=[pltpu.VMEM((2, 1024, C), F32), pltpu.VMEM((2, 1024, C), F32)],
+        compiler_params=params(),
+    )(*quarters, state, target, *ready)
+
+
+def mix_kernel(received, weight, direction, xf, xi_, spectra, planes, total, xi, arrival):
     step = pl.program_id(0)
-    first = pltpu.make_async_copy(xf_, xf, arrivals.at[0])
-    second = pltpu.make_async_copy(xi_, xi, arrivals.at[1])
+    second = pltpu.make_async_copy(xi_, xi, arrival)
 
     @pl.when(step == 0)
     def _():
-        first.start()
         second.start()
-        first.wait()
         spectra[...] = tall_dot(xf[...], received[...])
         total[...] = jnp.zeros_like(total)
 
@@ -325,9 +347,8 @@
     @pl.when(step == C // CB - 1)
     def _():
         second.wait()
-        out = dot(xi[...], three(jnp.concatenate(sums, axis=0))).reshape(NX, 8, C)
-        planes[:, 0] = out
-        planes[:, 1] = out
+        out = dot(xi[...], three(jnp.concatenate(sums, axis=0)))
+        planes[...] = out
 
 
 def mix_stage(received, weight, direction):
@@ -339,17 +360,16 @@
     return pl.pallas_call(
         mix_kernel,
         grid=(C // CB,),
-        in_specs=[whole(received.shape), moving, moving] + [pl.BlockSpec(memory_space=pltpu.HBM)] * 2,
-        out_specs=(whole((64, C)), whole((NX, 2, 8, C))),
-        out_shape=(jax.ShapeDtypeStruct((64, C), F32), jax.ShapeDtypeStruct((NX, 2, 8, C), F32)),
+        in_specs=[whole(received.shape), moving, moving, whole(xf.shape), pl.BlockSpec(memory_space=pltpu.HBM)],
+        out_specs=(whole((64, C)), whole((NX * 8, C))),
+        out_shape=(jax.ShapeDtypeStruct((64, C), F32), jax.ShapeDtypeStruct((NX * 8, C), F32)),
         scratch_shapes=[
             pltpu.VMEM((4, 32, C), F32),
-            pltpu.VMEM(xf.shape, BF16),
             pltpu.VMEM(xi.shape, BF16),
-            pltpu.SemaphoreType.DMA((2,)),
+            pltpu.SemaphoreType.DMA,
         ],
         compiler_params=params(),
-    )(received, weight, direction, jnp.asarray(xf), jnp.asarray(xi))
+    )(received, weight, direction, jnp.asarray(xf), pltpu.with_memory_space_constraint(jnp.asarray(xi), pltpu.HBM))
 
 
 def outer_kernel(received, spectra, xf, gradient, curvature, adjoint):
@@ -385,12 +405,13 @@
     )(received, spectra, jnp.asarray(xf))
 
 
-def exchange(rows):
-    return lax.all_to_all(rows.reshape(2 * NX, -1, C), WIDE, 0, 0, tiled=True).reshape(rows.shape)
-
-
-def summed(keep, give):
-    return keep + lax.ppermute(give, "co", [(0, 1), (1, 0)])
+def exchange(rows, group):
+    size = lax.axis_size(group)
+    return lax.all_to_all(rows.reshape(size, -1, C), group, 0, 0, tiled=True).reshape(rows.shape)
+
+
+def swap(rows, axis):
+    return lax.ppermute(rows, axis, [(0, 1), (1, 0)])
 
 
 def local(state, target, spectral_weight, direction_weight, inner_weight, outer_weight):
@@ -402,13 +423,19 @@
         return cells[:, 0].transpose(1, 2, 0).reshape(ROWS * NZ, C)
 
     state_rows = rows_of(state)
-    received = exchange(summed(*state_stage(place, state_rows, zf, yf)))
+    keep, give = state_stage(place, state_rows, zf, yf)
+    received = exchange(keep + swap(give, "co"), WIDE)
     spectra, planes = mix_stage(received, spectral_weight, direction_weight)
-    arrived = exchange(planes.reshape(1024, C))
-    other = lax.ppermute(arrived, "co", [(0, 1), (1, 0)])
-    weights = (inner_weight, outer_weight)
-    keep, give = field_stage(place, arrived, other, state_rows, rows_of(target), weights, (yi, zi, zf, yf))
-    adjoint = exchange(summed(keep, give))
+    q00 = exchange(planes, WIDE[:3])
+    q10 = swap(q00, "xh")
+    q01 = swap(q00, "co")
+    q00, target, w1, w2 = lax.optimization_barrier((q00, target, inner_weight, outer_weight))
+    ready = ready_stage(place, w1, w2, (yi, zi, zf, yf))
+    target_rows = rows_of(target)
+    q10, ready, target_rows = lax.optimization_barrier((q10, ready, target_rows))
+    q11 = swap(q10, "co")
+    keep, give = field_stage((q00, q10, q01, q11), state_rows, target_rows, ready)
+    adjoint = exchange(keep + swap(give, "co"), WIDE)
     gradient, curvature = outer_stage(adjoint, spectra)
     shape = (2, C, MX, 2, C)
     return gradient.reshape(shape), curvature.reshape(shape)

time: 118 us -> 114 us (0.966)
  blocking collectives: 81.3 us -> 74.4 us
  waiting for transfers between devices: 3.06 us -> 7.55 us
  local copies, waits for them, and re-layouts: 6.89 us -> 5.01 us
  starting transfers between devices: 0.69 us -> 1.91 us
    all_to_all x3, blocking collectives: 81.3 us -> 74.4 us  [exchange(): lax.all_to_all(rows.reshape(size, -1, C), group, 0, 0, tiled=True)]
    ppermute x3 -> x5, waiting for transfers between devices: 3.06 us -> 7.55 us  [swap(): return lax.ppermute(rows, axis, [(0, 1), (1, 0)])]
    unnamed x22 -> x20, local copies, waits for them, and re-layouts: 2.85 us -> 0.96 us
    ppermute x3 -> x5, starting transfers between devices: 0.69 us -> 1.91 us  [swap(): return lax.ppermute(rows, axis, [(0, 1), (1, 0)])]
    pallas_call x2 -> x3, Pallas kernels: 18.1 us -> 17.5 us  [the longest x1 15.4 us: field_stage(): pl.pallas_call(field_kernel, grid=(ROWS // ROWS_A_STEP,), in_specs=[whole...]
  transfers between devices with their start and end apart: 3 -> 5, of which waited for: 2 -> 4; matrix products, arithmetic and copies ran while one was open for 2% -> 2% of each run, Pallas kernels for 0% -> 1%
where the time goes in v2:
time: 114 us; the launch traced here: 113 us
  blocking collectives  74.4 us (65%)
  Pallas kernels  23.5 us (21%)
  waiting for transfers between devices  7.55 us (7%)
  local copies, waits for them, and re-layouts  5.01 us (4%)
  starting transfers between devices  1.91 us (2%)
    all_to_all x3, blocking collectives, exchange(): lax.all_to_all(rows.reshape(size, -1, C), group, 0, 0, tiled=True)  74.4 us
    pallas_call x1, Pallas kernels, field_stage(): pl.pallas_call(field_kernel, grid=(ROWS // ROWS_A_STEP,), in_specs=[whole...  15.4 us
    ppermute x5, waiting for transfers between devices, swap(): return lax.ppermute(rows, axis, [(0, 1), (1, 0)])  7.55 us
    transpose x2, local copies, waits for them, and re-layouts, rows_of(): return cells[:, 0].transpose(1, 2, 0).reshape(ROWS * NZ, C)  4.05 us
    pallas_call x1, Pallas kernels, outer_stage(): pl.pallas_call(outer_kernel, grid=(C // CB,), in_specs=[whole(received.sh...  3.27 us
    pallas_call x1, Pallas kernels, mix_stage(): pl.pallas_call(mix_kernel, grid=(C // CB,), in_specs=[whole(received.shap...  2.76 us
  transfers between devices with their start and end apart: 5, of which 4 were waited for; matrix products, arithmetic and copies ran while one was open for 2% of the time, Pallas kernels for 1%

profile of v2, /device:TPU:2, one launch (start us, length us, event | category | flops | bytes accessed | tf_op | source)
XLA Modules:
  0.0 113.4 jit_solution(16919519016699776189)
XLA Ops:
  0.6 0.0 copy-start.4
  0.6 0.0 copy-start.2
  0.7 0.0 copy-start.9
  0.7 2.1 %copy.15 = bf16[32,128,128]{2,1,0:T(8,128)(2,1)S(1)} copy(bf16[32,128,128]{1,0,2:T(8,128)(2,1)} %bitcast.33) | data formatting | bytes 2097152 | tf_op jit(solution)/shard_map/transpose | solution.py:423
  2.8 0.1 pad_add_fusion.place
  2.9 1.4 %shard_map.140 = (f32[512,128]{1,0:T(8,128)S(1)}, f32[512,128]{1,0:T(8,128)S(1)}) custom-call(s32[2]{0:T(128)S(1)} %pad_add_fusion.place, bf16[4096,128]{1,0:T(8,128)(2,1)S(1)} %bitcast.21, bf16[2,64,256]{2,1,0:T(8,128)(2,1)S(1)} %copy-done.4, bf16[4,64,192]{2,1,0:T(8,128)(2,1)S(1)} %copy-done.2), custom_call_target="tpu_custom_call" | custom-call | tf_op jit(solution)/shard_map/pallas_call | solution.py:282
  4.3 0.1 collective-permute-start
  4.4 1.5 %collective-permute-done = f32[512,128]{1,0:T(8,128)S(1)} collective-permute-done((f32[512,128]{1,0:T(8,128)S(1)}, f32[512,128]{1,0:T(8,128)S(1)}, u32[]{:S(2)}, u32[]{:S(2)}) %collective-permute-start) | collective-permute-done | bytes 262176 | tf_op jit(solution)/shard_map/ppermute | solution.py:414
  6.0 29.6 %all_to_all.15 = f32[128,4,128]{2,1,0:T(4,128)S(1)} all-to-all(f32[128,4,128]{2,1,0:T(4,128)S(1)} %bitcast.32), channel_id=1, replica_groups=mesh['xl'=2,'y'=4,'z'=8,'xh'=2,'co'=2] {'y','z','xl','xh'}, dimensions={0} | all-to-all | bytes 524288 | tf_op jit(solution)/shard_map/all_to_all | solution.py:410
  35.6 2.8 %shard_map.141 = (f32[64,128]{1,0:T(8,128)S(1)}, f32[512,128]{1,0:T(8,128)S(1)}) custom-call(f32[512,128]{1,0:T(8,128)S(1)} %bitcast.27, bf16[2,128,32,128]{3,2,1,0:T(8,128)(2,1)S(1)} %bitcast.24, bf16[2,128,32,128]{3,2,1,0:T(8,128)(2,1)S(1)} %bitcast.25, bf16[128,512]{1,0:T(8,128)(2,1)S(1)} %copy-done.9, bf16[512,384]{1,0:T(8,128)(2,1)} %constant.27.clone.xi_), custom_call_target="tpu_custom_call" | custom-call | tf_op jit(solution)/shard_map/pallas_call | solution.py:360
  38.3 0.0 copy-start.7
  38.4 16.3 %all_to_all.16 = f32[64,8,128]{2,1,0:T(8,128)S(1)} all-to-all(f32[64,8,128]{2,1,0:T(8,128)S(1)} %bitcast.31), channel_id=1, replica_groups=mesh['xl'=2,'y'=4,'z'=8,'xh'=2,'co'=2] {'y','z','xl'}, dimensions={0} | all-to-all | bytes 524288 | tf_op jit(solution)/shard_map/all_to_all | solution.py:410
  54.6 1.6 %collective-permute-start.1 = (f32[512,128]{1,0:T(8,128)S(1)}, f32[512,128]{1,0:T(8,128)S(1)}, u32[]{:S(2)}, u32[]{:S(2)}) collective-permute-start(f32[512,128]{1,0:T(8,128)S(1)} %bitcast.28), channel_id=1, source_target_pairs={{0,2},{2,0},{1,3},{3,1},{4,6},{6,4},{5,7},{7,5},{8,10},{10,8},{9,1... | collective-permute-start | bytes 786440 | tf_op jit(solution)/shard_map/ppermute | solution.py:414
  56.2 1.9 %copy.16 = bf16[32,128,128]{2,1,0:T(8,128)(2,1)S(1)} copy(bf16[32,128,128]{1,0,2:T(8,128)(2,1)} %bitcast.34) | data formatting | bytes 2097152 | tf_op jit(solution)/shard_map/transpose | solution.py:423
  58.2 0.9 copy-done.8
  59.1 0.7 shard_map.142
  59.8 2.7 %collective-permute-done.1.q10 = f32[512,128]{1,0:T(8,128)S(1)} collective-permute-done((f32[512,128]{1,0:T(8,128)S(1)}, f32[512,128]{1,0:T(8,128)S(1)}, u32[]{:S(2)}, u32[]{:S(2)}) %collective-permute-start.1) | collective-permute-done | bytes 262176 | tf_op jit(solution)/shard_map/ppermute | solution.py:414
  62.5 1.5 %collective-permute-done.3.q11 = f32[512,128]{1,0:T(8,128)S(1)} collective-permute-done((f32[512,128]{1,0:T(8,128)S(1)}, f32[512,128]{1,0:T(8,128)S(1)}, u32[]{:S(2)}, u32[]{:S(2)}) %collective-permute-start.3) | collective-permute-done | bytes 262176 | tf_op jit(solution)/shard_map/ppermute | solution.py:414
  64.1 15.4 %shard_map.143 = (f32[1024,128]{1,0:T(8,128)S(1)}, f32[1024,128]{1,0:T(8,128)S(1)}) custom-call(f32[512,128]{1,0:T(8,128)S(1)} %bitcast.30, f32[512,128]{1,0:T(8,128)S(1)} %collective-permute-done.1.q10, f32[512,128]{1,0:T(8,128)S(1)} %collective-permute-done.2.q01, f32[512,128]{1,0:T(8,128)S(1)} %collective-permute-done.3.q11, ...), custom_call_target="tpu_custom_call" | custom-call | tf_op jit(solution)/shard_map/pallas_call | solution.py:314
  79.5 0.2 collective-permute-start.4
  79.7 1.8 %collective-permute-done.4 = f32[1024,128]{1,0:T(8,128)S(1)} collective-permute-done((f32[1024,128]{1,0:T(8,128)S(1)}, f32[1024,128]{1,0:T(8,128)S(1)}, u32[]{:S(2)}, u32[]{:S(2)}) %collective-permute-start.4) | collective-permute-done | bytes 524320 | tf_op jit(solution)/shard_map/ppermute | solution.py:414
  81.5 0.1 add_bitcast_fusion
  81.6 28.5 %all_to_all.17 = f32[128,8,128]{2,1,0:T(8,128)S(1)} all-to-all(f32[128,8,128]{2,1,0:T(8,128)S(1)} %add_bitcast_fusion), channel_id=1, replica_groups=mesh['xl'=2,'y'=4,'z'=8,'xh'=2,'co'=2] {'y','z','xl','xh'}, dimensions={0} | all-to-all | bytes 1048576 | tf_op jit(solution)/shard_map/all_to_all | solution.py:410
  110.1 3.3 %shard_map.144 = (bf16[2,128,32,128]{3,2,1,0:T(8,128)(2,1)}, bf16[2,128,32,128]{3,2,1,0:T(8,128)(2,1)}) custom-call(f32[1024,128]{1,0:T(8,128)S(1)} %bitcast.26, f32[64,128]{1,0:T(8,128)S(1)} %get-tuple-element.59.spectra, bf16[256,1024]{1,0:T(8,128)(2,1)S(1)} %copy-done.3), custom_call_target="tpu_custom_call" | custom-call | tf_op jit(solution)/shard_map/pallas_call | solution.py:397
  (19 shorter events, 0.1 us)
Async XLA Ops:
  0.6 2.3 %copy-start.4 = (bf16[2,64,256]{2,1,0:T(8,128)(2,1)S(1)}, bf16[2,64,256]{2,1,0:T(8,128)(2,1)}, u32[]{:S(2)}) copy-start(bf16[2,64,256]{2,1,0:T(8,128)(2,1)} %constant.25.clone.zf.zf_) | copy-start | bytes 196612
  0.6 2.2 %copy-start.2 = (bf16[4,64,192]{2,1,0:T(8,128)(2,1)S(1)}, bf16[4,64,192]{2,1,0:T(8,128)(2,1)}, u32[]{:S(2)}) copy-start(bf16[4,64,192]{2,1,0:T(8,128)(2,1)} %constant.23.clone.yf.yf_) | copy-start | bytes 294916
  0.7 34.9 %copy-start = (bf16[2,128,16,2,128]{4,3,2,1,0:T(2,128)(2,1)S(1)}, bf16[2,128,16,2,128]{4,3,2,1,0:T(2,128)(2,1)}, u32[]{:S(2)}) copy-start(bf16[2,128,16,2,128]{4,3,2,1,0:T(2,128)(2,1)} %param.15) | copy-start | bytes 6291460
  0.7 34.9 %copy-start.9 = (bf16[128,512]{1,0:T(8,128)(2,1)S(1)}, bf16[128,512]{1,0:T(8,128)(2,1)}, u32[]{:S(2)}) copy-start(bf16[128,512]{1,0:T(8,128)(2,1)} %constant.26.clone.xf) | copy-start | bytes 393220
  2.8 32.8 %copy-start.1 = (bf16[2,128,16,2,128]{4,3,2,1,0:T(2,128)(2,1)S(1)}, bf16[2,128,16,2,128]{4,3,2,1,0:T(2,128)(2,1)}, u32[]{:S(2)}) copy-start(bf16[2,128,16,2,128]{4,3,2,1,0:T(2,128)(2,1)} %param.16) | copy-start | bytes 6291460
  4.3 1.6 %collective-permute-start = (f32[512,128]{1,0:T(8,128)S(1)}, f32[512,128]{1,0:T(8,128)S(1)}, u32[]{:S(2)}, u32[]{:S(2)}) collective-permute-start(f32[512,128]{1,0:T(8,128)S(1)} %get-tuple-element.33), channel_id=1, source_target_pairs={{0,1},{1,0},{2,3},{3,2},{4,5},{5,4},{6,7},{7,6},{8,9},{9,8},{10,11... | collective-permute-start | bytes 786440 | tf_op jit(solution)/shard_map/ppermute | solution.py:414
  38.3 19.9 %copy-start.5 = (bf16[128,512]{1,0:T(8,128)(2,1)S(1)}, bf16[128,512]{1,0:T(8,128)(2,1)}, u32[]{:S(2)}) copy-start(bf16[128,512]{1,0:T(8,128)(2,1)} %w1_) | copy-start | bytes 393220
  38.3 19.9 %copy-start.6 = (bf16[512,128]{1,0:T(8,128)(2,1)S(1)}, bf16[512,128]{1,0:T(8,128)(2,1)}, u32[]{:S(2)}) copy-start(bf16[512,128]{1,0:T(8,128)(2,1)} %w2_) | copy-start | bytes 393220
  38.3 19.9 %copy-start.7 = (bf16[4,128,96]{2,1,0:T(8,128)(2,1)S(1)}, bf16[4,128,96]{2,1,0:T(8,128)(2,1)}, u32[]{:S(2)}) copy-start(bf16[4,128,96]{2,1,0:T(8,128)(2,1)} %constant.24.clone.zi_) | copy-start | bytes 294916
  54.6 7.9 %collective-permute-start.1 = (f32[512,128]{1,0:T(8,128)S(1)}, f32[512,128]{1,0:T(8,128)S(1)}, u32[]{:S(2)}, u32[]{:S(2)}) collective-permute-start(f32[512,128]{1,0:T(8,128)S(1)} %bitcast.28), channel_id=1, source_target_pairs={{0,2},{2,0},{1,3},{3,1},{4,6},{6,4},{5,7},{7,5},{8,10},{10,8},{9,1... | collective-permute-start | bytes 786440 | tf_op jit(solution)/shard_map/ppermute | solution.py:414
  56.2 6.3 %collective-permute-start.2 = (f32[512,128]{1,0:T(8,128)S(1)}, f32[512,128]{1,0:T(8,128)S(1)}, u32[]{:S(2)}, u32[]{:S(2)}) collective-permute-start(f32[512,128]{1,0:T(8,128)S(1)} %bitcast.29), channel_id=1, source_target_pairs={{0,1},{1,0},{2,3},{3,2},{4,5},{5,4},{6,7},{7,6},{8,9},{9,8},{10,11... | collective-permute-start | bytes 786440 | tf_op jit(solution)/shard_map/ppermute | solution.py:414
  58.2 0.9 copy-start.8
  62.5 1.5 %collective-permute-start.3 = (f32[512,128]{1,0:T(8,128)S(1)}, f32[512,128]{1,0:T(8,128)S(1)}, u32[]{:S(2)}, u32[]{:S(2)}) collective-permute-start(f32[512,128]{1,0:T(8,128)S(1)} %collective-permute-done.1.q10), channel_id=1, source_target_pairs={{0,1},{1,0},{2,3},{3,2},{4,5},{5,4},{6,7},{7,6},{8,9},{9,8},{10,11... | collective-permute-start | bytes 786440 | tf_op jit(solution)/shard_map/ppermute | solution.py:414
  79.5 30.6 %copy-start.3 = (bf16[256,1024]{1,0:T(8,128)(2,1)S(1)}, bf16[256,1024]{1,0:T(8,128)(2,1)}, u32[]{:S(2)}) copy-start(bf16[256,1024]{1,0:T(8,128)(2,1)} %constant.28.clone.xf) | copy-start | bytes 1572868
  79.5 2.0 %collective-permute-start.4 = (f32[1024,128]{1,0:T(8,128)S(1)}, f32[1024,128]{1,0:T(8,128)S(1)}, u32[]{:S(2)}, u32[]{:S(2)}) collective-permute-start(f32[1024,128]{1,0:T(8,128)S(1)} %get-tuple-element.58), channel_id=1, source_target_pairs={{0,1},{1,0},{2,3},{3,2},{4,5},{5,4},{6,7},{7,6},{8,9},{9,8},{10,11... | collective-permute-start | bytes 1572872 | tf_op jit(solution)/shard_map/ppermute | solution.py:414

commit v3 on v2

--- a/solution.py
+++ b/solution.py
@@ -28,6 +28,7 @@
 ROWS_A_STEP = 16
 CHUNK = ROWS_A_STEP * NZ
 CB = 64
+MB = 32
 
 GX = ("xl", "y", "z")
 COL = ("xh", "co")
@@ -196,9 +197,10 @@
 
 
 def state_kernel(place, state, zf, yf, keep, give, after):
+    planes = jnp.transpose(state[...], (1, 0, 2))
     for y in range(0, ROWS, 2):
-        pair = jnp.concatenate([state[(y + i) * NZ : (y + i + 1) * NZ] for i in range(2)], axis=1)
-        rows = dot(zf[0, :, :NZ], pair)
+        pair = planes[y : y + 2].reshape(2 * C, NZ)
+        rows = lax.dot_general(zf[0, :, :NZ], pair, (((1,), (1,)), ((), ())), preferred_element_type=F32)
         rows = rows[: 2 * MZ] + rows[2 * MZ :]
         for i in range(2):
             after[0, pl.ds((y + i) * 2 * MZ, 2 * MZ), :] = rows[:, i * C : (i + 1) * C]
@@ -289,7 +291,7 @@
             scratch_shapes=[pltpu.VMEM((1, 1024, C), F32)],
         ),
         out_shape=(shape, shape),
-        compiler_params=params(),
+        compiler_params=params(16),
     )(place, state, zf, yf)
 
 
@@ -322,54 +324,61 @@
     )(*quarters, state, target, *ready)
 
 
-def mix_kernel(received, weight, direction, xf, xi_, spectra, planes, total, xi, arrival):
-    step = pl.program_id(0)
-    second = pltpu.make_async_copy(xi_, xi, arrival)
-
-    @pl.when(step == 0)
-    def _():
-        second.start()
-        spectra[...] = tall_dot(xf[...], received[...])
-        total[...] = jnp.zeros_like(total)
-
-    turned = pltpu.roll(spectra[...], C - step * CB, 1)
-    sums = [total[i] for i in range(4)]
-    for j in range(CB):
-        column = jnp.broadcast_to(turned[:, j : j + 1], (64, C))
+def mix_kernel(received, weight, direction, xf, xi_, spectra, planes, held, xi, arrivals, arrival):
+    last = pltpu.make_async_copy(xi_, xi, arrival)
+    copies = []
+    for i in range(C // MB):
+        at = pl.ds(i * MB, MB)
+        for s, source in ((0, weight), (1, direction)):
+            copies.append(pltpu.make_async_copy(source.at[:, at], held.at[s, :, at], arrivals.at[2 * i + s]))
+    for copy in copies:
+        copy.start()
+    last.start()
+    modes = tall_dot(xf[...], received[...])
+    spectra[...] = modes
+    sums = [jnp.zeros((32, C), F32) for i in range(4)]
+    for j in range(C):
+        if j % MB == 0:
+            copies[2 * (j // MB)].wait()
+            copies[2 * (j // MB) + 1].wait()
+        column = jnp.broadcast_to(modes[:, j : j + 1], (64, C))
         real, imag = column[:32], column[32:]
-        for s, w in ((0, weight), (1, direction)):
-            wr, wi = w[0, j].astype(F32), w[1, j].astype(F32)
+        for s in range(2):
+            wr, wi = held[s, 0, j].astype(F32), held[s, 1, j].astype(F32)
             sums[2 * s] = sums[2 * s] + (wr * real - wi * imag)
             sums[2 * s + 1] = sums[2 * s + 1] + (wr * imag + wi * real)
-    for i in range(4):
-        total[i] = sums[i]
-
-    @pl.when(step == C // CB - 1)
-    def _():
-        second.wait()
-        out = dot(xi[...], three(jnp.concatenate(sums, axis=0)))
-        planes[...] = out
+    last.wait()
+    planes[...] = dot(xi[...], three(jnp.concatenate(sums, axis=0)))
 
 
 def mix_stage(received, weight, direction):
     xf = x_forward_table(1, FORWARD_FACTOR)
     xi = x_inverse_table(INVERSE_FACTOR)
-    weight = weight.reshape(2, C, 32, C)
-    direction = direction.reshape(2, C, 32, C)
-    moving = pl.BlockSpec((2, CB, 32, C), lambda i: (0, i, 0, 0))
+    far = pl.BlockSpec(memory_space=pltpu.HBM)
+
+    def stay(array):
+        return pltpu.with_memory_space_constraint(array, pltpu.HBM)
+
     return pl.pallas_call(
         mix_kernel,
-        grid=(C // CB,),
-        in_specs=[whole(received.shape), moving, moving, whole(xf.shape), pl.BlockSpec(memory_space=pltpu.HBM)],
+        grid=(1,),
+        in_specs=[whole(received.shape), far, far, whole(xf.shape), far],
         out_specs=(whole((64, C)), whole((NX * 8, C))),
         out_shape=(jax.ShapeDtypeStruct((64, C), F32), jax.ShapeDtypeStruct((NX * 8, C), F32)),
         scratch_shapes=[
-            pltpu.VMEM((4, 32, C), F32),
+            pltpu.VMEM((2, 2, C, 32, C), BF16),
             pltpu.VMEM(xi.shape, BF16),
+            pltpu.SemaphoreType.DMA((2 * (C // MB),)),
             pltpu.SemaphoreType.DMA,
         ],
-        compiler_params=params(),
-    )(received, weight, direction, jnp.asarray(xf), pltpu.with_memory_space_constraint(jnp.asarray(xi), pltpu.HBM))
+        compiler_params=params(16),
+    )(
+        received,
+        stay(weight.reshape(2, C, 32, C)),
+        stay(direction.reshape(2, C, 32, C)),
+        jnp.asarray(xf),
+        stay(jnp.asarray(xi)),
+    )
 
 
 def outer_kernel(received, spectra, xf, gradient, curvature, adjoint):
@@ -401,7 +410,7 @@
         out_specs=(moving, moving),
         out_shape=(shape, shape),
         scratch_shapes=[pltpu.VMEM((128, C), F32)],
-        compiler_params=params(),
+        compiler_params=params(24),
     )(received, spectra, jnp.asarray(xf))
 
 
@@ -422,19 +431,18 @@
     def rows_of(cells):
         return cells[:, 0].transpose(1, 2, 0).reshape(ROWS * NZ, C)
 
-    state_rows = rows_of(state)
-    keep, give = state_stage(place, state_rows, zf, yf)
+    keep, give = state_stage(place, state.reshape(C, ROWS, NZ), zf, yf)
     received = exchange(keep + swap(give, "co"), WIDE)
     spectra, planes = mix_stage(received, spectral_weight, direction_weight)
     q00 = exchange(planes, WIDE[:3])
     q10 = swap(q00, "xh")
     q01 = swap(q00, "co")
-    q00, target, w1, w2 = lax.optimization_barrier((q00, target, inner_weight, outer_weight))
+    q00, state, target, w1, w2 = lax.optimization_barrier((q00, state, target, inner_weight, outer_weight))
     ready = ready_stage(place, w1, w2, (yi, zi, zf, yf))
-    target_rows = rows_of(target)
-    q10, ready, target_rows = lax.optimization_barrier((q10, ready, target_rows))
+    rows = rows_of(state), rows_of(target)
+    q10, ready, rows = lax.optimization_barrier((q10, ready, rows))
     q11 = swap(q10, "co")
-    keep, give = field_stage((q00, q10, q01, q11), state_rows, target_rows, ready)
+    keep, give = field_stage((q00, q10, q01, q11), *rows, ready)
     adjoint = exchange(keep + swap(give, "co"), WIDE)
     gradient, curvature = outer_stage(adjoint, spectra)
     shape = (2, C, MX, 2, C)

time: 114 us -> 115 us (level)
  local copies, waits for them, and re-layouts: 5.01 us -> 6.86 us
    unnamed x20 -> x24, local copies, waits for them, and re-layouts: 0.96 us -> 3.91 us
  transfers between devices with their start and end apart: 5 -> 5, of which waited for: 4 -> 4; matrix products, arithmetic and copies ran while one was open for 2% -> 3% of each run, Pallas kernels for 1% -> 1%
where the time goes in v3:
time: 115 us
  blocking collectives  74.3 us (65%)
  Pallas kernels  24.4 us (21%)
  local copies, waits for them, and re-layouts  6.86 us (6%)
  waiting for transfers between devices  6.47 us (6%)
  starting transfers between devices  1.9 us (2%)
    all_to_all x3, blocking collectives, exchange(): lax.all_to_all(rows.reshape(size, -1, C), group, 0, 0, tiled=True)  74.3 us
    pallas_call x1, Pallas kernels, field_stage(): pl.pallas_call(field_kernel, grid=(ROWS // ROWS_A_STEP,), in_specs=[whole...  15.4 us
    ppermute x5, waiting for transfers between devices, swap(): return lax.ppermute(rows, axis, [(0, 1), (1, 0)])  6.47 us
    unnamed x24, local copies, waits for them, and re-layouts  3.91 us
    pallas_call x1, Pallas kernels, mix_stage(): pl.pallas_call(mix_kernel, grid=(1,), in_specs=[whole(received.shape), fa...  3.35 us
    pallas_call x1, Pallas kernels, outer_stage(): pl.pallas_call(outer_kernel, grid=(C // CB,), in_specs=[whole(received.sh...  3.27 us
    transpose x2, local copies, waits for them, and re-layouts, rows_of(): return cells[:, 0].transpose(1, 2, 0).reshape(ROWS * NZ, C)  2.96 us
  transfers between devices with their start and end apart: 5, of which 4 were waited for; matrix products, arithmetic and copies ran while one was open for 3% of the time, Pallas kernels for 1%

profile of v3, /device:TPU:2, one launch (start us, length us, event | category | flops | bytes accessed | tf_op | source)
XLA Modules:
  0.0 114.9 jit_solution(17044285018729639280)
XLA Ops:
  0.6 0.1 pad_add_fusion.place
  0.7 1.2 %copy-done = bf16[128,1,32,128]{3,2,1,0:T(8,128)(2,1)S(1)} copy-done((bf16[128,1,32,128]{3,2,1,0:T(8,128)(2,1)S(1)}, bf16[128,1,32,128]{3,2,1,0:T(8,128)(2,1)}, u32[]{:S(2)}) %copy-start) | copy-done | bytes 1048600
  1.9 0.9 copy-done.2
  2.8 0.8 copy-done.5
  3.7 1.7 %shard_map.140 = (f32[512,128]{1,0:T(8,128)S(1)}, f32[512,128]{1,0:T(8,128)S(1)}) custom-call(s32[2]{0:T(128)S(1)} %pad_add_fusion.place, bf16[128,32,128]{2,1,0:T(8,128)(2,1)S(1)} %bitcast.22, bf16[2,64,256]{2,1,0:T(8,128)(2,1)S(1)} %copy-done.5, bf16[4,64,192]{2,1,0:T(8,128)(2,1)S(1)} %copy-done.2), custom_call_target="tpu_custom_call" | custom-call | tf_op jit(solution)/shard_map/pallas_call | solution.py:284
  5.3 0.1 collective-permute-start
  5.4 1.5 %collective-permute-done = f32[512,128]{1,0:T(8,128)S(1)} collective-permute-done((f32[512,128]{1,0:T(8,128)S(1)}, f32[512,128]{1,0:T(8,128)S(1)}, u32[]{:S(2)}, u32[]{:S(2)}) %collective-permute-start) | collective-permute-done | bytes 262176 | tf_op jit(solution)/shard_map/ppermute | solution.py:423
  7.0 29.6 %all_to_all.15 = f32[128,4,128]{2,1,0:T(4,128)S(1)} all-to-all(f32[128,4,128]{2,1,0:T(4,128)S(1)} %bitcast.34), channel_id=1, replica_groups=mesh['xl'=2,'y'=4,'z'=8,'xh'=2,'co'=2] {'y','z','xl','xh'}, dimensions={0} | all-to-all | bytes 524288 | tf_op jit(solution)/shard_map/all_to_all | solution.py:419
  36.6 3.4 %shard_map.141 = (f32[64,128]{1,0:T(8,128)S(1)}, f32[512,128]{1,0:T(8,128)S(1)}) custom-call(f32[512,128]{1,0:T(8,128)S(1)} %bitcast.27, bf16[2,128,32,128]{3,2,1,0:T(8,128)(2,1)} %bitcast.32, bf16[2,128,32,128]{3,2,1,0:T(8,128)(2,1)} %bitcast.33, bf16[128,512]{1,0:T(8,128)(2,1)S(1)} %copy-done.11, bf16[512,384]{1,0:T(8,128)(2,1)} %constant.27.clone.xi_), custom_call_target="tpu_custom_call" | custom-call | tf_op jit(solution)/shard_map/pallas_call | solution.py:362
  40.0 16.1 %all_to_all.16 = f32[64,8,128]{2,1,0:T(8,128)S(1)} all-to-all(f32[64,8,128]{2,1,0:T(8,128)S(1)} %bitcast.31), channel_id=1, replica_groups=mesh['xl'=2,'y'=4,'z'=8,'xh'=2,'co'=2] {'y','z','xl'}, dimensions={0} | all-to-all | bytes 524288 | tf_op jit(solution)/shard_map/all_to_all | solution.py:419
  56.1 1.6 %collective-permute-start.1 = (f32[512,128]{1,0:T(8,128)S(1)}, f32[512,128]{1,0:T(8,128)S(1)}, u32[]{:S(2)}, u32[]{:S(2)}) collective-permute-start(f32[512,128]{1,0:T(8,128)S(1)} %bitcast.28), channel_id=1, source_target_pairs={{0,2},{2,0},{1,3},{3,1},{4,6},{6,4},{5,7},{7,5},{8,10},{10,8},{9,1... | collective-permute-start | bytes 786440 | tf_op jit(solution)/shard_map/ppermute | solution.py:423
  57.7 0.0 copy-start.9
  57.7 1.0 copy.15
  58.7 2.0 %copy.16 = bf16[32,128,128]{2,1,0:T(8,128)(2,1)S(1)} copy(bf16[32,128,128]{1,0,2:T(8,128)(2,1)} %bitcast.35) | data formatting | bytes 2097152 | tf_op jit(solution)/shard_map/transpose | solution.py:432
  60.8 0.9 copy-done.10
  61.7 0.7 shard_map.142
  62.3 1.6 %collective-permute-done.1.q10 = f32[512,128]{1,0:T(8,128)S(1)} collective-permute-done((f32[512,128]{1,0:T(8,128)S(1)}, f32[512,128]{1,0:T(8,128)S(1)}, u32[]{:S(2)}, u32[]{:S(2)}) %collective-permute-start.1) | collective-permute-done | bytes 262176 | tf_op jit(solution)/shard_map/ppermute | solution.py:423
  64.0 1.5 %collective-permute-done.3.q11 = f32[512,128]{1,0:T(8,128)S(1)} collective-permute-done((f32[512,128]{1,0:T(8,128)S(1)}, f32[512,128]{1,0:T(8,128)S(1)}, u32[]{:S(2)}, u32[]{:S(2)}) %collective-permute-start.3) | collective-permute-done | bytes 262176 | tf_op jit(solution)/shard_map/ppermute | solution.py:423
  65.5 15.4 %shard_map.143 = (f32[1024,128]{1,0:T(8,128)S(1)}, f32[1024,128]{1,0:T(8,128)S(1)}) custom-call(f32[512,128]{1,0:T(8,128)S(1)} %bitcast.30, f32[512,128]{1,0:T(8,128)S(1)} %collective-permute-done.1.q10, f32[512,128]{1,0:T(8,128)S(1)} %collective-permute-done.2.q01, f32[512,128]{1,0:T(8,128)S(1)} %collective-permute-done.3.q11, ...), custom_call_target="tpu_custom_call" | custom-call | tf_op jit(solution)/shard_map/pallas_call | solution.py:316
  81.0 0.2 collective-permute-start.4
  81.2 1.8 %collective-permute-done.4 = f32[1024,128]{1,0:T(8,128)S(1)} collective-permute-done((f32[1024,128]{1,0:T(8,128)S(1)}, f32[1024,128]{1,0:T(8,128)S(1)}, u32[]{:S(2)}, u32[]{:S(2)}) %collective-permute-start.4) | collective-permute-done | bytes 524320 | tf_op jit(solution)/shard_map/ppermute | solution.py:423
  83.0 0.1 add_bitcast_fusion
  83.1 28.5 %all_to_all.17 = f32[128,8,128]{2,1,0:T(8,128)S(1)} all-to-all(f32[128,8,128]{2,1,0:T(8,128)S(1)} %add_bitcast_fusion), channel_id=1, replica_groups=mesh['xl'=2,'y'=4,'z'=8,'xh'=2,'co'=2] {'y','z','xl','xh'}, dimensions={0} | all-to-all | bytes 1048576 | tf_op jit(solution)/shard_map/all_to_all | solution.py:419
  111.6 3.3 %shard_map.144 = (bf16[2,128,32,128]{3,2,1,0:T(8,128)(2,1)}, bf16[2,128,32,128]{3,2,1,0:T(8,128)(2,1)}) custom-call(f32[1024,128]{1,0:T(8,128)S(1)} %bitcast.26, f32[64,128]{1,0:T(8,128)S(1)} %get-tuple-element.63.spectra, bf16[256,1024]{1,0:T(8,128)(2,1)S(1)} %copy-done.4), custom_call_target="tpu_custom_call" | custom-call | tf_op jit(solution)/shard_map/pallas_call | solution.py:406
  (23 shorter events, 0.1 us)
Async XLA Ops:
  0.7 1.2 %copy-start = (bf16[128,1,32,128]{3,2,1,0:T(8,128)(2,1)S(1)}, bf16[128,1,32,128]{3,2,1,0:T(8,128)(2,1)}, u32[]{:S(2)}) copy-start(bf16[128,1,32,128]{3,2,1,0:T(8,128)(2,1)} %param.13) | copy-start | bytes 3145732
  1.9 0.9 copy-start.2
  2.8 0.8 copy-start.5
  3.7 32.9 %copy-start.11 = (bf16[128,512]{1,0:T(8,128)(2,1)S(1)}, bf16[128,512]{1,0:T(8,128)(2,1)}, u32[]{:S(2)}) copy-start(bf16[128,512]{1,0:T(8,128)(2,1)} %constant.26.clone.xf) | copy-start | bytes 393220
  5.3 1.6 %collective-permute-start = (f32[512,128]{1,0:T(8,128)S(1)}, f32[512,128]{1,0:T(8,128)S(1)}, u32[]{:S(2)}, u32[]{:S(2)}) collective-permute-start(f32[512,128]{1,0:T(8,128)S(1)} %get-tuple-element.35), channel_id=1, source_target_pairs={{0,1},{1,0},{2,3},{3,2},{4,5},{5,4},{6,7},{7,6},{8,9},{9,8},{10,11... | collective-permute-start | bytes 786440 | tf_op jit(solution)/shard_map/ppermute | solution.py:423
  36.6 21.1 %copy-start.1 = (bf16[128,1,32,128]{3,2,1,0:T(8,128)(2,1)S(1)}, bf16[128,1,32,128]{3,2,1,0:T(8,128)(2,1)}, u32[]{:S(2)}) copy-start(bf16[128,1,32,128]{3,2,1,0:T(8,128)(2,1)} %param.13) | copy-start | bytes 3145732
  56.1 7.9 %collective-permute-start.1 = (f32[512,128]{1,0:T(8,128)S(1)}, f32[512,128]{1,0:T(8,128)S(1)}, u32[]{:S(2)}, u32[]{:S(2)}) collective-permute-start(f32[512,128]{1,0:T(8,128)S(1)} %bitcast.28), channel_id=1, source_target_pairs={{0,2},{2,0},{1,3},{3,1},{4,6},{6,4},{5,7},{7,5},{8,10},{10,8},{9,1... | collective-permute-start | bytes 786440 | tf_op jit(solution)/shard_map/ppermute | solution.py:423
  57.7 6.3 %collective-permute-start.2 = (f32[512,128]{1,0:T(8,128)S(1)}, f32[512,128]{1,0:T(8,128)S(1)}, u32[]{:S(2)}, u32[]{:S(2)}) collective-permute-start(f32[512,128]{1,0:T(8,128)S(1)} %bitcast.29), channel_id=1, source_target_pairs={{0,1},{1,0},{2,3},{3,2},{4,5},{5,4},{6,7},{7,6},{8,9},{9,8},{10,11... | collective-permute-start | bytes 786440 | tf_op jit(solution)/shard_map/ppermute | solution.py:423
  57.7 3.0 %copy-start.3 = (bf16[4,64,192]{2,1,0:T(8,128)(2,1)S(1)}, bf16[4,64,192]{2,1,0:T(8,128)(2,1)}, u32[]{:S(2)}) copy-start(bf16[4,64,192]{2,1,0:T(8,128)(2,1)} %constant.23.clone.yf.yf_) | copy-start | bytes 294916
  57.7 3.0 %copy-start.6 = (bf16[2,64,256]{2,1,0:T(8,128)(2,1)S(1)}, bf16[2,64,256]{2,1,0:T(8,128)(2,1)}, u32[]{:S(2)}) copy-start(bf16[2,64,256]{2,1,0:T(8,128)(2,1)} %constant.25.clone.zf.zf_) | copy-start | bytes 196612
  57.7 3.0 %copy-start.7 = (bf16[128,512]{1,0:T(8,128)(2,1)S(1)}, bf16[128,512]{1,0:T(8,128)(2,1)}, u32[]{:S(2)}) copy-start(bf16[128,512]{1,0:T(8,128)(2,1)} %w1_) | copy-start | bytes 393220
  57.7 3.0 %copy-start.8 = (bf16[512,128]{1,0:T(8,128)(2,1)S(1)}, bf16[512,128]{1,0:T(8,128)(2,1)}, u32[]{:S(2)}) copy-start(bf16[512,128]{1,0:T(8,128)(2,1)} %w2_) | copy-start | bytes 393220
  57.7 3.0 %copy-start.9 = (bf16[4,128,96]{2,1,0:T(8,128)(2,1)S(1)}, bf16[4,128,96]{2,1,0:T(8,128)(2,1)}, u32[]{:S(2)}) copy-start(bf16[4,128,96]{2,1,0:T(8,128)(2,1)} %constant.24.clone.zi_) | copy-start | bytes 294916
  60.8 0.9 copy-start.10
  64.0 1.5 %collective-permute-start.3 = (f32[512,128]{1,0:T(8,128)S(1)}, f32[512,128]{1,0:T(8,128)S(1)}, u32[]{:S(2)}, u32[]{:S(2)}) collective-permute-start(f32[512,128]{1,0:T(8,128)S(1)} %collective-permute-done.1.q10), channel_id=1, source_target_pairs={{0,1},{1,0},{2,3},{3,2},{4,5},{5,4},{6,7},{7,6},{8,9},{9,8},{10,11... | collective-permute-start | bytes 786440 | tf_op jit(solution)/shard_map/ppermute | solution.py:423
  81.0 30.6 %copy-start.4 = (bf16[256,1024]{1,0:T(8,128)(2,1)S(1)}, bf16[256,1024]{1,0:T(8,128)(2,1)}, u32[]{:S(2)}) copy-start(bf16[256,1024]{1,0:T(8,128)(2,1)} %constant.28.clone.xf) | copy-start | bytes 1572868
  81.0 2.0 %collective-permute-start.4 = (f32[1024,128]{1,0:T(8,128)S(1)}, f32[1024,128]{1,0:T(8,128)S(1)}, u32[]{:S(2)}, u32[]{:S(2)}) collective-permute-start(f32[1024,128]{1,0:T(8,128)S(1)} %get-tuple-element.62), channel_id=1, source_target_pairs={{0,1},{1,0},{2,3},{3,2},{4,5},{5,4},{6,7},{7,6},{8,9},{9,8},{10,11... | collective-permute-start | bytes 1572872 | tf_op jit(solution)/shard_map/ppermute | solution.py:423

commit v4 on v2

--- a/solution.py
+++ b/solution.py
@@ -28,6 +28,7 @@
 ROWS_A_STEP = 16
 CHUNK = ROWS_A_STEP * NZ
 CB = 64
+PIECES = 4
 
 GX = ("xl", "y", "z")
 COL = ("xh", "co")
@@ -195,14 +196,28 @@
                     sink[place, :] = rows[at : at + 16, i * C : (i + 1) * C]
 
 
-def state_kernel(place, state, zf, yf, keep, give, after):
-    for y in range(0, ROWS, 2):
-        pair = jnp.concatenate([state[(y + i) * NZ : (y + i + 1) * NZ] for i in range(2)], axis=1)
-        rows = dot(zf[0, :, :NZ], pair)
-        rows = rows[: 2 * MZ] + rows[2 * MZ :]
-        for i in range(2):
-            after[0, pl.ds((y + i) * 2 * MZ, 2 * MZ), :] = rows[:, i * C : (i + 1) * C]
-    columns_forward(1, yf[0], after, keep, give)
+def state_kernel(place, state_, zf_, yf_, keep, give, after, state, zf, yf, arrivals):
+    rows_each = ROWS // PIECES
+    copies = [pltpu.make_async_copy(zf_.at[place[1]], zf, arrivals.at[0])]
+    for i in range(PIECES):
+        at = pl.ds(i * rows_each, rows_each)
+        copies.append(pltpu.make_async_copy(state_.at[:, at], state.at[:, at], arrivals.at[i + 1]))
+    copies.append(pltpu.make_async_copy(yf_.at[place[0]], yf, arrivals.at[PIECES + 1]))
+    for copy in copies:
+        copy.start()
+    copies[0].wait()
+    for i in range(PIECES):
+        copies[i + 1].wait()
+        first = i * rows_each
+        planes = jnp.transpose(state[:, first : first + rows_each], (1, 0, 2))
+        for y in range(0, rows_each, 2):
+            pair = planes[y : y + 2].reshape(2 * C, NZ)
+            rows = lax.dot_general(zf[:, :NZ], pair, (((1,), (1,)), ((), ())), preferred_element_type=F32)
+            rows = rows[: 2 * MZ] + rows[2 * MZ :]
+            for j in range(2):
+                after[0, pl.ds((first + y + j) * 2 * MZ, 2 * MZ), :] = rows[:, j * C : (j + 1) * C]
+    copies[PIECES + 1].wait()
+    columns_forward(1, yf[...], after, keep, give)
 
 
 def ready_kernel(place, w1_, w2_, yi_, zi_, zf_, yf_, w1, w2, w1t, w2t, yi, zi, zf, yf):
@@ -277,6 +292,18 @@
     return pl.BlockSpec((1,) + table.shape[1:], lambda i, place: (place[index], 0, 0))
 
 
+FAR = pl.BlockSpec(memory_space=pltpu.HBM)
+MIB = 1024 * 1024
+
+
+def cost(flops, size):
+    return pl.CostEstimate(flops=flops, bytes_accessed=size, transcendentals=0)
+
+
+def stay(array):
+    return pltpu.with_memory_space_constraint(array, pltpu.HBM)
+
+
 def state_stage(place, state, zf, yf):
     shape = jax.ShapeDtypeStruct((512, C), F32)
     return pl.pallas_call(
@@ -284,13 +311,20 @@
         grid_spec=pltpu.PrefetchScalarGridSpec(
             num_scalar_prefetch=1,
             grid=(1,),
-            in_specs=[still(state.shape), picked(zf, 1), picked(yf, 0)],
+            in_specs=[FAR] * 3,
             out_specs=(still((512, C)), still((512, C))),
-            scratch_shapes=[pltpu.VMEM((1, 1024, C), F32)],
+            scratch_shapes=[
+                pltpu.VMEM((1, 1024, C), F32),
+                pltpu.VMEM(state.shape, BF16),
+                pltpu.VMEM(zf.shape[1:], BF16),
+                pltpu.VMEM(yf.shape[1:], BF16),
+                pltpu.SemaphoreType.DMA((PIECES + 2,)),
+            ],
         ),
         out_shape=(shape, shape),
-        compiler_params=params(),
-    )(place, state, zf, yf)
+        cost_estimate=cost(200_000_000, 8 * MIB),
+        compiler_params=params(16),
+    )(place, stay(state), stay(zf), stay(yf))
 
 
 def ready_stage(place, w1, w2, tables):
@@ -304,6 +338,7 @@
             out_specs=tuple(still(shape) for shape in shapes),
         ),
         out_shape=tuple(jax.ShapeDtypeStruct(shape, BF16) for shape in shapes),
+        cost_estimate=cost(0, 2 * MIB),
         compiler_params=params(16),
     )(place, w1, w2, *tables)
 
@@ -318,58 +353,79 @@
         out_specs=(whole((1024, C)), whole((1024, C))),
         out_shape=(shape, shape),
         scratch_shapes=[pltpu.VMEM((2, 1024, C), F32), pltpu.VMEM((2, 1024, C), F32)],
+        cost_estimate=cost(5_000_000_000, 50 * MIB),
         compiler_params=params(),
     )(*quarters, state, target, *ready)
 
 
-def mix_kernel(received, weight, direction, xf, xi_, spectra, planes, total, xi, arrival):
+def mix_kernel(received, weight, direction, xf, xi_, spectra, planes, total, held, xi, arrivals):
     step = pl.program_id(0)
-    second = pltpu.make_async_copy(xi_, xi, arrival)
+    copies = [
+        pltpu.make_async_copy(direction.at[:, pl.ds(i * CB, CB)], held.at[:, pl.ds(i * CB, CB)], arrivals.at[i])
+        for i in range(C // CB)
+    ]
+    last = pltpu.make_async_copy(xi_, xi, arrivals.at[C // CB])
 
     @pl.when(step == 0)
     def _():
-        second.start()
+        for copy in copies:
+            copy.start()
+        last.start()
         spectra[...] = tall_dot(xf[...], received[...])
         total[...] = jnp.zeros_like(total)
 
     turned = pltpu.roll(spectra[...], C - step * CB, 1)
-    sums = [total[i] for i in range(4)]
-    for j in range(CB):
-        column = jnp.broadcast_to(turned[:, j : j + 1], (64, C))
-        real, imag = column[:32], column[32:]
-        for s, w in ((0, weight), (1, direction)):
-            wr, wi = w[0, j].astype(F32), w[1, j].astype(F32)
-            sums[2 * s] = sums[2 * s] + (wr * real - wi * imag)
-            sums[2 * s + 1] = sums[2 * s + 1] + (wr * imag + wi * real)
-    for i in range(4):
-        total[i] = sums[i]
+
+    def gather(s, pair):
+        real_sum, imag_sum = total[2 * s], total[2 * s + 1]
+        for j in range(CB):
+            column = jnp.broadcast_to(turned[:, j : j + 1], (64, C))
+            real, imag = column[:32], column[32:]
+            wr, wi = pair(j)
+            real_sum = real_sum + (wr * real - wi * imag)
+            imag_sum = imag_sum + (wr * imag + wi * real)
+        total[2 * s], total[2 * s + 1] = real_sum, imag_sum
+
+    gather(0, lambda j: (weight[0, j].astype(F32), weight[1, j].astype(F32)))
+    for i in range(C // CB):
+
+        @pl.when(step == i)
+        def _():
+            copies[i].wait()
+
+    gather(1, lambda j: (held[0, step * CB + j].astype(F32), held[1, step * CB + j].astype(F32)))
 
     @pl.when(step == C // CB - 1)
     def _():
-        second.wait()
-        out = dot(xi[...], three(jnp.concatenate(sums, axis=0)))
-        planes[...] = out
+        last.wait()
+        planes[...] = dot(xi[...], three(total[...].reshape(128, C)))
 
 
 def mix_stage(received, weight, direction):
     xf = x_forward_table(1, FORWARD_FACTOR)
     xi = x_inverse_table(INVERSE_FACTOR)
-    weight = weight.reshape(2, C, 32, C)
-    direction = direction.reshape(2, C, 32, C)
     moving = pl.BlockSpec((2, CB, 32, C), lambda i: (0, i, 0, 0))
     return pl.pallas_call(
         mix_kernel,
         grid=(C // CB,),
-        in_specs=[whole(received.shape), moving, moving, whole(xf.shape), pl.BlockSpec(memory_space=pltpu.HBM)],
+        in_specs=[whole(received.shape), moving, FAR, whole(xf.shape), FAR],
         out_specs=(whole((64, C)), whole((NX * 8, C))),
         out_shape=(jax.ShapeDtypeStruct((64, C), F32), jax.ShapeDtypeStruct((NX * 8, C), F32)),
         scratch_shapes=[
             pltpu.VMEM((4, 32, C), F32),
+            pltpu.VMEM((2, C, 32, C), BF16),
             pltpu.VMEM(xi.shape, BF16),
-            pltpu.SemaphoreType.DMA,
+            pltpu.SemaphoreType.DMA((C // CB + 1,)),
         ],
-        compiler_params=params(),
-    )(received, weight, direction, jnp.asarray(xf), pltpu.with_memory_space_constraint(jnp.asarray(xi), pltpu.HBM))
+        cost_estimate=cost(100_000_000, 9 * MIB),
+        compiler_params=params(16),
+    )(
+        received,
+        weight.reshape(2, C, 32, C),
+        stay(direction.reshape(2, C, 32, C)),
+        jnp.asarray(xf),
+        stay(jnp.asarray(xi)),
+    )
 
 
 def outer_kernel(received, spectra, xf, gradient, curvature, adjoint):
@@ -401,7 +457,8 @@
         out_specs=(moving, moving),
         out_shape=(shape, shape),
         scratch_shapes=[pltpu.VMEM((128, C), F32)],
-        compiler_params=params(),
+        cost_estimate=cost(200_000_000, 11 * MIB),
+        compiler_params=params(24),
     )(received, spectra, jnp.asarray(xf))
 
 
@@ -422,19 +479,18 @@
     def rows_of(cells):
         return cells[:, 0].transpose(1, 2, 0).reshape(ROWS * NZ, C)
 
-    state_rows = rows_of(state)
-    keep, give = state_stage(place, state_rows, zf, yf)
+    keep, give = state_stage(place, state.reshape(C, ROWS, NZ), zf, yf)
     received = exchange(keep + swap(give, "co"), WIDE)
     spectra, planes = mix_stage(received, spectral_weight, direction_weight)
     q00 = exchange(planes, WIDE[:3])
     q10 = swap(q00, "xh")
     q01 = swap(q00, "co")
-    q00, target, w1, w2 = lax.optimization_barrier((q00, target, inner_weight, outer_weight))
+    q00, state, target, w1, w2 = lax.optimization_barrier((q00, state, target, inner_weight, outer_weight))
     ready = ready_stage(place, w1, w2, (yi, zi, zf, yf))
-    target_rows = rows_of(target)
-    q10, ready, target_rows = lax.optimization_barrier((q10, ready, target_rows))
+    rows = rows_of(state), rows_of(target)
+    q10, ready, rows = lax.optimization_barrier((q10, ready, rows))
     q11 = swap(q10, "co")
-    keep, give = field_stage((q00, q10, q01, q11), state_rows, target_rows, ready)
+    keep, give = field_stage((q00, q10, q01, q11), *rows, ready)
     adjoint = exchange(keep + swap(give, "co"), WIDE)
     gradient, curvature = outer_stage(adjoint, spectra)
     shape = (2, C, MX, 2, C)

time: 114 us -> 115 us (level)
  Pallas kernels: 23.5 us -> 26.9 us
  waiting for transfers between devices: 7.55 us -> 6.33 us
    pallas_call x1, Pallas kernels: 1.4 us -> 3.21 us  [state_stage(): pl.pallas_call(state_kernel, grid_spec=pltpu.PrefetchScalarGridSpec(num_s...]
    ppermute x5, waiting for transfers between devices: 7.55 us -> 6.33 us  [swap(): return lax.ppermute(rows, axis, [(0, 1), (1, 0)])]
  transfers between devices with their start and end apart: 5 -> 5, of which waited for: 4 -> 4; matrix products, arithmetic and copies ran while one was open for 2% -> 3% of each run, Pallas kernels for 1% -> 1%
where the time goes in v4:
time: 115 us; the launch traced here: 114 us
  blocking collectives  74.3 us (65%)
  Pallas kernels  26.9 us (23%)
  waiting for transfers between devices  6.33 us (6%)
  local copies, waits for them, and re-layouts  4.04 us (4%)
  starting transfers between devices  1.9 us (2%)
    all_to_all x3, blocking collectives, exchange(): lax.all_to_all(rows.reshape(size, -1, C), group, 0, 0, tiled=True)  74.3 us
    pallas_call x1, Pallas kernels, field_stage(): pl.pallas_call(field_kernel, grid=(ROWS // ROWS_A_STEP,), in_specs=[whole...  16.4 us
    ppermute x5, waiting for transfers between devices, swap(): return lax.ppermute(rows, axis, [(0, 1), (1, 0)])  6.33 us
    transpose x2, local copies, waits for them, and re-layouts, rows_of(): return cells[:, 0].transpose(1, 2, 0).reshape(ROWS * NZ, C)  3.99 us
    pallas_call x1, Pallas kernels, mix_stage(): pl.pallas_call(mix_kernel, grid=(C // CB,), in_specs=[whole(received.shap...  3.42 us
    pallas_call x1, Pallas kernels, outer_stage(): pl.pallas_call(outer_kernel, grid=(C // CB,), in_specs=[whole(received.sh...  3.27 us
    pallas_call x1, Pallas kernels, state_stage(): pl.pallas_call(state_kernel, grid_spec=pltpu.PrefetchScalarGridSpec(num_s...  3.21 us
  transfers between devices with their start and end apart: 5, of which 4 were waited for; matrix products, arithmetic and copies ran while one was open for 3% of the time, Pallas kernels for 1%

profile of v4, /device:TPU:2, one launch (start us, length us, event | category | flops | bytes accessed | tf_op | source)
XLA Modules:
  0.0 114.4 jit_solution(142678590011342736)
XLA Ops:
  0.6 0.0 copy-start.8
  0.7 0.1 pad_add_fusion.place
  0.7 3.2 %shard_map.140 = (f32[512,128]{1,0:T(8,128)S(1)}, f32[512,128]{1,0:T(8,128)S(1)}) custom-call(s32[2]{0:T(128)S(1)} %pad_add_fusion.place, bf16[128,32,128]{2,1,0:T(8,128)(2,1)} %bitcast.31, bf16[2,64,256]{2,1,0:T(8,128)(2,1)} %constant.25.clone.zf_, bf16[4,64,192]{2,1,0:T(8,128)(2,1)} %constant.23.clone.yf_), custom_call_target="tpu_custom_call" | custom-call | flops 200000000 | bytes 8388608 | tf_op jit(solution)/shard_map/pallas_call | solution.py:309
  3.9 0.1 collective-permute-start
  4.0 1.5 %collective-permute-done = f32[512,128]{1,0:T(8,128)S(1)} collective-permute-done((f32[512,128]{1,0:T(8,128)S(1)}, f32[512,128]{1,0:T(8,128)S(1)}, u32[]{:S(2)}, u32[]{:S(2)}) %collective-permute-start) | collective-permute-done | bytes 262176 | tf_op jit(solution)/shard_map/ppermute | solution.py:471
  5.6 29.6 %all_to_all.15 = f32[128,4,128]{2,1,0:T(4,128)S(1)} all-to-all(f32[128,4,128]{2,1,0:T(4,128)S(1)} %bitcast.34), channel_id=1, replica_groups=mesh['xl'=2,'y'=4,'z'=8,'xh'=2,'co'=2] {'y','z','xl','xh'}, dimensions={0} | all-to-all | bytes 524288 | tf_op jit(solution)/shard_map/all_to_all | solution.py:467
  35.2 3.4 %shard_map.141 = (f32[64,128]{1,0:T(8,128)S(1)}, f32[512,128]{1,0:T(8,128)S(1)}) custom-call(f32[512,128]{1,0:T(8,128)S(1)} %bitcast.24, bf16[2,128,32,128]{3,2,1,0:T(8,128)(2,1)S(1)} %bitcast.22, bf16[2,128,32,128]{3,2,1,0:T(8,128)(2,1)} %bitcast.33, bf16[128,512]{1,0:T(8,128)(2,1)S(1)} %copy-done.8, bf16[512,384]{1,0:T(8,128)(2,1)} %constant.27.clone.xi_), custom_call_target="tpu_custom_call" | custom-call | flops 100000000 | bytes 9437184 | tf_op jit(solution)/shard_map/pallas_call | solution.py:408
  38.6 16.1 %all_to_all.16 = f32[64,8,128]{2,1,0:T(8,128)S(1)} all-to-all(f32[64,8,128]{2,1,0:T(8,128)S(1)} %bitcast.30), channel_id=1, replica_groups=mesh['xl'=2,'y'=4,'z'=8,'xh'=2,'co'=2] {'y','z','xl'}, dimensions={0} | all-to-all | bytes 524288 | tf_op jit(solution)/shard_map/all_to_all | solution.py:467
  54.8 1.6 %collective-permute-start.1 = (f32[512,128]{1,0:T(8,128)S(1)}, f32[512,128]{1,0:T(8,128)S(1)}, u32[]{:S(2)}, u32[]{:S(2)}) collective-permute-start(f32[512,128]{1,0:T(8,128)S(1)} %bitcast.27), channel_id=1, source_target_pairs={{0,2},{2,0},{1,3},{3,1},{4,6},{6,4},{5,7},{7,5},{8,10},{10,8},{9,1... | collective-permute-start | bytes 786440 | tf_op jit(solution)/shard_map/ppermute | solution.py:471
  56.4 0.0 copy-start.5
  56.4 0.0 copy-start.6
  56.4 0.0 copy-start.7
  56.4 2.0 %copy.15 = bf16[32,128,128]{2,1,0:T(8,128)(2,1)S(1)} copy(bf16[32,128,128]{1,0,2:T(8,128)(2,1)} %bitcast.32) | data formatting | bytes 2097152 | tf_op jit(solution)/shard_map/transpose | solution.py:480
  58.5 2.0 %copy.16 = bf16[32,128,128]{2,1,0:T(8,128)(2,1)S(1)} copy(bf16[32,128,128]{1,0,2:T(8,128)(2,1)} %bitcast.35) | data formatting | bytes 2097152 | tf_op jit(solution)/shard_map/transpose | solution.py:480
  60.5 0.7 shard_map.142
  61.2 1.5 %collective-permute-done.1.q10 = f32[512,128]{1,0:T(8,128)S(1)} collective-permute-done((f32[512,128]{1,0:T(8,128)S(1)}, f32[512,128]{1,0:T(8,128)S(1)}, u32[]{:S(2)}, u32[]{:S(2)}) %collective-permute-start.1) | collective-permute-done | bytes 262176 | tf_op jit(solution)/shard_map/ppermute | solution.py:471
  62.7 1.5 %collective-permute-done.3.q11 = f32[512,128]{1,0:T(8,128)S(1)} collective-permute-done((f32[512,128]{1,0:T(8,128)S(1)}, f32[512,128]{1,0:T(8,128)S(1)}, u32[]{:S(2)}, u32[]{:S(2)}) %collective-permute-start.3) | collective-permute-done | bytes 262176 | tf_op jit(solution)/shard_map/ppermute | solution.py:471
  64.2 16.4 %shard_map.143 = (f32[1024,128]{1,0:T(8,128)S(1)}, f32[1024,128]{1,0:T(8,128)S(1)}) custom-call(f32[512,128]{1,0:T(8,128)S(1)} %bitcast.29, f32[512,128]{1,0:T(8,128)S(1)} %collective-permute-done.1.q10, f32[512,128]{1,0:T(8,128)} %collective-permute-done.2.q01, f32[512,128]{1,0:T(8,128)S(1)} %collective-permute-done.3.q11, bf16[4096,128]{1,0:T(8,128)(2,1)S(1)} %bitcast.25, ...), custom_call_target="tpu_custom_call" | custom-call | flops 5000000000 | bytes 52428800 | tf_op jit(solution)/shard_map/pallas_call | solution.py:349
  80.6 0.0 copy-start.2
  80.6 0.2 collective-permute-start.4
  80.8 1.8 %collective-permute-done.4 = f32[1024,128]{1,0:T(8,128)S(1)} collective-permute-done((f32[1024,128]{1,0:T(8,128)S(1)}, f32[1024,128]{1,0:T(8,128)S(1)}, u32[]{:S(2)}, u32[]{:S(2)}) %collective-permute-start.4) | collective-permute-done | bytes 524320 | tf_op jit(solution)/shard_map/ppermute | solution.py:471
  82.6 0.1 add_bitcast_fusion
  82.6 28.5 %all_to_all.17 = f32[128,8,128]{2,1,0:T(8,128)S(1)} all-to-all(f32[128,8,128]{2,1,0:T(8,128)S(1)} %add_bitcast_fusion), channel_id=1, replica_groups=mesh['xl'=2,'y'=4,'z'=8,'xh'=2,'co'=2] {'y','z','xl','xh'}, dimensions={0} | all-to-all | bytes 1048576 | tf_op jit(solution)/shard_map/all_to_all | solution.py:467
  111.2 3.3 %shard_map.144 = (bf16[2,128,32,128]{3,2,1,0:T(8,128)(2,1)}, bf16[2,128,32,128]{3,2,1,0:T(8,128)(2,1)}) custom-call(f32[1024,128]{1,0:T(8,128)S(1)} %bitcast.23, f32[64,128]{1,0:T(8,128)S(1)} %get-tuple-element.63.spectra, bf16[256,1024]{1,0:T(8,128)(2,1)S(1)} %copy-done.2), custom_call_target="tpu_custom_call" | custom-call | flops 200000000 | bytes 11534336 | tf_op jit(solution)/shard_map/pallas_call | solution.py:453
  (17 shorter events, 0.1 us)
Async XLA Ops:
  0.6 34.6 %copy-start.8 = (bf16[128,512]{1,0:T(8,128)(2,1)S(1)}, bf16[128,512]{1,0:T(8,128)(2,1)}, u32[]{:S(2)}) copy-start(bf16[128,512]{1,0:T(8,128)(2,1)} %constant.26.clone.xf) | copy-start | bytes 393220
  0.6 34.6 %copy-start = (bf16[2,128,16,2,128]{4,3,2,1,0:T(2,128)(2,1)S(1)}, bf16[2,128,16,2,128]{4,3,2,1,0:T(2,128)(2,1)}, u32[]{:S(2)}) copy-start(bf16[2,128,16,2,128]{4,3,2,1,0:T(2,128)(2,1)} %param.15) | copy-start | bytes 6291460
  3.9 1.6 %collective-permute-start = (f32[512,128]{1,0:T(8,128)S(1)}, f32[512,128]{1,0:T(8,128)S(1)}, u32[]{:S(2)}, u32[]{:S(2)}) collective-permute-start(f32[512,128]{1,0:T(8,128)S(1)} %get-tuple-element.35), channel_id=1, source_target_pairs={{0,1},{1,0},{2,3},{3,2},{4,5},{5,4},{6,7},{7,6},{8,9},{9,8},{10,11... | collective-permute-start | bytes 786440 | tf_op jit(solution)/shard_map/ppermute | solution.py:471
  54.8 7.9 %collective-permute-start.1 = (f32[512,128]{1,0:T(8,128)S(1)}, f32[512,128]{1,0:T(8,128)S(1)}, u32[]{:S(2)}, u32[]{:S(2)}) collective-permute-start(f32[512,128]{1,0:T(8,128)S(1)} %bitcast.27), channel_id=1, source_target_pairs={{0,2},{2,0},{1,3},{3,1},{4,6},{6,4},{5,7},{7,5},{8,10},{10,8},{9,1... | collective-permute-start | bytes 786440 | tf_op jit(solution)/shard_map/ppermute | solution.py:471
  56.4 6.3 %collective-permute-start.2 = (f32[512,128]{1,0:T(8,128)S(1)}, f32[512,128]{1,0:T(8,128)}, u32[]{:S(2)}, u32[]{:S(2)}) collective-permute-start(f32[512,128]{1,0:T(8,128)S(1)} %bitcast.28), channel_id=1, source_target_pairs={{0,1},{1,0},{2,3},{3,2},{4,5},{5,4},{6,7},{7,6},{8,9},{9,8},{10,11... | collective-permute-start | bytes 786440 | tf_op jit(solution)/shard_map/ppermute | solution.py:471
  56.4 4.1 %copy-start.1 = (bf16[4,64,192]{2,1,0:T(8,128)(2,1)S(1)}, bf16[4,64,192]{2,1,0:T(8,128)(2,1)}, u32[]{:S(2)}) copy-start(bf16[4,64,192]{2,1,0:T(8,128)(2,1)} %constant.23.clone.yf_) | copy-start | bytes 294916
  56.4 4.1 %copy-start.3 = (bf16[2,64,256]{2,1,0:T(8,128)(2,1)S(1)}, bf16[2,64,256]{2,1,0:T(8,128)(2,1)}, u32[]{:S(2)}) copy-start(bf16[2,64,256]{2,1,0:T(8,128)(2,1)} %constant.25.clone.zf_) | copy-start | bytes 196612
  56.4 4.1 %copy-start.4 = (bf16[128,512]{1,0:T(8,128)(2,1)S(1)}, bf16[128,512]{1,0:T(8,128)(2,1)}, u32[]{:S(2)}) copy-start(bf16[128,512]{1,0:T(8,128)(2,1)} %w1_) | copy-start | bytes 393220
  56.4 4.1 %copy-start.5 = (bf16[512,128]{1,0:T(8,128)(2,1)S(1)}, bf16[512,128]{1,0:T(8,128)(2,1)}, u32[]{:S(2)}) copy-start(bf16[512,128]{1,0:T(8,128)(2,1)} %w2_) | copy-start | bytes 393220
  56.4 4.1 %copy-start.6 = (bf16[4,128,96]{2,1,0:T(8,128)(2,1)S(1)}, bf16[4,128,96]{2,1,0:T(8,128)(2,1)}, u32[]{:S(2)}) copy-start(bf16[4,128,96]{2,1,0:T(8,128)(2,1)} %constant.24.clone.zi_) | copy-start | bytes 294916
  56.4 4.1 %copy-start.7 = (bf16[4,64,192]{2,1,0:T(8,128)(2,1)S(1)}, bf16[4,64,192]{2,1,0:T(8,128)(2,1)}, u32[]{:S(2)}) copy-start(bf16[4,64,192]{2,1,0:T(8,128)(2,1)} %constant.22.clone.yi_) | copy-start | bytes 294916
  62.6 1.5 %collective-permute-start.3 = (f32[512,128]{1,0:T(8,128)S(1)}, f32[512,128]{1,0:T(8,128)S(1)}, u32[]{:S(2)}, u32[]{:S(2)}) collective-permute-start(f32[512,128]{1,0:T(8,128)S(1)} %collective-permute-done.1.q10), channel_id=1, source_target_pairs={{0,1},{1,0},{2,3},{3,2},{4,5},{5,4},{6,7},{7,6},{8,9},{9,8},{10,11... | collective-permute-start | bytes 786440 | tf_op jit(solution)/shard_map/ppermute | solution.py:471
  80.6 30.6 %copy-start.2 = (bf16[256,1024]{1,0:T(8,128)(2,1)S(1)}, bf16[256,1024]{1,0:T(8,128)(2,1)}, u32[]{:S(2)}) copy-start(bf16[256,1024]{1,0:T(8,128)(2,1)} %constant.28.clone.xf) | copy-start | bytes 1572868
  80.6 2.0 %collective-permute-start.4 = (f32[1024,128]{1,0:T(8,128)S(1)}, f32[1024,128]{1,0:T(8,128)S(1)}, u32[]{:S(2)}, u32[]{:S(2)}) collective-permute-start(f32[1024,128]{1,0:T(8,128)S(1)} %get-tuple-element.62), channel_id=1, source_target_pairs={{0,1},{1,0},{2,3},{3,2},{4,5},{5,4},{6,7},{7,6},{8,9},{9,8},{10,11... | collective-permute-start | bytes 1572872 | tf_op jit(solution)/shard_map/ppermute | solution.py:471

commit v5 on v2

--- a/solution.py
+++ b/solution.py
@@ -216,28 +216,37 @@
     yf[...] = yf_[0]
 
 
+def y_inverse(parts, table, half):
+    for k in range(4 * len(parts)):
+        rows = []
+        for s in range(2):
+            p = [parts[k // 4][place, :] for i in range(2) for place in back_rows(k, 2 * s + i)]
+            rows.append(jnp.concatenate(p, axis=0))
+        rows = dot(table, three(jnp.concatenate(rows, axis=1)))
+        for s in range(2):
+            half[s, pl.ds(k * 64, 64), :] = rows[:, s * C : (s + 1) * C]
+
+
+def early_kernel(q00, q10, q01, yi, half):
+    y_inverse((q00, q10, q01), yi[...], half)
+
+
 def field_kernel(
-    q00, q10, q01, q11, state, target, w1, w2, w1t, w2t, yi, zi, zf, yf, keep, give, half, after
+    early, q11, state, target, w1, w2, w1t, w2t, yi, zi, zf, yf, keep, give, late, after
 ):
     step = pl.program_id(0)
 
     @pl.when(step == 0)
     def _():
-        for k in range(MZ):
-            source = (q00, q10, q01, q11)[k // 4]
-            parts = []
-            for s in range(2):
-                p = [source[place, :] for i in range(2) for place in back_rows(k, 2 * s + i)]
-                parts.append(jnp.concatenate(p, axis=0))
-            rows = dot(yi[...], three(jnp.concatenate(parts, axis=1)))
-            for s in range(2):
-                half[s, pl.ds(k * 64, 64), :] = rows[:, s * C : (s + 1) * C]
+        y_inverse((q11,), yi[...], late)
 
     first = step * ROWS_A_STEP
     fields = []
     for i in range(ROWS_A_STEP):
-        taken = [half[s, pl.ds(first + i, 2 * MZ, stride=ROWS), :] for s in range(2)]
-        fields.append(dot(zi[...], three(jnp.concatenate(taken, axis=1))))
+        taken = []
+        for part, count in ((early, 24), (late, 8)):
+            taken.append(jnp.concatenate([part[s, pl.ds(first + i, count, stride=ROWS), :] for s in range(2)], axis=1))
+        fields.append(dot(zi[...], three(jnp.concatenate(taken, axis=0))))
     fields = jnp.concatenate(fields, axis=0).astype(BF16)
     primal, tangent = fields[:, :C], fields[:, C:]
     layer_input = state[...].astype(F32) + primal.astype(F32)
@@ -308,18 +317,30 @@
     )(place, w1, w2, *tables)
 
 
-def field_stage(quarters, state, target, ready):
+def early_stage(q00, q10, q01, yi):
+    shape = (2, 768, C)
+    return pl.pallas_call(
+        early_kernel,
+        grid=(1,),
+        in_specs=[whole((512, C))] * 3 + [whole(yi.shape)],
+        out_specs=whole(shape),
+        out_shape=jax.ShapeDtypeStruct(shape, F32),
+        compiler_params=params(16),
+    )(q00, q10, q01, yi)
+
+
+def field_stage(early, q11, state, target, ready):
     moving = pl.BlockSpec((CHUNK, C), lambda i: (i, 0))
     shape = jax.ShapeDtypeStruct((1024, C), F32)
     return pl.pallas_call(
         field_kernel,
         grid=(ROWS // ROWS_A_STEP,),
-        in_specs=[whole((512, C))] * 4 + [moving] * 2 + [whole(r.shape) for r in ready],
+        in_specs=[whole(early.shape), whole((512, C))] + [moving] * 2 + [whole(r.shape) for r in ready],
         out_specs=(whole((1024, C)), whole((1024, C))),
         out_shape=(shape, shape),
-        scratch_shapes=[pltpu.VMEM((2, 1024, C), F32), pltpu.VMEM((2, 1024, C), F32)],
+        scratch_shapes=[pltpu.VMEM((2, 256, C), F32), pltpu.VMEM((2, 1024, C), F32)],
         compiler_params=params(),
-    )(*quarters, state, target, *ready)
+    )(early, q11, state, target, *ready)
 
 
 def mix_kernel(received, weight, direction, xf, xi_, spectra, planes, total, xi, arrival):
@@ -434,7 +455,8 @@
     target_rows = rows_of(target)
     q10, ready, target_rows = lax.optimization_barrier((q10, ready, target_rows))
     q11 = swap(q10, "co")
-    keep, give = field_stage((q00, q10, q01, q11), state_rows, target_rows, ready)
+    early = early_stage(q00, q10, q01, ready[4])
+    keep, give = field_stage(early, q11, state_rows, target_rows, ready)
     adjoint = exchange(keep + swap(give, "co"), WIDE)
     gradient, curvature = outer_stage(adjoint, spectra)
     shape = (2, C, MX, 2, C)

time: 114 us -> 113 us (level)
  no operation moved by 1% of the time
where the time goes in v5:
time: 113 us
  blocking collectives  74.4 us (66%)
  Pallas kernels  23.7 us (21%)
  waiting for transfers between devices  6.91 us (6%)
  local copies, waits for them, and re-layouts  5.01 us (4%)
  starting transfers between devices  1.91 us (2%)
    all_to_all x3, blocking collectives, exchange(): lax.all_to_all(rows.reshape(size, -1, C), group, 0, 0, tiled=True)  74.4 us
    pallas_call x1, Pallas kernels, field_stage(): pl.pallas_call(field_kernel, grid=(ROWS // ROWS_A_STEP,), in_specs=[whole...  14.9 us
    ppermute x5, waiting for transfers between devices, swap(): return lax.ppermute(rows, axis, [(0, 1), (1, 0)])  6.91 us
    transpose x2, local copies, waits for them, and re-layouts, rows_of(): return cells[:, 0].transpose(1, 2, 0).reshape(ROWS * NZ, C)  4.05 us
    pallas_call x1, Pallas kernels, outer_stage(): pl.pallas_call(outer_kernel, grid=(C // CB,), in_specs=[whole(received.sh...  3.27 us
    pallas_call x1, Pallas kernels, mix_stage(): pl.pallas_call(mix_kernel, grid=(C // CB,), in_specs=[whole(received.shap...  2.76 us
  transfers between devices with their start and end apart: 5, of which 4 were waited for; matrix products, arithmetic and copies ran while one was open for 2% of the time, Pallas kernels for 1%

profile of v5, /device:TPU:2, one launch (start us, length us, event | category | flops | bytes accessed | tf_op | source)
XLA Modules:
  0.0 112.9 jit_solution(3586057020497140295)
XLA Ops:
  0.6 0.0 copy-start.4
  0.6 0.0 copy-start.2
  0.7 0.0 copy-start.9
  0.7 2.1 %copy.15 = bf16[32,128,128]{2,1,0:T(8,128)(2,1)S(1)} copy(bf16[32,128,128]{1,0,2:T(8,128)(2,1)} %bitcast.33) | data formatting | bytes 2097152 | tf_op jit(solution)/shard_map/transpose | solution.py:444
  2.8 0.1 pad_add_fusion.place
  2.9 1.4 %shard_map.140 = (f32[512,128]{1,0:T(8,128)S(1)}, f32[512,128]{1,0:T(8,128)S(1)}) custom-call(s32[2]{0:T(128)S(1)} %pad_add_fusion.place, bf16[4096,128]{1,0:T(8,128)(2,1)S(1)} %bitcast.21, bf16[2,64,256]{2,1,0:T(8,128)(2,1)S(1)} %copy-done.4, bf16[4,64,192]{2,1,0:T(8,128)(2,1)S(1)} %copy-done.2), custom_call_target="tpu_custom_call" | custom-call | tf_op jit(solution)/shard_map/pallas_call | solution.py:291
  4.3 0.1 collective-permute-start
  4.4 1.5 %collective-permute-done = f32[512,128]{1,0:T(8,128)S(1)} collective-permute-done((f32[512,128]{1,0:T(8,128)S(1)}, f32[512,128]{1,0:T(8,128)S(1)}, u32[]{:S(2)}, u32[]{:S(2)}) %collective-permute-start) | collective-permute-done | bytes 262176 | tf_op jit(solution)/shard_map/ppermute | solution.py:435
  6.0 29.6 %all_to_all.15 = f32[128,4,128]{2,1,0:T(4,128)S(1)} all-to-all(f32[128,4,128]{2,1,0:T(4,128)S(1)} %bitcast.32), channel_id=1, replica_groups=mesh['xl'=2,'y'=4,'z'=8,'xh'=2,'co'=2] {'y','z','xl','xh'}, dimensions={0} | all-to-all | bytes 524288 | tf_op jit(solution)/shard_map/all_to_all | solution.py:431
  35.6 2.8 %shard_map.141 = (f32[64,128]{1,0:T(8,128)S(1)}, f32[512,128]{1,0:T(8,128)S(1)}) custom-call(f32[512,128]{1,0:T(8,128)S(1)} %bitcast.30, bf16[2,128,32,128]{3,2,1,0:T(8,128)(2,1)S(1)} %bitcast.24, bf16[2,128,32,128]{3,2,1,0:T(8,128)(2,1)S(1)} %bitcast.25, bf16[128,512]{1,0:T(8,128)(2,1)S(1)} %copy-done.9, bf16[512,384]{1,0:T(8,128)(2,1)} %constant.27.clone.xi_), custom_call_target="tpu_custom_call" | custom-call | tf_op jit(solution)/shard_map/pallas_call | solution.py:381
  38.4 16.3 %all_to_all.16 = f32[64,8,128]{2,1,0:T(8,128)S(1)} all-to-all(f32[64,8,128]{2,1,0:T(8,128)S(1)} %bitcast.31), channel_id=1, replica_groups=mesh['xl'=2,'y'=4,'z'=8,'xh'=2,'co'=2] {'y','z','xl'}, dimensions={0} | all-to-all | bytes 524288 | tf_op jit(solution)/shard_map/all_to_all | solution.py:431
  54.6 1.6 %collective-permute-start.1 = (f32[512,128]{1,0:T(8,128)S(1)}, f32[512,128]{1,0:T(8,128)S(1)}, u32[]{:S(2)}, u32[]{:S(2)}) collective-permute-start(f32[512,128]{1,0:T(8,128)S(1)} %bitcast.27), channel_id=1, source_target_pairs={{0,2},{2,0},{1,3},{3,1},{4,6},{6,4},{5,7},{7,5},{8,10},{10,8},{9,1... | collective-permute-start | bytes 786440 | tf_op jit(solution)/shard_map/ppermute | solution.py:435
  56.2 1.9 %copy.16 = bf16[32,128,128]{2,1,0:T(8,128)(2,1)S(1)} copy(bf16[32,128,128]{1,0,2:T(8,128)(2,1)} %bitcast.34) | data formatting | bytes 2097152 | tf_op jit(solution)/shard_map/transpose | solution.py:444
  58.2 0.9 copy-done.8
  59.1 0.7 shard_map.142
  59.8 2.7 %collective-permute-done.1.q10 = f32[512,128]{1,0:T(8,128)S(1)} collective-permute-done((f32[512,128]{1,0:T(8,128)S(1)}, f32[512,128]{1,0:T(8,128)S(1)}, u32[]{:S(2)}, u32[]{:S(2)}) %collective-permute-start.1) | collective-permute-done | bytes 262176 | tf_op jit(solution)/shard_map/ppermute | solution.py:435
  62.5 0.6 shard_map.143.early
  63.2 0.9 collective-permute-done.3.q11
  64.1 14.9 %shard_map.144 = (f32[1024,128]{1,0:T(8,128)S(1)}, f32[1024,128]{1,0:T(8,128)S(1)}) custom-call(f32[2,768,128]{2,1,0:T(8,128)S(1)} %shard_map.143.early, f32[512,128]{1,0:T(8,128)S(1)} %collective-permute-done.3.q11, bf16[4096,128]{1,0:T(8,128)(2,1)S(1)} %bitcast.22, bf16[4096,128]{1,0:T(8,128)(2,1)S(1)} %bitcast.23, ...), custom_call_target="tpu_custom_call" | custom-call | tf_op jit(solution)/shard_map/pallas_call | solution.py:335
  79.0 0.2 collective-permute-start.4
  79.2 1.8 %collective-permute-done.4 = f32[1024,128]{1,0:T(8,128)S(1)} collective-permute-done((f32[1024,128]{1,0:T(8,128)S(1)}, f32[1024,128]{1,0:T(8,128)S(1)}, u32[]{:S(2)}, u32[]{:S(2)}) %collective-permute-start.4) | collective-permute-done | bytes 524320 | tf_op jit(solution)/shard_map/ppermute | solution.py:435
  81.0 0.1 add_bitcast_fusion
  81.1 28.5 %all_to_all.17 = f32[128,8,128]{2,1,0:T(8,128)S(1)} all-to-all(f32[128,8,128]{2,1,0:T(8,128)S(1)} %add_bitcast_fusion), channel_id=1, replica_groups=mesh['xl'=2,'y'=4,'z'=8,'xh'=2,'co'=2] {'y','z','xl','xh'}, dimensions={0} | all-to-all | bytes 1048576 | tf_op jit(solution)/shard_map/all_to_all | solution.py:431
  109.6 3.3 %shard_map.145 = (bf16[2,128,32,128]{3,2,1,0:T(8,128)(2,1)}, bf16[2,128,32,128]{3,2,1,0:T(8,128)(2,1)}) custom-call(f32[1024,128]{1,0:T(8,128)S(1)} %bitcast.26, f32[64,128]{1,0:T(8,128)S(1)} %get-tuple-element.59.spectra, bf16[256,1024]{1,0:T(8,128)(2,1)S(1)} %copy-done.3), custom_call_target="tpu_custom_call" | custom-call | tf_op jit(solution)/shard_map/pallas_call | solution.py:418
  (20 shorter events, 0.1 us)
Async XLA Ops:
  0.6 2.3 %copy-start.4 = (bf16[2,64,256]{2,1,0:T(8,128)(2,1)S(1)}, bf16[2,64,256]{2,1,0:T(8,128)(2,1)}, u32[]{:S(2)}) copy-start(bf16[2,64,256]{2,1,0:T(8,128)(2,1)} %constant.25.clone.zf.zf_) | copy-start | bytes 196612
  0.6 2.2 %copy-start.2 = (bf16[4,64,192]{2,1,0:T(8,128)(2,1)S(1)}, bf16[4,64,192]{2,1,0:T(8,128)(2,1)}, u32[]{:S(2)}) copy-start(bf16[4,64,192]{2,1,0:T(8,128)(2,1)} %constant.23.clone.yf.yf_) | copy-start | bytes 294916
  0.7 34.9 %copy-start = (bf16[2,128,16,2,128]{4,3,2,1,0:T(2,128)(2,1)S(1)}, bf16[2,128,16,2,128]{4,3,2,1,0:T(2,128)(2,1)}, u32[]{:S(2)}) copy-start(bf16[2,128,16,2,128]{4,3,2,1,0:T(2,128)(2,1)} %param.15) | copy-start | bytes 6291460
  0.7 34.9 %copy-start.9 = (bf16[128,512]{1,0:T(8,128)(2,1)S(1)}, bf16[128,512]{1,0:T(8,128)(2,1)}, u32[]{:S(2)}) copy-start(bf16[128,512]{1,0:T(8,128)(2,1)} %constant.26.clone.xf) | copy-start | bytes 393220
  2.8 32.8 %copy-start.1 = (bf16[2,128,16,2,128]{4,3,2,1,0:T(2,128)(2,1)S(1)}, bf16[2,128,16,2,128]{4,3,2,1,0:T(2,128)(2,1)}, u32[]{:S(2)}) copy-start(bf16[2,128,16,2,128]{4,3,2,1,0:T(2,128)(2,1)} %param.16) | copy-start | bytes 6291460
  4.3 1.6 %collective-permute-start = (f32[512,128]{1,0:T(8,128)S(1)}, f32[512,128]{1,0:T(8,128)S(1)}, u32[]{:S(2)}, u32[]{:S(2)}) collective-permute-start(f32[512,128]{1,0:T(8,128)S(1)} %get-tuple-element.33), channel_id=1, source_target_pairs={{0,1},{1,0},{2,3},{3,2},{4,5},{5,4},{6,7},{7,6},{8,9},{9,8},{10,11... | collective-permute-start | bytes 786440 | tf_op jit(solution)/shard_map/ppermute | solution.py:435
  38.3 19.9 %copy-start.5 = (bf16[128,512]{1,0:T(8,128)(2,1)S(1)}, bf16[128,512]{1,0:T(8,128)(2,1)}, u32[]{:S(2)}) copy-start(bf16[128,512]{1,0:T(8,128)(2,1)} %w1_) | copy-start | bytes 393220
  38.3 19.9 %copy-start.6 = (bf16[512,128]{1,0:T(8,128)(2,1)S(1)}, bf16[512,128]{1,0:T(8,128)(2,1)}, u32[]{:S(2)}) copy-start(bf16[512,128]{1,0:T(8,128)(2,1)} %w2_) | copy-start | bytes 393220
  38.3 19.9 %copy-start.7 = (bf16[4,128,96]{2,1,0:T(8,128)(2,1)S(1)}, bf16[4,128,96]{2,1,0:T(8,128)(2,1)}, u32[]{:S(2)}) copy-start(bf16[4,128,96]{2,1,0:T(8,128)(2,1)} %constant.24.clone.zi_) | copy-start | bytes 294916
  54.6 7.9 %collective-permute-start.1 = (f32[512,128]{1,0:T(8,128)S(1)}, f32[512,128]{1,0:T(8,128)S(1)}, u32[]{:S(2)}, u32[]{:S(2)}) collective-permute-start(f32[512,128]{1,0:T(8,128)S(1)} %bitcast.27), channel_id=1, source_target_pairs={{0,2},{2,0},{1,3},{3,1},{4,6},{6,4},{5,7},{7,5},{8,10},{10,8},{9,1... | collective-permute-start | bytes 786440 | tf_op jit(solution)/shard_map/ppermute | solution.py:435
  56.2 6.3 %collective-permute-start.2 = (f32[512,128]{1,0:T(8,128)S(1)}, f32[512,128]{1,0:T(8,128)S(1)}, u32[]{:S(2)}, u32[]{:S(2)}) collective-permute-start(f32[512,128]{1,0:T(8,128)S(1)} %bitcast.28), channel_id=1, source_target_pairs={{0,1},{1,0},{2,3},{3,2},{4,5},{5,4},{6,7},{7,6},{8,9},{9,8},{10,11... | collective-permute-start | bytes 786440 | tf_op jit(solution)/shard_map/ppermute | solution.py:435
  58.2 0.9 copy-start.8
  62.5 1.5 %collective-permute-start.3 = (f32[512,128]{1,0:T(8,128)S(1)}, f32[512,128]{1,0:T(8,128)S(1)}, u32[]{:S(2)}, u32[]{:S(2)}) collective-permute-start(f32[512,128]{1,0:T(8,128)S(1)} %collective-permute-done.1.q10), channel_id=1, source_target_pairs={{0,1},{1,0},{2,3},{3,2},{4,5},{5,4},{6,7},{7,6},{8,9},{9,8},{10,11... | collective-permute-start | bytes 786440 | tf_op jit(solution)/shard_map/ppermute | solution.py:435
  79.0 30.6 %copy-start.3 = (bf16[256,1024]{1,0:T(8,128)(2,1)S(1)}, bf16[256,1024]{1,0:T(8,128)(2,1)}, u32[]{:S(2)}) copy-start(bf16[256,1024]{1,0:T(8,128)(2,1)} %constant.28.clone.xf) | copy-start | bytes 1572868
  79.0 2.0 %collective-permute-start.4 = (f32[1024,128]{1,0:T(8,128)S(1)}, f32[1024,128]{1,0:T(8,128)S(1)}, u32[]{:S(2)}, u32[]{:S(2)}) collective-permute-start(f32[1024,128]{1,0:T(8,128)S(1)} %get-tuple-element.58), channel_id=1, source_target_pairs={{0,1},{1,0},{2,3},{3,2},{4,5},{5,4},{6,7},{7,6},{8,9},{9,8},{10,11... | collective-permute-start | bytes 1572872 | tf_op jit(solution)/shard_map/ppermute | solution.py:435

commit v6 on v5

--- a/solution.py
+++ b/solution.py
@@ -178,8 +178,8 @@
         after[s, pl.ds(start, 2 * MZ), :] = rows[:, s * C : (s + 1) * C]
 
 
-def columns_forward(fields, table, after, keep, give):
-    pieces = [(k, s) for k in range(MZ) for s in range(fields)]
+def columns_forward(fields, table, after, sink, half):
+    pieces = [(k, s) for k in range(8 * half, 8 * half + 8) for s in range(fields)]
     for pair in zip(pieces[::2], pieces[1::2]):
         parts = []
         for k, s in pair:
@@ -187,7 +187,6 @@
             parts.append(jnp.concatenate(q, axis=0))
         rows = dot(table, three(jnp.concatenate(parts, axis=1)))
         for i, (k, s) in enumerate(pair):
-            sink = keep if k < 8 else give
             for r in range(2):
                 places = mode_rows(k, 2 * s + r) if fields == 2 else state_rows_of(k, r)
                 for xl, place in enumerate(places):
@@ -195,14 +194,33 @@
                     sink[place, :] = rows[at : at + 16, i * C : (i + 1) * C]
 
 
-def state_kernel(place, state, zf, yf, keep, give, after):
+def kept_kernel(place, after, yf, keep):
+    columns_forward(after.shape[0], yf[0], after, keep, 0)
+
+
+def kept_stage(place, after, yf):
+    shape = (512 * after.shape[0], C)
+    return pl.pallas_call(
+        kept_kernel,
+        grid_spec=pltpu.PrefetchScalarGridSpec(
+            num_scalar_prefetch=1,
+            grid=(1,),
+            in_specs=[still(after.shape), picked(yf, 0)],
+            out_specs=still(shape),
+        ),
+        out_shape=jax.ShapeDtypeStruct(shape, F32),
+        compiler_params=params(16),
+    )(place, after, yf)
+
+
+def state_kernel(place, state, zf, yf, after, give):
     for y in range(0, ROWS, 2):
         pair = jnp.concatenate([state[(y + i) * NZ : (y + i + 1) * NZ] for i in range(2)], axis=1)
         rows = dot(zf[0, :, :NZ], pair)
         rows = rows[: 2 * MZ] + rows[2 * MZ :]
         for i in range(2):
             after[0, pl.ds((y + i) * 2 * MZ, 2 * MZ), :] = rows[:, i * C : (i + 1) * C]
-    columns_forward(1, yf[0], after, keep, give)
+    columns_forward(1, yf[0], after, give, 1)
 
 
 def ready_kernel(place, w1_, w2_, yi_, zi_, zf_, yf_, w1, w2, w1t, w2t, yi, zi, zf, yf):
@@ -232,7 +250,7 @@
 
 
 def field_kernel(
-    early, q11, state, target, w1, w2, w1t, w2t, yi, zi, zf, yf, keep, give, late, after
+    early, q11, state, target, w1, w2, w1t, w2t, yi, zi, zf, yf, after, give, late
 ):
     step = pl.program_id(0)
 
@@ -271,7 +289,7 @@
 
     @pl.when(step == ROWS // ROWS_A_STEP - 1)
     def _():
-        columns_forward(2, yf[...], after, keep, give)
+        columns_forward(2, yf[...], after, give, 1)
 
 
 def whole(shape):
@@ -287,17 +305,16 @@
 
 
 def state_stage(place, state, zf, yf):
-    shape = jax.ShapeDtypeStruct((512, C), F32)
+    shapes = (1, 1024, C), (512, C)
     return pl.pallas_call(
         state_kernel,
         grid_spec=pltpu.PrefetchScalarGridSpec(
             num_scalar_prefetch=1,
             grid=(1,),
             in_specs=[still(state.shape), picked(zf, 1), picked(yf, 0)],
-            out_specs=(still((512, C)), still((512, C))),
-            scratch_shapes=[pltpu.VMEM((1, 1024, C), F32)],
+            out_specs=tuple(still(shape) for shape in shapes),
         ),
-        out_shape=(shape, shape),
+        out_shape=tuple(jax.ShapeDtypeStruct(shape, F32) for shape in shapes),
         compiler_params=params(),
     )(place, state, zf, yf)
 
@@ -331,14 +348,14 @@
 
 def field_stage(early, q11, state, target, ready):
     moving = pl.BlockSpec((CHUNK, C), lambda i: (i, 0))
-    shape = jax.ShapeDtypeStruct((1024, C), F32)
+    shapes = (2, 1024, C), (1024, C)
     return pl.pallas_call(
         field_kernel,
         grid=(ROWS // ROWS_A_STEP,),
         in_specs=[whole(early.shape), whole((512, C))] + [moving] * 2 + [whole(r.shape) for r in ready],
-        out_specs=(whole((1024, C)), whole((1024, C))),
-        out_shape=(shape, shape),
-        scratch_shapes=[pltpu.VMEM((2, 256, C), F32), pltpu.VMEM((2, 1024, C), F32)],
+        out_specs=tuple(whole(shape) for shape in shapes),
+        out_shape=tuple(jax.ShapeDtypeStruct(shape, F32) for shape in shapes),
+        scratch_shapes=[pltpu.VMEM((2, 256, C), F32)],
         compiler_params=params(),
     )(early, q11, state, target, *ready)
 
@@ -444,8 +461,8 @@
         return cells[:, 0].transpose(1, 2, 0).reshape(ROWS * NZ, C)
 
     state_rows = rows_of(state)
-    keep, give = state_stage(place, state_rows, zf, yf)
-    received = exchange(keep + swap(give, "co"), WIDE)
+    after, give = state_stage(place, state_rows, zf, yf)
+    received = exchange(swap(give, "co") + kept_stage(place, after, yf), WIDE)
     spectra, planes = mix_stage(received, spectral_weight, direction_weight)
     q00 = exchange(planes, WIDE[:3])
     q10 = swap(q00, "xh")
@@ -456,8 +473,8 @@
     q10, ready, target_rows = lax.optimization_barrier((q10, ready, target_rows))
     q11 = swap(q10, "co")
     early = early_stage(q00, q10, q01, ready[4])
-    keep, give = field_stage(early, q11, state_rows, target_rows, ready)
-    adjoint = exchange(keep + swap(give, "co"), WIDE)
+    after, give = field_stage(early, q11, state_rows, target_rows, ready)
+    adjoint = exchange(swap(give, "co") + kept_stage(0 * place, after, ready[7][None]), WIDE)
     gradient, curvature = outer_stage(adjoint, spectra)
     shape = (2, C, MX, 2, C)
     return gradient.reshape(shape), curvature.reshape(shape)

time: 113 us -> 114 us (level)
  waiting for transfers between devices: 6.91 us -> 4.81 us
  local copies, waits for them, and re-layouts: 5.01 us -> 6.49 us
  Pallas kernels: 23.7 us -> 24.9 us
    ppermute x5, waiting for transfers between devices: 6.91 us -> 4.81 us  [swap(): return lax.ppermute(rows, axis, [(0, 1), (1, 0)])]
    pallas_call x0 -> x2, Pallas kernels: none -> 2.09 us  [kept_stage(): pl.pallas_call(kept_kernel, grid_spec=pltpu.PrefetchScalarGridSpec(num_sc...]
    unnamed x20, local copies, waits for them, and re-layouts: 0.96 us -> 2.54 us
  transfers between devices with their start and end apart: 5 -> 5, of which waited for: 4 -> 4; matrix products, arithmetic and copies ran while one was open for 2% -> 2% of each run, Pallas kernels for 1% -> 3%
where the time goes in v6:
time: 114 us; the launch traced here: 113 us
  blocking collectives  74.4 us (65%)
  Pallas kernels  24.9 us (22%)
  local copies, waits for them, and re-layouts  6.49 us (6%)
  waiting for transfers between devices  4.81 us (4%)
  starting transfers between devices  1.9 us (2%)
    all_to_all x3, blocking collectives, exchange(): lax.all_to_all(rows.reshape(size, -1, C), group, 0, 0, tiled=True)  74.4 us
    pallas_call x1, Pallas kernels, field_stage(): pl.pallas_call(field_kernel, grid=(ROWS // ROWS_A_STEP,), in_specs=[whole...  14.3 us
    ppermute x5, waiting for transfers between devices, swap(): return lax.ppermute(rows, axis, [(0, 1), (1, 0)])  4.81 us
    transpose x2, local copies, waits for them, and re-layouts, rows_of(): return cells[:, 0].transpose(1, 2, 0).reshape(ROWS * NZ, C)  3.95 us
    pallas_call x1, Pallas kernels, outer_stage(): pl.pallas_call(outer_kernel, grid=(C // CB,), in_specs=[whole(received.sh...  3.28 us
    pallas_call x1, Pallas kernels, mix_stage(): pl.pallas_call(mix_kernel, grid=(C // CB,), in_specs=[whole(received.shap...  2.74 us
    unnamed x20, local copies, waits for them, and re-layouts  2.54 us
  transfers between devices with their start and end apart: 5, of which 4 were waited for; matrix products, arithmetic and copies ran while one was open for 2% of the time, Pallas kernels for 3%

profile of v6, /device:TPU:2, one launch (start us, length us, event | category | flops | bytes accessed | tf_op | source)
XLA Modules:
  0.0 113.5 jit_solution(15775952523678017760)
XLA Ops:
  0.7 2.0 %copy.15 = bf16[32,128,128]{2,1,0:T(8,128)(2,1)S(1)} copy(bf16[32,128,128]{1,0,2:T(8,128)(2,1)} %bitcast.35) | data formatting | bytes 2097152 | tf_op jit(solution)/shard_map/transpose | solution.py:461
  2.7 0.1 pad_add_fusion.place
  2.8 1.2 %shard_map.140 = (f32[1,1024,128]{2,1,0:T(8,128)S(1)}, f32[512,128]{1,0:T(8,128)S(1)}) custom-call(s32[2]{0:T(128)S(1)} %pad_add_fusion.place, bf16[4096,128]{1,0:T(8,128)(2,1)S(1)} %bitcast.22, bf16[2,64,256]{2,1,0:T(8,128)(2,1)S(1)} %copy-done.4, bf16[4,64,192]{2,1,0:T(8,128)(2,1)S(1)} %copy-done.2), custom_call_target="tpu_custom_call" | custom-call | tf_op jit(solution)/shard_map/pallas_call | solution.py:309
  4.0 0.1 collective-permute-start
  4.1 0.9 shard_map.141
  5.0 0.6 collective-permute-done
  5.6 29.6 %all_to_all.15 = f32[128,4,128]{2,1,0:T(4,128)S(1)} all-to-all(f32[128,4,128]{2,1,0:T(4,128)S(1)} %bitcast.34), channel_id=1, replica_groups=mesh['xl'=2,'y'=4,'z'=8,'xh'=2,'co'=2] {'y','z','xl','xh'}, dimensions={0} | all-to-all | bytes 524288 | tf_op jit(solution)/shard_map/all_to_all | solution.py:448
  35.2 1.6 %copy-done.1 = bf16[2,128,16,2,128]{4,3,2,1,0:T(2,128)(2,1)S(1)} copy-done((bf16[2,128,16,2,128]{4,3,2,1,0:T(2,128)(2,1)S(1)}, bf16[2,128,16,2,128]{4,3,2,1,0:T(2,128)(2,1)}, u32[]{:S(2)}) %copy-start.1) | copy-done | bytes 2097176
  36.8 2.7 %shard_map.142 = (f32[64,128]{1,0:T(8,128)S(1)}, f32[512,128]{1,0:T(8,128)S(1)}) custom-call(f32[512,128]{1,0:T(8,128)S(1)} %bitcast.31, bf16[2,128,32,128]{3,2,1,0:T(8,128)(2,1)S(1)} %bitcast.25, bf16[2,128,32,128]{3,2,1,0:T(8,128)(2,1)S(1)} %bitcast.26, bf16[128,512]{1,0:T(8,128)(2,1)S(1)} %copy-done.9, bf16[512,384]{1,0:T(8,128)(2,1)} %constant.29.clone.xi_), custom_call_target="tpu_custom_call" | custom-call | tf_op jit(solution)/shard_map/pallas_call | solution.py:398
  39.6 16.3 %all_to_all.16 = f32[64,8,128]{2,1,0:T(8,128)S(1)} all-to-all(f32[64,8,128]{2,1,0:T(8,128)S(1)} %bitcast.32), channel_id=1, replica_groups=mesh['xl'=2,'y'=4,'z'=8,'xh'=2,'co'=2] {'y','z','xl'}, dimensions={0} | all-to-all | bytes 524288 | tf_op jit(solution)/shard_map/all_to_all | solution.py:448
  55.9 1.6 %collective-permute-start.1 = (f32[512,128]{1,0:T(8,128)S(1)}, f32[512,128]{1,0:T(8,128)S(1)}, u32[]{:S(2)}, u32[]{:S(2)}) collective-permute-start(f32[512,128]{1,0:T(8,128)S(1)} %bitcast.28), channel_id=1, source_target_pairs={{0,2},{2,0},{1,3},{3,1},{4,6},{6,4},{5,7},{7,5},{8,10},{10,8},{9,1... | collective-permute-start | bytes 786440 | tf_op jit(solution)/shard_map/ppermute | solution.py:452
  57.5 1.9 %copy.16 = bf16[32,128,128]{2,1,0:T(8,128)(2,1)S(1)} copy(bf16[32,128,128]{1,0,2:T(8,128)(2,1)} %bitcast.36) | data formatting | bytes 2097152 | tf_op jit(solution)/shard_map/transpose | solution.py:461
  59.5 0.9 copy-done.8
  60.4 0.7 shard_map.143
  61.0 2.7 %collective-permute-done.1.q10 = f32[512,128]{1,0:T(8,128)S(1)} collective-permute-done((f32[512,128]{1,0:T(8,128)S(1)}, f32[512,128]{1,0:T(8,128)S(1)}, u32[]{:S(2)}, u32[]{:S(2)}) %collective-permute-start.1) | collective-permute-done | bytes 262176 | tf_op jit(solution)/shard_map/ppermute | solution.py:452
  63.8 0.6 shard_map.144.early
  64.4 0.9 collective-permute-done.3.q11
  65.3 14.3 %shard_map.145 = (f32[2,1024,128]{2,1,0:T(8,128)S(1)}, f32[1024,128]{1,0:T(8,128)S(1)}) custom-call(f32[2,768,128]{2,1,0:T(8,128)S(1)} %shard_map.144.early, f32[512,128]{1,0:T(8,128)S(1)} %collective-permute-done.3.q11, bf16[4096,128]{1,0:T(8,128)(2,1)S(1)} %bitcast.23, bf16[4096,128]{1,0:T(8,128)(2,1)S(1)} %bitcast.24, ...), custom_call_target="tpu_custom_call" | custom-call | tf_op jit(solution)/shard_map/pallas_call | solution.py:352
  79.6 0.2 collective-permute-start.4
  79.8 1.2 %shard_map.146 = f32[1024,128]{1,0:T(8,128)S(1)} custom-call(s32[2]{0:T(128)S(1)} %broadcast_1_place.2.place, f32[2,1024,128]{2,1,0:T(8,128)S(1)} %get-tuple-element.58.after, bf16[1,64,192]{2,1,0:T(8,128)(2,1)S(1)} %bitcast.33), custom_call_target="tpu_custom_call" | custom-call | tf_op jit(solution)/shard_map/pallas_call | solution.py:203
  81.0 0.6 collective-permute-done.4
  81.6 0.1 add_bitcast_fusion
  81.7 28.5 %all_to_all.17 = f32[128,8,128]{2,1,0:T(8,128)S(1)} all-to-all(f32[128,8,128]{2,1,0:T(8,128)S(1)} %add_bitcast_fusion), channel_id=1, replica_groups=mesh['xl'=2,'y'=4,'z'=8,'xh'=2,'co'=2] {'y','z','xl','xh'}, dimensions={0} | all-to-all | bytes 1048576 | tf_op jit(solution)/shard_map/all_to_all | solution.py:448
  110.2 3.3 %shard_map.147 = (bf16[2,128,32,128]{3,2,1,0:T(8,128)(2,1)}, bf16[2,128,32,128]{3,2,1,0:T(8,128)(2,1)}) custom-call(f32[1024,128]{1,0:T(8,128)S(1)} %bitcast.27, f32[64,128]{1,0:T(8,128)S(1)} %get-tuple-element.59.spectra, bf16[256,1024]{1,0:T(8,128)(2,1)S(1)} %copy-done.3), custom_call_target="tpu_custom_call" | custom-call | tf_op jit(solution)/shard_map/pallas_call | solution.py:435
  (23 shorter events, 0.1 us)
Async XLA Ops:
  0.6 2.2 %copy-start.2 = (bf16[4,64,192]{2,1,0:T(8,128)(2,1)S(1)}, bf16[4,64,192]{2,1,0:T(8,128)(2,1)}, u32[]{:S(2)}) copy-start(bf16[4,64,192]{2,1,0:T(8,128)(2,1)} %constant.25.clone.yf.yf_) | copy-start | bytes 294916
  0.6 2.1 %copy-start.4 = (bf16[2,64,256]{2,1,0:T(8,128)(2,1)S(1)}, bf16[2,64,256]{2,1,0:T(8,128)(2,1)}, u32[]{:S(2)}) copy-start(bf16[2,64,256]{2,1,0:T(8,128)(2,1)} %constant.27.clone.zf.zf_) | copy-start | bytes 196612
  2.7 32.5 %copy-start = (bf16[2,128,16,2,128]{4,3,2,1,0:T(2,128)(2,1)S(1)}, bf16[2,128,16,2,128]{4,3,2,1,0:T(2,128)(2,1)}, u32[]{:S(2)}) copy-start(bf16[2,128,16,2,128]{4,3,2,1,0:T(2,128)(2,1)} %param.15) | copy-start | bytes 6291460
  2.7 32.5 %copy-start.9 = (bf16[128,512]{1,0:T(8,128)(2,1)S(1)}, bf16[128,512]{1,0:T(8,128)(2,1)}, u32[]{:S(2)}) copy-start(bf16[128,512]{1,0:T(8,128)(2,1)} %constant.28.clone.xf) | copy-start | bytes 393220
  4.0 1.6 %collective-permute-start = (f32[512,128]{1,0:T(8,128)S(1)}, f32[512,128]{1,0:T(8,128)S(1)}, u32[]{:S(2)}, u32[]{:S(2)}) collective-permute-start(f32[512,128]{1,0:T(8,128)S(1)} %get-tuple-element.32), channel_id=1, source_target_pairs={{0,1},{1,0},{2,3},{3,2},{4,5},{5,4},{6,7},{7,6},{8,9},{9,8},{10,11... | collective-permute-start | bytes 786440 | tf_op jit(solution)/shard_map/ppermute | solution.py:452
  35.2 1.6 %copy-start.1 = (bf16[2,128,16,2,128]{4,3,2,1,0:T(2,128)(2,1)S(1)}, bf16[2,128,16,2,128]{4,3,2,1,0:T(2,128)(2,1)}, u32[]{:S(2)}) copy-start(bf16[2,128,16,2,128]{4,3,2,1,0:T(2,128)(2,1)} %param.16) | copy-start | bytes 6291460
  39.6 19.9 %copy-start.5 = (bf16[128,512]{1,0:T(8,128)(2,1)S(1)}, bf16[128,512]{1,0:T(8,128)(2,1)}, u32[]{:S(2)}) copy-start(bf16[128,512]{1,0:T(8,128)(2,1)} %w1_) | copy-start | bytes 393220
  39.6 19.9 %copy-start.6 = (bf16[512,128]{1,0:T(8,128)(2,1)S(1)}, bf16[512,128]{1,0:T(8,128)(2,1)}, u32[]{:S(2)}) copy-start(bf16[512,128]{1,0:T(8,128)(2,1)} %w2_) | copy-start | bytes 393220
  39.6 19.9 %copy-start.7 = (bf16[4,64,192]{2,1,0:T(8,128)(2,1)S(1)}, bf16[4,64,192]{2,1,0:T(8,128)(2,1)}, u32[]{:S(2)}) copy-start(bf16[4,64,192]{2,1,0:T(8,128)(2,1)} %constant.24.clone.yi_) | copy-start | bytes 294916
  55.9 7.9 %collective-permute-start.1 = (f32[512,128]{1,0:T(8,128)S(1)}, f32[512,128]{1,0:T(8,128)S(1)}, u32[]{:S(2)}, u32[]{:S(2)}) collective-permute-start(f32[512,128]{1,0:T(8,128)S(1)} %bitcast.28), channel_id=1, source_target_pairs={{0,2},{2,0},{1,3},{3,1},{4,6},{6,4},{5,7},{7,5},{8,10},{10,8},{9,1... | collective-permute-start | bytes 786440 | tf_op jit(solution)/shard_map/ppermute | solution.py:452
  57.5 6.3 %collective-permute-start.2 = (f32[512,128]{1,0:T(8,128)S(1)}, f32[512,128]{1,0:T(8,128)S(1)}, u32[]{:S(2)}, u32[]{:S(2)}) collective-permute-start(f32[512,128]{1,0:T(8,128)S(1)} %bitcast.29), channel_id=1, source_target_pairs={{0,1},{1,0},{2,3},{3,2},{4,5},{5,4},{6,7},{7,6},{8,9},{9,8},{10,11... | collective-permute-start | bytes 786440 | tf_op jit(solution)/shard_map/ppermute | solution.py:452
  59.5 0.9 copy-start.8
  63.8 1.5 %collective-permute-start.3 = (f32[512,128]{1,0:T(8,128)S(1)}, f32[512,128]{1,0:T(8,128)S(1)}, u32[]{:S(2)}, u32[]{:S(2)}) collective-permute-start(f32[512,128]{1,0:T(8,128)S(1)} %collective-permute-done.1.q10), channel_id=1, source_target_pairs={{0,1},{1,0},{2,3},{3,2},{4,5},{5,4},{6,7},{7,6},{8,9},{9,8},{10,11... | collective-permute-start | bytes 786440 | tf_op jit(solution)/shard_map/ppermute | solution.py:452
  79.6 2.0 %collective-permute-start.4 = (f32[1024,128]{1,0:T(8,128)S(1)}, f32[1024,128]{1,0:T(8,128)S(1)}, u32[]{:S(2)}, u32[]{:S(2)}) collective-permute-start(f32[1024,128]{1,0:T(8,128)S(1)} %get-tuple-element.57), channel_id=1, source_target_pairs={{0,1},{1,0},{2,3},{3,2},{4,5},{5,4},{6,7},{7,6},{8,9},{9,8},{10,11... | collective-permute-start | bytes 1572872 | tf_op jit(solution)/shard_map/ppermute | solution.py:452
  79.8 30.4 %copy-start.3 = (bf16[256,1024]{1,0:T(8,128)(2,1)S(1)}, bf16[256,1024]{1,0:T(8,128)(2,1)}, u32[]{:S(2)}) copy-start(bf16[256,1024]{1,0:T(8,128)(2,1)} %constant.30.clone.xf) | copy-start | bytes 1572868

commit v7 on v6

--- a/solution.py
+++ b/solution.py
@@ -213,13 +213,14 @@
     )(place, after, yf)
 
 
-def state_kernel(place, state, zf, yf, after, give):
+def state_kernel(place, state, zf, yf, keep, give, after):
     for y in range(0, ROWS, 2):
         pair = jnp.concatenate([state[(y + i) * NZ : (y + i + 1) * NZ] for i in range(2)], axis=1)
         rows = dot(zf[0, :, :NZ], pair)
         rows = rows[: 2 * MZ] + rows[2 * MZ :]
         for i in range(2):
             after[0, pl.ds((y + i) * 2 * MZ, 2 * MZ), :] = rows[:, i * C : (i + 1) * C]
+    columns_forward(1, yf[0], after, keep, 0)
     columns_forward(1, yf[0], after, give, 1)
 
 
@@ -305,16 +306,17 @@
 
 
 def state_stage(place, state, zf, yf):
-    shapes = (1, 1024, C), (512, C)
+    shape = jax.ShapeDtypeStruct((512, C), F32)
     return pl.pallas_call(
         state_kernel,
         grid_spec=pltpu.PrefetchScalarGridSpec(
             num_scalar_prefetch=1,
             grid=(1,),
             in_specs=[still(state.shape), picked(zf, 1), picked(yf, 0)],
-            out_specs=tuple(still(shape) for shape in shapes),
+            out_specs=(still((512, C)), still((512, C))),
+            scratch_shapes=[pltpu.VMEM((1, 1024, C), F32)],
         ),
-        out_shape=tuple(jax.ShapeDtypeStruct(shape, F32) for shape in shapes),
+        out_shape=(shape, shape),
         compiler_params=params(),
     )(place, state, zf, yf)
 
@@ -461,8 +463,8 @@
         return cells[:, 0].transpose(1, 2, 0).reshape(ROWS * NZ, C)
 
     state_rows = rows_of(state)
-    after, give = state_stage(place, state_rows, zf, yf)
-    received = exchange(swap(give, "co") + kept_stage(place, after, yf), WIDE)
+    keep, give = state_stage(place, state_rows, zf, yf)
+    received = exchange(keep + swap(give, "co"), WIDE)
     spectra, planes = mix_stage(received, spectral_weight, direction_weight)
     q00 = exchange(planes, WIDE[:3])
     q10 = swap(q00, "xh")

time: 114 us -> 112 us (0.982)
  local copies, waits for them, and re-layouts: 6.49 us -> 5 us
    unnamed x20, local copies, waits for them, and re-layouts: 2.54 us -> 0.95 us
  transfers between devices with their start and end apart: 5 -> 5, of which waited for: 4 -> 4; matrix products, arithmetic and copies ran while one was open for 2% -> 2% of each run, Pallas kernels for 3% -> 2%
where the time goes in v7:
time: 112 us
  blocking collectives  74.4 us (66%)
  Pallas kernels  24.2 us (22%)
  waiting for transfers between devices  5.74 us (5%)
  local copies, waits for them, and re-layouts  5 us (4%)
  starting transfers between devices  1.91 us (2%)
    all_to_all x3, blocking collectives, exchange(): lax.all_to_all(rows.reshape(size, -1, C), group, 0, 0, tiled=True)  74.4 us
    pallas_call x1, Pallas kernels, field_stage(): pl.pallas_call(field_kernel, grid=(ROWS // ROWS_A_STEP,), in_specs=[whole...  14.3 us
    ppermute x5, waiting for transfers between devices, swap(): return lax.ppermute(rows, axis, [(0, 1), (1, 0)])  5.74 us
    transpose x2, local copies, waits for them, and re-layouts, rows_of(): return cells[:, 0].transpose(1, 2, 0).reshape(ROWS * NZ, C)  4.05 us
    pallas_call x1, Pallas kernels, outer_stage(): pl.pallas_call(outer_kernel, grid=(C // CB,), in_specs=[whole(received.sh...  3.27 us
    pallas_call x1, Pallas kernels, mix_stage(): pl.pallas_call(mix_kernel, grid=(C // CB,), in_specs=[whole(received.shap...  2.76 us
  transfers between devices with their start and end apart: 5, of which 4 were waited for; matrix products, arithmetic and copies ran while one was open for 2% of the time, Pallas kernels for 2%

profile of v7, /device:TPU:2, one launch (start us, length us, event | category | flops | bytes accessed | tf_op | source)
XLA Modules:
  0.0 112.2 jit_solution(18093629455310469324)
XLA Ops:
  0.6 0.0 copy-start.2
  0.6 0.0 copy-start.4
  0.7 2.1 %copy.15 = bf16[32,128,128]{2,1,0:T(8,128)(2,1)S(1)} copy(bf16[32,128,128]{1,0,2:T(8,128)(2,1)} %bitcast.35) | data formatting | bytes 2097152 | tf_op jit(solution)/shard_map/transpose | solution.py:463
  2.8 0.1 pad_add_fusion.place
  2.9 1.4 %shard_map.140 = (f32[512,128]{1,0:T(8,128)S(1)}, f32[512,128]{1,0:T(8,128)S(1)}) custom-call(s32[2]{0:T(128)S(1)} %pad_add_fusion.place, bf16[4096,128]{1,0:T(8,128)(2,1)S(1)} %bitcast.22, bf16[2,64,256]{2,1,0:T(8,128)(2,1)S(1)} %copy-done.4, bf16[4,64,192]{2,1,0:T(8,128)(2,1)S(1)} %copy-done.2), custom_call_target="tpu_custom_call" | custom-call | tf_op jit(solution)/shard_map/pallas_call | solution.py:310
  4.3 0.1 collective-permute-start
  4.4 1.5 %collective-permute-done = f32[512,128]{1,0:T(8,128)S(1)} collective-permute-done((f32[512,128]{1,0:T(8,128)S(1)}, f32[512,128]{1,0:T(8,128)S(1)}, u32[]{:S(2)}, u32[]{:S(2)}) %collective-permute-start) | collective-permute-done | bytes 262176 | tf_op jit(solution)/shard_map/ppermute | solution.py:454
  6.0 29.6 %all_to_all.15 = f32[128,4,128]{2,1,0:T(4,128)S(1)} all-to-all(f32[128,4,128]{2,1,0:T(4,128)S(1)} %bitcast.34), channel_id=1, replica_groups=mesh['xl'=2,'y'=4,'z'=8,'xh'=2,'co'=2] {'y','z','xl','xh'}, dimensions={0} | all-to-all | bytes 524288 | tf_op jit(solution)/shard_map/all_to_all | solution.py:450
  35.6 2.8 %shard_map.141 = (f32[64,128]{1,0:T(8,128)S(1)}, f32[512,128]{1,0:T(8,128)S(1)}) custom-call(f32[512,128]{1,0:T(8,128)S(1)} %bitcast.31, bf16[2,128,32,128]{3,2,1,0:T(8,128)(2,1)S(1)} %bitcast.25, bf16[2,128,32,128]{3,2,1,0:T(8,128)(2,1)S(1)} %bitcast.26, bf16[128,512]{1,0:T(8,128)(2,1)S(1)} %copy-done.9, bf16[512,384]{1,0:T(8,128)(2,1)} %constant.29.clone.xi_), custom_call_target="tpu_custom_call" | custom-call | tf_op jit(solution)/shard_map/pallas_call | solution.py:400
  38.4 16.3 %all_to_all.16 = f32[64,8,128]{2,1,0:T(8,128)S(1)} all-to-all(f32[64,8,128]{2,1,0:T(8,128)S(1)} %bitcast.32), channel_id=1, replica_groups=mesh['xl'=2,'y'=4,'z'=8,'xh'=2,'co'=2] {'y','z','xl'}, dimensions={0} | all-to-all | bytes 524288 | tf_op jit(solution)/shard_map/all_to_all | solution.py:450
  54.6 1.6 %collective-permute-start.1 = (f32[512,128]{1,0:T(8,128)S(1)}, f32[512,128]{1,0:T(8,128)S(1)}, u32[]{:S(2)}, u32[]{:S(2)}) collective-permute-start(f32[512,128]{1,0:T(8,128)S(1)} %bitcast.28), channel_id=1, source_target_pairs={{0,2},{2,0},{1,3},{3,1},{4,6},{6,4},{5,7},{7,5},{8,10},{10,8},{9,1... | collective-permute-start | bytes 786440 | tf_op jit(solution)/shard_map/ppermute | solution.py:454
  56.2 1.9 %copy.16 = bf16[32,128,128]{2,1,0:T(8,128)(2,1)S(1)} copy(bf16[32,128,128]{1,0,2:T(8,128)(2,1)} %bitcast.36) | data formatting | bytes 2097152 | tf_op jit(solution)/shard_map/transpose | solution.py:463
  58.2 0.9 copy-done.8
  59.1 0.7 shard_map.142
  59.8 2.7 %collective-permute-done.1.q10 = f32[512,128]{1,0:T(8,128)S(1)} collective-permute-done((f32[512,128]{1,0:T(8,128)S(1)}, f32[512,128]{1,0:T(8,128)S(1)}, u32[]{:S(2)}, u32[]{:S(2)}) %collective-permute-start.1) | collective-permute-done | bytes 262176 | tf_op jit(solution)/shard_map/ppermute | solution.py:454
  62.5 0.6 shard_map.143.early
  63.2 0.9 collective-permute-done.3.q11
  64.0 14.3 %shard_map.144 = (f32[2,1024,128]{2,1,0:T(8,128)S(1)}, f32[1024,128]{1,0:T(8,128)S(1)}) custom-call(f32[2,768,128]{2,1,0:T(8,128)S(1)} %shard_map.143.early, f32[512,128]{1,0:T(8,128)S(1)} %collective-permute-done.3.q11, bf16[4096,128]{1,0:T(8,128)(2,1)S(1)} %bitcast.23, bf16[4096,128]{1,0:T(8,128)(2,1)S(1)} %bitcast.24, ...), custom_call_target="tpu_custom_call" | custom-call | tf_op jit(solution)/shard_map/pallas_call | solution.py:354
  78.3 0.2 collective-permute-start.4
  78.6 1.2 %shard_map.145 = f32[1024,128]{1,0:T(8,128)S(1)} custom-call(s32[2]{0:T(128)S(1)} %broadcast_1_place.2.place, f32[2,1024,128]{2,1,0:T(8,128)S(1)} %get-tuple-element.58.after, bf16[1,64,192]{2,1,0:T(8,128)(2,1)S(1)} %bitcast.33), custom_call_target="tpu_custom_call" | custom-call | tf_op jit(solution)/shard_map/pallas_call | solution.py:203
  79.7 0.6 collective-permute-done.4
  80.3 0.1 add_bitcast_fusion
  80.4 28.5 %all_to_all.17 = f32[128,8,128]{2,1,0:T(8,128)S(1)} all-to-all(f32[128,8,128]{2,1,0:T(8,128)S(1)} %add_bitcast_fusion), channel_id=1, replica_groups=mesh['xl'=2,'y'=4,'z'=8,'xh'=2,'co'=2] {'y','z','xl','xh'}, dimensions={0} | all-to-all | bytes 1048576 | tf_op jit(solution)/shard_map/all_to_all | solution.py:450
  108.9 3.3 %shard_map.146 = (bf16[2,128,32,128]{3,2,1,0:T(8,128)(2,1)}, bf16[2,128,32,128]{3,2,1,0:T(8,128)(2,1)}) custom-call(f32[1024,128]{1,0:T(8,128)S(1)} %bitcast.27, f32[64,128]{1,0:T(8,128)S(1)} %get-tuple-element.59.spectra, bf16[256,1024]{1,0:T(8,128)(2,1)S(1)} %copy-done.3), custom_call_target="tpu_custom_call" | custom-call | tf_op jit(solution)/shard_map/pallas_call | solution.py:437
  (22 shorter events, 0.1 us)
Async XLA Ops:
  0.6 2.3 %copy-start.2 = (bf16[4,64,192]{2,1,0:T(8,128)(2,1)S(1)}, bf16[4,64,192]{2,1,0:T(8,128)(2,1)}, u32[]{:S(2)}) copy-start(bf16[4,64,192]{2,1,0:T(8,128)(2,1)} %constant.25.clone.yf.yf_) | copy-start | bytes 294916
  0.6 2.2 %copy-start.4 = (bf16[2,64,256]{2,1,0:T(8,128)(2,1)S(1)}, bf16[2,64,256]{2,1,0:T(8,128)(2,1)}, u32[]{:S(2)}) copy-start(bf16[2,64,256]{2,1,0:T(8,128)(2,1)} %constant.27.clone.zf.zf_) | copy-start | bytes 196612
  0.7 34.9 %copy-start = (bf16[2,128,16,2,128]{4,3,2,1,0:T(2,128)(2,1)S(1)}, bf16[2,128,16,2,128]{4,3,2,1,0:T(2,128)(2,1)}, u32[]{:S(2)}) copy-start(bf16[2,128,16,2,128]{4,3,2,1,0:T(2,128)(2,1)} %param.15) | copy-start | bytes 6291460
  0.7 34.9 %copy-start.9 = (bf16[128,512]{1,0:T(8,128)(2,1)S(1)}, bf16[128,512]{1,0:T(8,128)(2,1)}, u32[]{:S(2)}) copy-start(bf16[128,512]{1,0:T(8,128)(2,1)} %constant.28.clone.xf) | copy-start | bytes 393220
  2.8 32.8 %copy-start.1 = (bf16[2,128,16,2,128]{4,3,2,1,0:T(2,128)(2,1)S(1)}, bf16[2,128,16,2,128]{4,3,2,1,0:T(2,128)(2,1)}, u32[]{:S(2)}) copy-start(bf16[2,128,16,2,128]{4,3,2,1,0:T(2,128)(2,1)} %param.16) | copy-start | bytes 6291460
  4.3 1.6 %collective-permute-start = (f32[512,128]{1,0:T(8,128)S(1)}, f32[512,128]{1,0:T(8,128)S(1)}, u32[]{:S(2)}, u32[]{:S(2)}) collective-permute-start(f32[512,128]{1,0:T(8,128)S(1)} %get-tuple-element.33), channel_id=1, source_target_pairs={{0,1},{1,0},{2,3},{3,2},{4,5},{5,4},{6,7},{7,6},{8,9},{9,8},{10,11... | collective-permute-start | bytes 786440 | tf_op jit(solution)/shard_map/ppermute | solution.py:454
  38.3 19.9 %copy-start.5 = (bf16[128,512]{1,0:T(8,128)(2,1)S(1)}, bf16[128,512]{1,0:T(8,128)(2,1)}, u32[]{:S(2)}) copy-start(bf16[128,512]{1,0:T(8,128)(2,1)} %w1_) | copy-start | bytes 393220
  38.3 19.9 %copy-start.6 = (bf16[512,128]{1,0:T(8,128)(2,1)S(1)}, bf16[512,128]{1,0:T(8,128)(2,1)}, u32[]{:S(2)}) copy-start(bf16[512,128]{1,0:T(8,128)(2,1)} %w2_) | copy-start | bytes 393220
  38.3 19.9 %copy-start.7 = (bf16[4,64,192]{2,1,0:T(8,128)(2,1)S(1)}, bf16[4,64,192]{2,1,0:T(8,128)(2,1)}, u32[]{:S(2)}) copy-start(bf16[4,64,192]{2,1,0:T(8,128)(2,1)} %constant.24.clone.yi_) | copy-start | bytes 294916
  54.6 7.9 %collective-permute-start.1 = (f32[512,128]{1,0:T(8,128)S(1)}, f32[512,128]{1,0:T(8,128)S(1)}, u32[]{:S(2)}, u32[]{:S(2)}) collective-permute-start(f32[512,128]{1,0:T(8,128)S(1)} %bitcast.28), channel_id=1, source_target_pairs={{0,2},{2,0},{1,3},{3,1},{4,6},{6,4},{5,7},{7,5},{8,10},{10,8},{9,1... | collective-permute-start | bytes 786440 | tf_op jit(solution)/shard_map/ppermute | solution.py:454
  56.2 6.3 %collective-permute-start.2 = (f32[512,128]{1,0:T(8,128)S(1)}, f32[512,128]{1,0:T(8,128)S(1)}, u32[]{:S(2)}, u32[]{:S(2)}) collective-permute-start(f32[512,128]{1,0:T(8,128)S(1)} %bitcast.29), channel_id=1, source_target_pairs={{0,1},{1,0},{2,3},{3,2},{4,5},{5,4},{6,7},{7,6},{8,9},{9,8},{10,11... | collective-permute-start | bytes 786440 | tf_op jit(solution)/shard_map/ppermute | solution.py:454
  58.2 0.9 copy-start.8
  62.5 1.5 %collective-permute-start.3 = (f32[512,128]{1,0:T(8,128)S(1)}, f32[512,128]{1,0:T(8,128)S(1)}, u32[]{:S(2)}, u32[]{:S(2)}) collective-permute-start(f32[512,128]{1,0:T(8,128)S(1)} %collective-permute-done.1.q10), channel_id=1, source_target_pairs={{0,1},{1,0},{2,3},{3,2},{4,5},{5,4},{6,7},{7,6},{8,9},{9,8},{10,11... | collective-permute-start | bytes 786440 | tf_op jit(solution)/shard_map/ppermute | solution.py:454
  78.3 2.0 %collective-permute-start.4 = (f32[1024,128]{1,0:T(8,128)S(1)}, f32[1024,128]{1,0:T(8,128)S(1)}, u32[]{:S(2)}, u32[]{:S(2)}) collective-permute-start(f32[1024,128]{1,0:T(8,128)S(1)} %get-tuple-element.57), channel_id=1, source_target_pairs={{0,1},{1,0},{2,3},{3,2},{4,5},{5,4},{6,7},{7,6},{8,9},{9,8},{10,11... | collective-permute-start | bytes 1572872 | tf_op jit(solution)/shard_map/ppermute | solution.py:454
  78.6 30.4 %copy-start.3 = (bf16[256,1024]{1,0:T(8,128)(2,1)S(1)}, bf16[256,1024]{1,0:T(8,128)(2,1)}, u32[]{:S(2)}) copy-start(bf16[256,1024]{1,0:T(8,128)(2,1)} %constant.30.clone.xf) | copy-start | bytes 1572868
